TPU v7x, 512 devices: a whole 4x4x16 slice. The times are simulated.
512 devices in a mesh: ctx: 64 (over z_lo, y, core), head: 8 (over x, z_hi).
Axes of the slice: x: 4, y: 4, z: 16 (z_hi: 2, z_lo: 8; z = z_hi * 8 + z_lo), core: 2. Of those that a mesh axis runs over, the one named last changes fastest.
Arguments:
- queries: bfloat16 [8192, 6144], P('ctx', 'head'), may hold values from -5 to 5
- keys: bfloat16 [8192, 1024], P('ctx', 'head'), may hold values from -5 to 5
- values: bfloat16 [8192, 1024], P('ctx', 'head'), may hold values from -6 to 6
- cotangent: bfloat16 [8192, 6144], P('ctx', 'head'), may hold values from -6 to 6
- seg_lengths: int32 [128], replicated, may hold values from 1 to 1024, 8192 in all
- seg_return: float32 [128], replicated, may hold values from -1 to 1
- owner_slot: int32 [8192], P('ctx'), may hold values from 0 to 8191, each once
- ref_term: float32 [8192], P(('ctx', 'head')), may hold values from -1 to 1
Outputs:
- grad_queries: bfloat16 [8192, 6144], P('ctx', 'head')
- grad_keys: bfloat16 [8192, 1024], P('ctx', 'head')
- grad_values: bfloat16 [8192, 1024], P('ctx', 'head')
Inputs may be any that keep to these rules, and one draw needn't show every extreme that they name: `seg_lengths`: the lengths sum to 8192; the largest is exactly 1024. `owner_slot`: every value appears exactly once.
All inputs are finite; a program needn't handle non-finite values.
Results may differ from a plain program's by a relative error of at most 0.012.
Values may be sent and summed in bfloat16 or wider, within the bound.
No kernel may reach another device: no remote copies, remote signals or barrier semaphores. Data moves between devices by JAX's collectives and lax.ppermute only.
A program may use at most 64 MiB of HBM per device.

v0:
```python
import math

import jax
import jax.numpy as jnp
from jax import lax
from jax.sharding import PartitionSpec as P

E = 128


NEG = -1e30


def shortened(x):

    def short(part):
        return part.astype(jnp.bfloat16) if part.dtype == jnp.float32 else part

    return jax.tree.map(short, x)


def passed_along(value, axis, steps):
    count = lax.axis_size(axis)
    pairs = [(source, (source + steps) % count) for source in range(count)]
    return lax.ppermute(value, axis, pairs)


def positions(device, local_rows, half_rows, ctx_count):
    upper_half = local_rows >= half_rows
    early = device * half_rows + local_rows
    late = (2 * ctx_count - 1 - device) * half_rows + local_rows - half_rows
    return jnp.where(upper_half, late, early)


def tile_scores(left_part, right_part, keys_major):
    einsum_form = "qhge,khe->hgkq" if keys_major else "qhge,khe->hgqk"
    return jnp.einsum(einsum_form, left_part, right_part, preferred_element_type=jnp.float32)


def forward_tile(
    row_stats, query_part, grad_part, key_part, value_part, causal_mask, keys_major, score_scale
):
    run_max, run_total, run_dot = row_stats
    reduce_axis = -2 if keys_major else -1
    scores = tile_scores(query_part, key_part, keys_major) * score_scale
    dot_terms = tile_scores(grad_part, value_part, keys_major)
    if causal_mask is not None:
        scores = jnp.where(causal_mask, scores, NEG)
    new_max = jnp.maximum(run_max, jnp.max(scores, axis=reduce_axis))
    factor = jnp.exp(run_max - new_max)
    prob_tile = jnp.exp(scores - jnp.expand_dims(new_max, reduce_axis))
    if causal_mask is not None:
        prob_tile = jnp.where(causal_mask, prob_tile, 0.0)
    new_total = factor * run_total + jnp.sum(prob_tile, axis=reduce_axis)
    new_dot = factor * run_dot + jnp.sum(prob_tile * dot_terms, axis=reduce_axis)
    return (new_max, new_total, new_dot)


def backward_tile(
    query_part,
    grad_part,
    key_part,
    value_part,
    log_part,
    dot_part,
    causal_mask,
    keys_major,
    score_scale,
):
    reduce_axis = -2 if keys_major else -1
    scores = tile_scores(query_part, key_part, keys_major) * score_scale
    dot_terms = tile_scores(grad_part, value_part, keys_major)
    prob_tile = jnp.exp(scores - jnp.expand_dims(log_part, reduce_axis))
    if causal_mask is not None:
        prob_tile = jnp.where(causal_mask, prob_tile, 0.0)
    slope = (prob_tile * (dot_terms - jnp.expand_dims(dot_part, reduce_axis))).astype(jnp.bfloat16)
    prob_low = prob_tile.astype(jnp.bfloat16)
    tile_form = "hgkq" if keys_major else "hgqk"
    grad_query = (
        jnp.einsum(tile_form + ",khe->qhge", slope, key_part, preferred_element_type=jnp.float32)
        * score_scale
    )
    grad_key = (
        jnp.einsum(tile_form + ",qhge->khe", slope, query_part, preferred_element_type=jnp.float32)
        * score_scale
    )
    grad_value = jnp.einsum(
        tile_form + ",qhge->khe", prob_low, grad_part, preferred_element_type=jnp.float32
    )
    return (grad_query, grad_key, grad_value)


def split_stack(kv_stack, row_count):
    return (kv_stack[0].reshape(row_count, -1, E), kv_stack[1].reshape(row_count, -1, E))


def forward_visit(row_stats, kv_stack, owner, context):
    my_index, query_rows, grad_rows, my_pos, half_rows, score_scale = context
    row_count = query_rows.shape[0]
    key_rows, value_rows = split_stack(kv_stack, row_count)

    def forward_earlier(stats_in):
        return forward_tile(
            stats_in,
            query_rows,
            grad_rows,
            key_rows[:half_rows],
            value_rows[:half_rows],
            None,
            True,
            score_scale,
        )

    def forward_same(stats_in):
        causal_mask = my_pos[None, :] <= my_pos[:, None]
        return forward_tile(
            stats_in, query_rows, grad_rows, key_rows, value_rows, causal_mask, False, score_scale
        )

    def forward_later(stats_in):
        upper_stats = tuple((piece_stat[..., half_rows:] for piece_stat in stats_in))
        fresh_stats = forward_tile(
            upper_stats,
            query_rows[half_rows:],
            grad_rows[half_rows:],
            key_rows,
            value_rows,
            None,
            False,
            score_scale,
        )
        return tuple(
            (
                jnp.concatenate([old_stat[..., :half_rows], new_stat], axis=-1)
                for old_stat, new_stat in zip(stats_in, fresh_stats)
            )
        )

    branch = jnp.sign(owner - my_index) + 1
    return lax.switch(branch, [forward_earlier, forward_same, forward_later], row_stats)


def backward_visit(accum_pair, kv_stack, owner, context):
    my_index, query_rows, grad_rows, my_pos, half_rows, score_scale, log_total, dot_total = context
    row_count = query_rows.shape[0]
    key_rows, value_rows = split_stack(kv_stack, row_count)

    def backward_earlier(pair_in):
        q_accum, kv_accum = pair_in
        grad_query, grad_key, grad_value = backward_tile(
            query_rows,
            grad_rows,
            key_rows[:half_rows],
            value_rows[:half_rows],
            log_total,
            dot_total,
            None,
            True,
            score_scale,
        )
        kv_add = jnp.stack([grad_key, grad_value]).reshape(2, half_rows, -1)
        return (q_accum + grad_query, kv_accum.at[:, :half_rows].add(kv_add))

    def backward_same(pair_in):
        q_accum, kv_accum = pair_in
        causal_mask = my_pos[None, :] <= my_pos[:, None]
        grad_query, grad_key, grad_value = backward_tile(
            query_rows,
            grad_rows,
            key_rows,
            value_rows,
            log_total,
            dot_total,
            causal_mask,
            False,
            score_scale,
        )
        kv_add = jnp.stack([grad_key, grad_value]).reshape(2, row_count, -1)
        return (q_accum + grad_query, kv_accum + kv_add)

    def backward_later(pair_in):
        q_accum, kv_accum = pair_in
        grad_query, grad_key, grad_value = backward_tile(
            query_rows[half_rows:],
            grad_rows[half_rows:],
            key_rows,
            value_rows,
            log_total[..., half_rows:],
            dot_total[..., half_rows:],
            None,
            False,
            score_scale,
        )
        kv_add = jnp.stack([grad_key, grad_value]).reshape(2, row_count, -1)
        return (q_accum.at[half_rows:].add(grad_query), kv_accum + kv_add)

    branch = jnp.sign(owner - my_index) + 1
    return lax.switch(branch, [backward_earlier, backward_same, backward_later], accum_pair)


def per_device(queries, keys, values, cotangent, seg_lengths, seg_return, owner_slot, ref_term):
    ctx_count = lax.axis_size("ctx")
    my_index = lax.axis_index("ctx")
    row_count = queries.shape[0]
    half_rows = row_count // 2
    kv_heads = keys.shape[1] // E
    score_scale = 1.0 / math.sqrt(E)
    my_pos = positions(my_index, jnp.arange(row_count, dtype=jnp.int32), half_rows, ctx_count)
    ref_all = lax.all_gather(ref_term, ("ctx", "head"), axis=0, tiled=True)
    ends = jnp.cumsum(seg_lengths)
    starts = ends - seg_lengths
    inside = (my_pos[:, None] >= starts[None, :]) & (my_pos[:, None] < ends[None, :])
    seg_term = jnp.sum(jnp.where(inside, seg_return[None, :], 0.0), axis=1)
    weight = jnp.exp(seg_term - ref_all[owner_slot])
    grad_out = (weight[:, None] * cotangent.astype(jnp.float32)).astype(jnp.bfloat16)
    query_rows = queries.reshape(row_count, kv_heads, -1, E)
    grad_rows = grad_out.reshape(row_count, kv_heads, -1, E)
    group_count = query_rows.shape[2]
    kv_stack = jnp.stack([keys, values])
    context = (my_index, query_rows, grad_rows, my_pos, half_rows, score_scale)
    stat_shape = (kv_heads, group_count, row_count)
    start_stats = (
        jnp.full(stat_shape, NEG, jnp.float32),
        jnp.zeros(stat_shape, jnp.float32),
        jnp.zeros(stat_shape, jnp.float32),
    )
    row_stats = forward_visit(start_stats, kv_stack, my_index, context)

    def forward_turn(turn_index, carry):
        stats_now, visiting = carry
        visiting = jax.tree.map(
            lambda part, own: part.astype(own.dtype),
            passed_along(shortened(visiting), "ctx", 1),
            visiting,
        )
        owner = (my_index - turn_index) % ctx_count
        return (forward_visit(stats_now, visiting, owner, context), visiting)

    row_stats, unused_keys = lax.fori_loop(1, ctx_count, forward_turn, (row_stats, kv_stack))
    run_max, run_total, run_dot = row_stats
    log_total = run_max + jnp.log(run_total)
    dot_total = run_dot / run_total
    back_context = (
        my_index,
        query_rows,
        grad_rows,
        my_pos,
        half_rows,
        score_scale,
        log_total,
        dot_total,
    )
    q_zero = jnp.zeros(query_rows.shape, jnp.float32)
    kv_zero = jnp.zeros(kv_stack.shape, jnp.float32)
    q_accum, own_grads = backward_visit((q_zero, kv_zero), kv_stack, my_index, back_context)

    def backward_turn(turn_index, carry):
        q_now, kv_accum, visiting = carry
        visiting = jax.tree.map(
            lambda part, own: part.astype(own.dtype),
            passed_along(shortened(visiting), "ctx", 1),
            visiting,
        )
        kv_accum = passed_along(kv_accum, "ctx", 1)
        owner = (my_index - turn_index) % ctx_count
        q_now, kv_accum = backward_visit((q_now, kv_accum), visiting, owner, back_context)
        return (q_now, kv_accum, visiting)

    q_accum, kv_accum, unused_keys = lax.fori_loop(
        1, ctx_count, backward_turn, (q_accum, own_grads, kv_stack)
    )
    kv_grads = jax.tree.map(
        lambda part, own: part.astype(own.dtype),
        passed_along(shortened(kv_accum), "ctx", 1),
        kv_accum,
    )
    grad_queries = q_accum.reshape(row_count, -1).astype(jnp.bfloat16)
    grad_keys = kv_grads[0].astype(jnp.bfloat16)
    grad_values = kv_grads[1].astype(jnp.bfloat16)
    return (grad_queries, grad_keys, grad_values)


def solution(mesh):
    return jax.shard_map(
        per_device,
        mesh=mesh,
        in_specs=(
            P("ctx", "head"),
            P("ctx", "head"),
            P("ctx", "head"),
            P("ctx", "head"),
            P(),
            P(),
            P("ctx"),
            P(("ctx", "head")),
        ),
        out_specs=(P("ctx", "head"), P("ctx", "head"), P("ctx", "head")),
        check_vma=False,
    )
```

profile of v0, /device:TPU:1, one launch (start us, length us, event | category | flops | bytes accessed | tf_op | source)
XLA Modules:
  0.0 2321.8 jit_solution(7169393291617382829)
XLA Ops:
  3.8 111.1 %all-reduce = f32[8192]{0:T(1024)S(1)} all-reduce(f32[8192]{0:T(1024)S(1)} %dynamic-update-slice.6), channel_id=1, replica_groups=mesh['ctx'=64,'head'=8] {'ctx','head'}, use_global_device_ids=true, to_apply=%add | all-reduce | flops 8192 | bytes 65536
  119.3 1045.0 %while.44 = (s32[]{:T(128)}, f32[1,6,128]{2,1,0:T(8,128)S(1)}, f32[1,6,128]{2,1,0:T(8,128)S(1)}, f32[1,6,128]{2,1,0:T(8,128)S(1)}, bf16[2,128,128]{2,1,0:T(8,128...) while((s32[]{:T(128)}, f32[1,6,128]{2,1,0:T(8,128)S(1)}, ...), condition=%wide.region_18.19_spmd.clone, body=%wide.region_5.18_spmd.clone.sunk | while | flops 51334032 | bytes 2287194 | solution.py:239
  144.0 12.3 collective-permute-done
  160.8 12.3 collective-permute-done
  177.6 12.3 collective-permute-done
  194.3 12.3 collective-permute-done
  211.1 12.3 collective-permute-done
  227.8 12.3 collective-permute-done
  261.3 12.3 collective-permute-done
  278.1 12.3 collective-permute-done
  328.4 12.3 collective-permute-done
  345.1 12.3 collective-permute-done
  395.4 12.3 collective-permute-done
  412.2 12.3 collective-permute-done
  462.4 12.3 collective-permute-done
  479.2 12.3 collective-permute-done
  529.5 12.3 collective-permute-done
  546.2 12.3 collective-permute-done
  579.7 12.3 collective-permute-done
  596.5 12.3 collective-permute-done
  646.8 12.3 collective-permute-done
  663.5 12.3 collective-permute-done
  713.8 12.3 collective-permute-done
  730.6 12.3 collective-permute-done
  780.8 12.3 collective-permute-done
  797.6 12.3 collective-permute-done
  847.9 12.3 collective-permute-done
  864.6 12.3 collective-permute-done
  898.1 12.3 collective-permute-done
  914.9 12.3 collective-permute-done
  965.2 12.3 collective-permute-done
  1166.0 1140.3 %while.45 = (s32[]{:T(128)}, f32[128,1,6,128]{3,0,2,1:T(8,128)S(1)}, f32[2,128,128]{2,1,0:T(8,128)S(1)}, bf16[2,128,128]{2,1,0:T(8,128)(2,1)S(1)}, s32[]{:T(128)...) while((s32[]{:T(128)}, ...), condition=%wide.region_23.24_spmd.clone, body=%wide.region_19.23_spmd.clone.sunk | while | flops 126812816 | bytes 5318298 | solution.py:269
  (1913 shorter events, 2022.0 us)
Async XLA Ops:
  1185.3 15.1 collective-permute-start.2
  1203.5 15.0 collective-permute-start.2
  1221.6 15.0 collective-permute-start.2
  1257.8 15.0 collective-permute-start.2
  1294.1 15.0 collective-permute-start.2
  1330.3 15.0 collective-permute-start.2
  1366.5 15.0 collective-permute-start.2
  1402.7 15.0 collective-permute-start.2
  1438.9 15.0 collective-permute-start.2
  1475.2 15.0 collective-permute-start.2
  1511.4 15.0 collective-permute-start.2
  1547.6 15.0 collective-permute-start.2
  1583.8 15.0 collective-permute-start.2
  1620.0 15.0 collective-permute-start.2
  1656.2 15.0 collective-permute-start.2
  1692.5 15.0 collective-permute-start.2
  1728.7 15.0 collective-permute-start.2
  1764.9 15.0 collective-permute-start.2
  1801.1 15.0 collective-permute-start.2
  1837.3 15.0 collective-permute-start.2
  1873.6 15.0 collective-permute-start.2
  1909.8 15.0 collective-permute-start.2
  1946.0 15.0 collective-permute-start.2
  1982.2 15.0 collective-permute-start.2
  2018.4 15.0 collective-permute-start.2
  2054.7 15.0 collective-permute-start.2
  2090.9 15.0 collective-permute-start.2
  2127.1 15.0 collective-permute-start.2
  2163.3 15.0 collective-permute-start.2
  2199.5 15.0 collective-permute-start.2
  2235.8 15.0 collective-permute-start.2
  2272.0 15.0 collective-permute-start.2
  (168 other events, 2535.8 us)
where the time goes:
time: 2350 us; the launch traced here: 2320 us
  waiting for transfers between devices  1600 us (68%)
  starting transfers between devices  366 us (16%)
  blocking collectives  111 us (5%)
  matrix products  99 us (4%)
  other arithmetic  75.7 us (3%)
  local copies, waits for them, and re-layouts  58.9 us (3%)
    ppermute x190, waiting for transfers between devices, passed_along(): return lax.ppermute(value, axis, pairs)  1600 us
    ppermute x190, starting transfers between devices, passed_along(): return lax.ppermute(value, axis, pairs)  366 us
    unnamed x1, blocking collectives  111 us
    dot_general x254, matrix products, tile_scores(): jnp.einsum(einsum_form, left_part, right_part, preferred_element_type=jnp...  60.2 us
  transfers between devices with their start and end apart: 190, of which 190 were waited for; matrix products, arithmetic and copies ran while one was open for 0% of the time, Pallas kernels for 0%

commit v1 on v0

v1 whole, which is shorter than its diff:
```python
import functools
import math

import jax
import jax.numpy as jnp
from jax import lax
from jax.experimental import pallas as pl
from jax.experimental.pallas import tpu as pltpu
from jax.sharding import Mesh, PartitionSpec as P

E = 128
GROUP = 6
HALF = 64
ROWS = 2 * HALF
TEAM = 4
QUADS = 4
RING = 4
TILE = RING * HALF
HEAD_COLS = TEAM * HALF
COLS = GROUP * HEAD_COLS
LAST = 2 * (2 * QUADS * RING) * 2 - 1
NEG = -1e30
SCALE = 1.0 / math.sqrt(E)
SCALE2 = SCALE * math.log2(math.e)
LOG2E = math.log2(math.e)
F32 = jnp.float32
BF16 = jnp.bfloat16
I32 = jnp.int32
VMEM = 48 * 1024 * 1024


def dot(left, right, left_dim, right_dim):
    return lax.dot_general(
        left, right, (((left_dim,), (right_dim,)), ((), ())), preferred_element_type=F32
    )


def iota(shape, dim):
    return lax.broadcasted_iota(I32, shape, dim)


def call(kernel, outs, scratch=(), scalars=0, inputs=0, cost=None):
    spec = pl.BlockSpec(memory_space=pltpu.VMEM)
    return pl.pallas_call(
        kernel,
        out_shape=outs,
        in_specs=[pl.BlockSpec(memory_space=pltpu.SMEM)] * scalars + [spec] * inputs,
        out_specs=jax.tree.map(lambda _: spec, outs),
        scratch_shapes=list(scratch),
        compiler_params=pltpu.CompilerParams(vmem_limit_bytes=VMEM),
        cost_estimate=cost,
    )


def pack_kernel(q_ref, g_ref, slot_ref, k_ref, v_ref, qg_ref, kv_ref):
    width = GROUP * E
    qg_ref[:ROWS, :width] = q_ref[...]
    qg_ref[:ROWS, width:] = g_ref[...]
    slot = slot_ref[...]
    row = iota((16, ROWS), 0)
    coded = jnp.where(row == 0, slot >> 7, jnp.where(row == 1, slot & 127, 0))
    qg_ref[ROWS:, :] = jnp.zeros((16, 2 * width), BF16)
    qg_ref[ROWS:, :ROWS] = coded.astype(F32).astype(BF16)
    for copy in range(QUADS):
        kv_ref[copy, :, :E] = k_ref[...]
        kv_ref[copy, :, E:] = v_ref[...]


def arrange(slots, refs, first, out_ref):
    for group in range(2):
        for head in range(GROUP):
            for ref, slot in zip(refs, slots):
                start = pl.multiple_of(head * HEAD_COLS + slot * HALF, HALF)
                column = first + head * E
                out_ref[group, pl.ds(start, HALF), :] = ref[
                    group * HALF : (group + 1) * HALF, column : column + E
                ]


def place(where_ref):
    quad, pair, ring, core = (where_ref[i] for i in range(4))
    mine = 2 * pair + core
    return quad, pair, ring, core, (mine, mine ^ 1, mine ^ 2, mine ^ 3)


def causal_mask(group, quad, pair, ring, core):
    key_row = iota((TILE, 1), 0)
    key_owner = 2 * ((2 * quad + pair) * RING + (key_row >> 6)) + core
    column = iota((1, HEAD_COLS), 1)
    slot = column >> 6
    query_owner = 2 * ((2 * quad + (slot >> 1)) * RING + ring) + (slot & 1)
    if group == 1:
        key_owner, query_owner = LAST - key_owner, LAST - query_owner
    key_pos = key_owner * HALF + (key_row & 63)
    query_pos = query_owner * HALF + (column & 63)
    return key_pos <= query_pos


def free_visit(index, quad):
    wide = index < QUADS
    rest = index - QUADS
    early = rest < quad
    group = jnp.where(wide, 1, jnp.where(early, 0, 1))
    half = jnp.where(wide, 0, jnp.where(early, 0, 1))
    part = jnp.where(wide, index, jnp.where(early, rest, rest + 1))
    return group, half, part


def key_value_tile(kv_ref, half, part):
    start = pl.multiple_of(half * HALF, HALF)
    return kv_ref[:, part, pl.ds(start, HALF), :].reshape(TILE, 2 * E)


def forward_kernel(
    where_ref, qg0_ref, qg1_ref, qg2_ref, qg3_ref, kv_ref, table_ref, length_ref, return_ref,
    stat_ref, qs_ref, gs_ref, top_ref, sum_ref, term_ref,
):
    quad, pair, ring, core, slots = place(where_ref)
    refs = (qg0_ref, qg1_ref, qg2_ref, qg3_ref)
    arrange(slots, refs, 0, qs_ref)
    arrange(slots, refs, GROUP * E, gs_ref)
    top_ref[...] = jnp.full(top_ref.shape, NEG, F32)
    sum_ref[...] = jnp.zeros(sum_ref.shape, F32)
    term_ref[...] = jnp.zeros(term_ref.shape, F32)

    def visit(group, half, part, mask):
        key_value = key_value_tile(kv_ref, half, part)
        key, value = key_value[:, :E], key_value[:, E:]
        for head in range(GROUP):
            cols = slice(head * HEAD_COLS, (head + 1) * HEAD_COLS)
            scores = dot(key, qs_ref[group, cols, :], 1, 1) * SCALE2
            dots = dot(value, gs_ref[group, cols, :], 1, 1)
            if mask is not None:
                scores = jnp.where(mask, scores, NEG)
            scores = scores.reshape(TILE // 8, 8, HEAD_COLS)
            dots = dots.reshape(TILE // 8, 8, HEAD_COLS)
            old = top_ref[group, :, cols]
            top = jnp.maximum(old, jnp.max(scores, axis=0))
            factor = jnp.exp2(old - top)
            prob = jnp.exp2(scores - top[None])
            top_ref[group, :, cols] = top
            sum_ref[group, :, cols] = factor * sum_ref[group, :, cols] + jnp.sum(prob, axis=0)
            term_ref[group, :, cols] = factor * term_ref[group, :, cols] + jnp.sum(
                prob * dots, axis=0
            )

    @pl.loop(0, 2 * QUADS - 1)
    def _(index):
        visit(*free_visit(index, quad), None)

    for group in range(2):
        visit(group, group, quad, causal_mask(group, quad, pair, ring, core))

    stat_ref[...] = jnp.zeros(stat_ref.shape, F32)
    for group in range(2):
        top = top_ref[group]
        best = jnp.max(top, axis=0, keepdims=True)
        factor = jnp.exp2(top - best)
        stat_ref[3 * group : 3 * group + 1, :] = best
        stat_ref[3 * group + 1 : 3 * group + 2, :] = jnp.sum(
            factor * sum_ref[group], axis=0, keepdims=True
        )
        stat_ref[3 * group + 2 : 3 * group + 3, :] = jnp.sum(
            factor * term_ref[group], axis=0, keepdims=True
        )

    table = table_ref[...].reshape(QUADS * RING * 8, E)
    high = table.astype(BF16)
    rest = table - high.astype(F32)
    middle = rest.astype(BF16)
    low = (rest - middle.astype(F32)).astype(BF16)
    lane = iota((E, ROWS), 0)
    line = iota((8, ROWS), 0)
    block = jnp.zeros((8, ROWS), F32)
    for ref, slot in zip(refs, slots):
        code = ref[ROWS : ROWS + 16, :ROWS].astype(F32)
        owner = code[0:1].astype(I32)
        entry = code[1:2].astype(I32)
        pick = (lane == (entry & 15)).astype(F32).astype(BF16)
        picked = dot(high, pick, 1, 0) + dot(middle, pick, 1, 0) + dot(low, pick, 1, 0)
        row = ((owner >> 4) * RING + ((owner >> 1) & 3)) * 8 + (entry >> 4)
        held = (((owner >> 3) & 1) == pair) & ((owner & 1) == core)
        row = jnp.where(held, row, -1)
        part = jnp.sum(jnp.where(lane == row, picked, 0.0), axis=0, keepdims=True)
        block = jnp.where(line == slot, part, block)
    before = iota((E, E), 1) <= iota((E, E), 0)
    ends = jnp.sum(
        jnp.where(before, length_ref[...].astype(F32), 0.0), axis=1, keepdims=True
    )
    own = iota((E, E), 1) == iota((E, E), 0)
    lengths = jnp.sum(jnp.where(own, length_ref[...].astype(F32), 0.0), axis=1, keepdims=True)
    returns = jnp.sum(jnp.where(own, return_ref[...], 0.0), axis=1, keepdims=True)
    starts = ends - lengths
    column = iota((1, ROWS), 1)
    for slot in range(TEAM):
        owner = 2 * ((2 * quad + slot // 2) * RING + ring) + slot % 2
        place_of = jnp.where(column < HALF, owner, LAST - owner)
        pos = (place_of * HALF + (column & 63)).astype(F32)
        inside = (pos >= starts) & (pos < ends)
        part = jnp.sum(jnp.where(inside, returns, 0.0), axis=0, keepdims=True)
        block = jnp.where(line == TEAM + slot, part, block)
    stat_ref[8:16, :ROWS] = block


def backward_kernel(
    where_ref, qg0_ref, qg1_ref, qg2_ref, qg3_ref, kv_ref,
    stat0_ref, stat1_ref, stat2_ref, stat3_ref,
    dkv_ref, dq0_ref, dqc_ref, dq2_ref,
    qs_ref, gs_ref, dqt_ref, acc_ref, shift_ref, term_ref, prob_ref, slope_ref, turn_ref,
):
    quad, pair, ring, core, slots = place(where_ref)
    refs = (qg0_ref, qg1_ref, qg2_ref, qg3_ref)
    stats = (stat0_ref, stat1_ref, stat2_ref, stat3_ref)
    arrange(slots, refs, 0, qs_ref)
    arrange(slots, refs, GROUP * E, gs_ref)
    dqt_ref[...] = jnp.zeros(dqt_ref.shape, F32)
    acc_ref[...] = jnp.zeros(acc_ref.shape, F32)
    logw = [
        stat0_ref[12 + s : 13 + s, :ROWS] - sum(st[8 + s : 9 + s, :ROWS] for st in stats)
        for s in range(TEAM)
    ]
    low_lane = iota((1, ROWS), 1) < HALF
    for group in range(2):
        tops = [st[3 * group : 3 * group + 1, :] for st in stats]
        best = functools.reduce(jnp.maximum, tops)
        factors = [jnp.exp2(top - best) for top in tops]
        total = sum(f * st[3 * group + 1 : 3 * group + 2, :] for f, st in zip(factors, stats))
        term = sum(f * st[3 * group + 2 : 3 * group + 3, :] for f, st in zip(factors, stats))
        shift = best + jnp.log2(total)
        term_ref[group] = term / total
        pieces = []
        for first in (0, 2):
            a, b = logw[first], logw[first + 1]
            if group == 0:
                b = pltpu.roll(jnp.broadcast_to(b, (8, ROWS)), HALF, 1)[0:1]
            else:
                a = pltpu.roll(jnp.broadcast_to(a, (8, ROWS)), HALF, 1)[0:1]
            pieces.append(jnp.where(low_lane, a, b))
        weights = jnp.concatenate(pieces, axis=1) * LOG2E
        for head in range(GROUP):
            cols = slice(head * HEAD_COLS, (head + 1) * HEAD_COLS)
            shift_ref[group, :, cols] = shift[:, cols] - weights

    def visit(group, half, part, mask):
        key_value = key_value_tile(kv_ref, half, part)
        key, value = key_value[:, :E], key_value[:, E:]
        for head in range(GROUP):
            cols = slice(head * HEAD_COLS, (head + 1) * HEAD_COLS)
            scores = dot(key, qs_ref[group, cols, :], 1, 1) * SCALE2
            dots = dot(value, gs_ref[group, cols, :], 1, 1)
            if mask is not None:
                scores = jnp.where(mask, scores, NEG)
            prob = jnp.exp2(scores - shift_ref[group, :, cols])
            prob_ref[:, cols] = prob.astype(BF16)
            slope_ref[:, cols] = (prob * (dots - term_ref[group, :, cols])).astype(BF16)
        slope = slope_ref[...]
        acc_ref[half, part, :, :E] += dot(slope, qs_ref[group], 1, 0)
        acc_ref[half, part, :, E:] += dot(prob_ref[...], gs_ref[group], 1, 0)
        dqt_ref[group] += dot(key, slope, 0, 0)

    @pl.loop(0, 2 * QUADS - 1)
    def _(index):
        visit(*free_visit(index, quad), None)

    for group in range(2):
        visit(group, group, quad, causal_mask(group, quad, pair, ring, core))

    scales = jnp.where(iota((1, 2 * E), 1) < E, SCALE, 1.0)
    for half in range(2):
        for part in range(QUADS):
            tile = (acc_ref[half, part] * scales).astype(BF16)
            dkv_ref[:, part, half * HALF : (half + 1) * HALF, :] = tile.reshape(RING, HALF, 2 * E)
    targets = (dq0_ref, dqc_ref.at[0], dq2_ref, dqc_ref.at[1])
    for group in range(2):
        for head in range(GROUP):
            cols = slice(head * HEAD_COLS, (head + 1) * HEAD_COLS)
            turn_ref[...] = dqt_ref[group, :, cols].T * SCALE
            for ref, slot in zip(targets, slots):
                start = pl.multiple_of(slot * HALF, HALF)
                ref[group * HALF : (group + 1) * HALF, head * E : (head + 1) * E] = turn_ref[
                    pl.ds(start, HALF), :
                ].astype(ref.dtype)


def shape(dims, dtype):
    return jax.ShapeDtypeStruct(dims, dtype)


def swapped(x, axis):
    return lax.ppermute(x, axis, [(0, 1), (1, 0)])


def both_swapped(x):
    return lax.ppermute(x, ("pair", "core"), [(i, 3 - i) for i in range(4)])


def per_device(queries, keys, values, cotangent, seg_lengths, seg_return, owner_slot, ref_term):
    quad, pair = lax.axis_index("quad"), lax.axis_index("pair")
    ring, core = lax.axis_index("ring"), lax.axis_index("core")
    where = jnp.stack([quad, pair, ring, core]).astype(I32)
    width = GROUP * E

    qg, kv_own = call(
        pack_kernel,
        (shape((ROWS + 16, 2 * width), BF16), shape((QUADS, ROWS, 2 * E), BF16)),
        inputs=5,
    )(queries, cotangent, owner_slot.reshape(1, ROWS), keys, values)

    head = lax.axis_index("col") * 2 + lax.axis_index("far")
    terms = jnp.pad(ref_term.reshape(1, 16), ((0, 7), (0, E - 16)))
    terms = jnp.where(iota((8, E), 0) == head, terms[0:1], 0.0)
    terms = terms + swapped(terms, "far")
    for step in (1, 2):
        terms = terms + lax.ppermute(terms, "col", [(i, i ^ step) for i in range(4)])

    kv_z = lax.all_to_all(kv_own, "quad", 0, 0, tiled=True)
    qg1 = swapped(qg, "core")
    qg2 = swapped(qg, "pair")
    qg3 = swapped(qg2, "core")
    kv_all = lax.all_to_all(
        jnp.broadcast_to(kv_z[None], (RING, QUADS, ROWS, 2 * E)), "ring", 0, 0, tiled=True
    )
    table = lax.all_to_all(
        jnp.broadcast_to(terms[None], (QUADS * RING, 8, E)), ("quad", "ring"), 0, 0, tiled=True
    )
    team = (qg, qg1, qg2, qg3)
    pairs = 9 * TILE * COLS
    kv_scratch = [pltpu.VMEM((2, COLS, E), BF16), pltpu.VMEM((2, COLS, E), BF16)]
    stat = call(
        forward_kernel,
        shape((16, COLS), F32),
        kv_scratch + [pltpu.VMEM((2, 8, COLS), F32)] * 3,
        scalars=1,
        inputs=8,
        cost=pl.CostEstimate(flops=4 * E * pairs, bytes_accessed=4 << 20, transcendentals=pairs),
    )(where, *team, kv_all, table, seg_lengths.reshape(1, E), seg_return.reshape(1, E))

    stats = (stat, swapped(stat, "core"), swapped(stat, "pair"), both_swapped(stat))
    dkv, dq0, dqc, dq2 = call(
        backward_kernel,
        (
            shape((RING, QUADS, ROWS, 2 * E), BF16),
            shape((ROWS, width), F32),
            shape((2, ROWS, width), BF16),
            shape((ROWS, width), F32),
        ),
        kv_scratch
        + [
            pltpu.VMEM((2, E, COLS), F32),
            pltpu.VMEM((2, QUADS, TILE, 2 * E), F32),
            pltpu.VMEM((2, 1, COLS), F32),
            pltpu.VMEM((2, 1, COLS), F32),
            pltpu.VMEM((TILE, COLS), BF16),
            pltpu.VMEM((TILE, COLS), BF16),
            pltpu.VMEM((HEAD_COLS, E), F32),
        ],
        scalars=1,
        inputs=9,
        cost=pl.CostEstimate(flops=10 * E * pairs, bytes_accessed=5 << 20, transcendentals=pairs),
    )(where, *team, kv_all, *stats)

    from_core = swapped(dqc, "core").astype(F32)
    from_pair = swapped((dq2 + from_core[1]).astype(BF16), "pair").astype(F32)
    grad_queries = (dq0 + from_core[0] + from_pair).astype(BF16)

    parts = lax.all_to_all(dkv, "ring", 0, 0, tiled=True)
    parts = jnp.sum(parts.astype(F32), axis=0).astype(BF16)
    parts = lax.all_to_all(parts, "quad", 0, 0, tiled=True)
    kv_grad = jnp.sum(parts.astype(F32), axis=0).astype(BF16)
    return grad_queries, kv_grad[:, :E], kv_grad[:, E:]


def solution(mesh):
    fine = Mesh(
        mesh.devices.reshape(QUADS, 2, RING, 2, 4, 2),
        ("quad", "pair", "ring", "core", "col", "far"),
    )
    ctx = ("quad", "pair", "ring", "core")
    head = ("col", "far")
    return jax.shard_map(
        per_device,
        mesh=fine,
        in_specs=(
            P(ctx, head), P(ctx, head), P(ctx, head), P(ctx, head),
            P(), P(), P(ctx), P(ctx + head),
        ),
        out_specs=(P(ctx, head), P(ctx, head), P(ctx, head)),
        check_vma=False,
    )
```

time: 2350 us -> 161 us (0.07); the launches traced: 2320 us -> 159 us
  waiting for transfers between devices: 1600 us -> 45.5 us
  starting transfers between devices: 366 us -> 83.7 us
  blocking collectives: 111 us -> 0 us
  matrix products: 99 us -> 0 us
  other arithmetic: 75.7 us -> 2.09 us
  local copies, waits for them, and re-layouts: 58.9 us -> 7.1 us
    ppermute x190 -> x11, waiting for transfers between devices: 1600 us -> 12.1 us  [the longest x8 9.65 us: swapped(): return lax.ppermute(x, axis, [(0, 1), (1, 0)])]
    ppermute x190 -> x11, starting transfers between devices: 366 us -> 59.3 us  [the longest x8 39.2 us: swapped(): return lax.ppermute(x, axis, [(0, 1), (1, 0)])]
    unnamed x1 -> x0, blocking collectives: 111 us -> none
    dot_general x446 -> x0, matrix products: 99 us -> none  [the longest x254 60.2 us: tile_scores(): jnp.einsum(einsum_form, left_part, right_part, preferred_element_type=jnp...]
    concatenate x124 -> x0, other arithmetic: 46.5 us -> none  [forward_later(): jnp.concatenate([old_stat[..., :half_rows], new_stat], axis=-1)]
    while x253 -> x0, local copies, waits for them, and re-layouts: 44.8 us -> none
    all_to_all x0 -> x5, waiting for transfers between devices: none -> 33.4 us  [the longest x1 13 us: per_device(): parts = lax.all_to_all(dkv, 'ring', 0, 0, tiled=True)]
    all_to_all x0 -> x5, starting transfers between devices: none -> 24.4 us  [the longest x1 10.4 us: per_device(): lax.all_to_all(jnp.broadcast_to(terms[None], (QUADS * RING, 8, E)), ('qua...]
  transfers between devices with their start and end apart: 190 -> 16, of which waited for: 190 -> 10; matrix products, arithmetic and copies ran while one was open for 0% -> 2% of each run, Pallas kernels for 0% -> 0%
where the time goes in v1:
time: 161 us; the launch traced here: 159 us
  starting transfers between devices  83.7 us (52%)
  waiting for transfers between devices  45.5 us (28%)
  Pallas kernels  20.1 us (12%)
  local copies, waits for them, and re-layouts  7.1 us (4%)
  other arithmetic  2.09 us (1%)
    ppermute x8, starting transfers between devices, swapped(): return lax.ppermute(x, axis, [(0, 1), (1, 0)])  39.2 us
    all_to_all x1, waiting for transfers between devices, per_device(): parts = lax.all_to_all(dkv, 'ring', 0, 0, tiled=True)  13 us
    ppermute x1, starting transfers between devices, both_swapped(): return lax.ppermute(x, ('pair', 'core'), [(i, 3 - i) for i in range(4)])  12.3 us
    pallas_call x1, Pallas kernels, per_device(): call(backward_kernel, (shape((RING, QUADS, ROWS, 2 * E), BF16), shape((RO...  12 us
    all_to_all x1, starting transfers between devices, per_device(): lax.all_to_all(jnp.broadcast_to(terms[None], (QUADS * RING, 8, E)), ('qua...  10.4 us
    ppermute x8, waiting for transfers between devices, swapped(): return lax.ppermute(x, axis, [(0, 1), (1, 0)])  9.65 us
    all_to_all x1, waiting for transfers between devices, per_device(): lax.all_to_all(jnp.broadcast_to(terms[None], (QUADS * RING, 8, E)), ('qua...  8.81 us
    ppermute x2, starting transfers between devices, per_device(): lax.ppermute(terms, 'col', [(i, i ^ step) for i in range(4)])  7.75 us
  transfers between devices with their start and end apart: 16, of which 10 were waited for; matrix products, arithmetic and copies ran while one was open for 2% of the time, Pallas kernels for 0%

profile of v1, /device:TPU:1, one launch (start us, length us, event | category | flops | bytes accessed | tf_op | source)
XLA Modules:
  0.0 159.3 jit_solution(8433734013540807653)
XLA Ops:
  1.4 16.3 %collective-permute-start.3 = (f32[8,128]{1,0:T(8,128)S(1)}, f32[8,128]{1,0:T(8,128)S(1)}, u32[]{:S(2)}, u32[]{:S(2)}) collective-permute-start(f32[8,128]{1,0:T(8,128)S(1)} %broadcast_select_fusion), channel_id=1, source_target_pairs={{0,1},{1,0},{2,3},{3,2},{4,5},{5,4},{6,7},{7,6},{8,9},{9,8},{10,11... | collective-permute-start | bytes 12296 | tf_op jit(solution)/shard_map/ppermute | solution.py:290
  17.7 1.0 collective-permute-done.3
  18.8 3.1 %collective-permute-start.4 = (f32[8,128]{1,0:T(8,128)S(1)}, f32[8,128]{1,0:T(8,128)S(1)}, u32[]{:S(2)}, u32[]{:S(2)}) collective-permute-start(f32[8,128]{1,0:T(8,128)S(1)} %fusion.5), channel_id=1, source_target_pairs={{0,2},{2,0},{4,6},{6,4},{1,3},{3,1},{5,7},{7,5},{8,10},{10,8},{12,... | collective-permute-start | bytes 12296 | tf_op jit(solution)/shard_map/ppermute | solution.py:314
  21.9 1.2 collective-permute-done.4
  23.2 4.6 %collective-permute-start.5 = (f32[8,128]{1,0:T(8,128)S(1)}, f32[8,128]{1,0:T(8,128)S(1)}, u32[]{:S(2)}, u32[]{:S(2)}) collective-permute-start(f32[8,128]{1,0:T(8,128)S(1)} %fusion.8), channel_id=1, source_target_pairs={{0,4},{2,6},{4,0},{6,2},{1,5},{3,7},{5,1},{7,3},{8,12},{10,14},{12... | collective-permute-start | bytes 12296 | tf_op jit(solution)/shard_map/ppermute | solution.py:314
  27.8 1.2 collective-permute-done.5
  29.7 10.4 %all-to-all-start.2 = ((f32[16,8,128]{2,1,0:T(8,128)}), f32[16,8,128]{2,1,0:T(8,128)S(1)}, u32[]{:S(2)}, u32[]{:S(2)}) async-start(f32[16,8,128]{2,1,0:T(8,128)} %broadcast_in_dim.30), calls=%async_computation.2 | async-start | bytes 131072 | tf_op jit(solution)/shard_map/all_to_all | solution.py:323
  40.7 0.9 copy-done.1
  42.4 8.8 %all-to-all-done.2.table_ref = f32[16,8,128]{2,1,0:T(8,128)S(1)} async-done(((f32[16,8,128]{2,1,0:T(8,128)}), f32[16,8,128]{2,1,0:T(8,128)S(1)}, u32[]{:S(2)}, u32[]{:S(2)}) %all-to-all-start.2) | async-done | bytes 65568 | tf_op jit(solution)/shard_map/all_to_all | solution.py:323
  51.2 3.4 %all-to-all-start = ((bf16[4,128,256]{2,1,0:T(8,128)(2,1)}), bf16[4,128,256]{2,1,0:T(8,128)(2,1)S(1)}, u32[]{:S(2)}, u32[]{:S(2)}) async-start(bf16[4,128,256]{2,1,0:T(8,128)(2,1)} %get-tuple-element.10), calls=%async_computation | async-start | bytes 524288 | tf_op jit(solution)/shard_map/all_to_all | solution.py:316
  54.6 3.5 %collective-permute-start.1 = (bf16[144,1536]{1,0:T(8,128)(2,1)S(1)}, bf16[144,1536]{1,0:T(8,128)(2,1)S(1)}, u32[]{:S(2)}, u32[]{:S(2)}) collective-permute-start(bf16[144,1536]{1,0:T(8,128)(2,1)S(1)} %get-tuple-element.9.qg0_ref), channel_id=1, source_target_pairs={{0,64},{64,0},{1,65},{65,1},{2,66},{66,2},{3,67},{67,3},{4,68},{68... | collective-permute-start | bytes 1327112 | tf_op jit(solution)/shard_map/ppermute | solution.py:290
  58.2 5.7 %all-to-all-done = bf16[4,128,256]{2,1,0:T(8,128)(2,1)S(1)} async-done(((bf16[4,128,256]{2,1,0:T(8,128)(2,1)}), bf16[4,128,256]{2,1,0:T(8,128)(2,1)S(1)}, u32[]{:S(2)}, u32[]{:S(2)}) %all-to-all-start) | async-done | bytes 262176 | tf_op jit(solution)/shard_map/all_to_all | solution.py:316
  63.9 1.1 broadcast_in_dim.26
  65.0 3.5 %all-to-all-start.1 = ((bf16[4,4,128,256]{3,2,1,0:T(8,128)(2,1)}), bf16[4,4,128,256]{3,2,1,0:T(8,128)(2,1)S(1)}, u32[]{:S(2)}, u32[]{:S(2)}) async-start(bf16[4,4,128,256]{3,2,1,0:T(8,128)(2,1)} %broadcast_in_dim.26), calls=%async_computation.1 | async-start | bytes 2097152 | tf_op jit(solution)/shard_map/all_to_all | solution.py:320
  68.5 8.5 %collective-permute-start = (bf16[144,1536]{1,0:T(8,128)(2,1)S(1)}, bf16[144,1536]{1,0:T(8,128)(2,1)S(1)}, u32[]{:S(2)}, u32[]{:S(2)}) collective-permute-start(bf16[144,1536]{1,0:T(8,128)(2,1)S(1)} %get-tuple-element.9.qg0_ref), channel_id=1, source_target_pairs={{0,8},{8,0},{1,9},{9,1},{2,10},{10,2},{3,11},{11,3},{4,12},{12,4},... | collective-permute-start | bytes 1327112 | tf_op jit(solution)/shard_map/ppermute | solution.py:290
  77.0 1.9 %collective-permute-start.2 = (bf16[144,1536]{1,0:T(8,128)(2,1)S(1)}, bf16[144,1536]{1,0:T(8,128)(2,1)S(1)}, u32[]{:S(2)}, u32[]{:S(2)}) collective-permute-start(bf16[144,1536]{1,0:T(8,128)(2,1)S(1)} %collective-permute-done.1.qg2_ref), channel_id=1, source_target_pairs={{0,8},{8,0},{1,9},{9,1},{2,10},{10,2},{3,11},{11,3},{4,12},{12,4},... | collective-permute-start | bytes 1327112 | tf_op jit(solution)/shard_map/ppermute | solution.py:290
  79.1 1.7 %collective-permute-done.2.qg3_ref = bf16[144,1536]{1,0:T(8,128)(2,1)S(1)} collective-permute-done((bf16[144,1536]{1,0:T(8,128)(2,1)S(1)}, bf16[144,1536]{1,0:T(8,128)(2,1)S(1)}, u32[]{:S(2)}, u32[]{:S(2)}) %collective-permute-start.2) | collective-permute-done | bytes 442400 | tf_op jit(solution)/shard_map/ppermute | solution.py:290
  81.5 7.3 %shard_map.104.stat0_ref = f32[16,1536]{1,0:T(8,128)S(1)} custom-call(s32[4]{0:T(128)S(1)} %pad_add_fusion.where_ref, bf16[144,1536]{1,0:T(8,128)(2,1)S(1)} %get-tuple-element.9.qg0_ref, bf16[144,1536]{1,0:T(8,128)(2,1)S(1)} %collective-permute-done.qg1_ref, bf16[144,1536]{1,0:T(8,128)(2,1)S(1)} %collective-permute-done.1.qg2_ref, ...), custom_call_target="tpu_custom_call" | custom-call | flops 1811939328 | bytes 4194304 | tf_op jit(solution)/shard_map/pallas_call | solution.py:329
  88.8 12.3 %collective-permute-start.8 = (f32[16,1536]{1,0:T(8,128)S(1)}, f32[16,1536]{1,0:T(8,128)S(1)}, u32[]{:S(2)}, u32[]{:S(2)}) collective-permute-start(f32[16,1536]{1,0:T(8,128)S(1)} %shard_map.104.stat0_ref), channel_id=1, source_target_pairs={{0,72},{8,64},{64,8},{72,0},{1,73},{9,65},{65,9},{73,1},{2,74},{10... | collective-permute-start | bytes 294920 | tf_op jit(solution)/shard_map/ppermute | solution.py:294
  101.2 1.9 %collective-permute-start.7 = (f32[16,1536]{1,0:T(8,128)S(1)}, f32[16,1536]{1,0:T(8,128)S(1)}, u32[]{:S(2)}, u32[]{:S(2)}) collective-permute-start(f32[16,1536]{1,0:T(8,128)S(1)} %shard_map.104.stat0_ref), channel_id=1, source_target_pairs={{0,64},{64,0},{1,65},{65,1},{2,66},{66,2},{3,67},{67,3},{4,68},{68... | collective-permute-start | bytes 294920 | tf_op jit(solution)/shard_map/ppermute | solution.py:290
  103.1 2.3 %collective-permute-start.6 = (f32[16,1536]{1,0:T(8,128)S(1)}, f32[16,1536]{1,0:T(8,128)S(1)}, u32[]{:S(2)}, u32[]{:S(2)}) collective-permute-start(f32[16,1536]{1,0:T(8,128)S(1)} %shard_map.104.stat0_ref), channel_id=1, source_target_pairs={{0,8},{8,0},{1,9},{9,1},{2,10},{10,2},{3,11},{11,3},{4,12},{12,4},... | collective-permute-start | bytes 294920 | tf_op jit(solution)/shard_map/ppermute | solution.py:290
  105.4 1.1 collective-permute-done.7.stat2_ref
  106.5 1.0 copy-done.6
  107.5 12.0 %shard_map.105 = (bf16[4,4,128,256]{3,2,1,0:T(8,128)(2,1)}, f32[128,768]{1,0:T(8,128)S(1)}, bf16[2,128,768]{2,1,0:T(8,128)(2,1)S(1)}, f32[128,768]{1,0:T(8,128)S(1)}) custom-call(s32[4]{0:T(128)S(1)} %pad_add_fusion.where_ref, bf16[144,1536]{1,0:T(8,128)(2,1)S(1)} %get-tuple-element.9.qg0_ref, bf16[144,1536]{1,0:T(8,128)(2,1)S(1)} %collective-permute-done.qg1_ref, ...), custom_call_target="tpu_custom_call" | custom-call | flops 4529848320 | bytes 5242880 | tf_op jit(solution)/shard_map/pallas_call | solution.py:339
  120.2 3.6 %all-to-all-start.3 = ((bf16[4,4,128,256]{3,2,1,0:T(8,128)(2,1)}), bf16[4,4,128,256]{3,2,1,0:T(8,128)(2,1)S(1)}, u32[]{:S(2)}, u32[]{:S(2)}) async-start(bf16[4,4,128,256]{3,2,1,0:T(8,128)(2,1)} %get-tuple-element.14), calls=%async_computation.3 | async-start | bytes 2097152 | tf_op jit(solution)/shard_map/all_to_all | solution.py:366
  123.9 2.1 %collective-permute-start.9 = (bf16[2,128,768]{2,1,0:T(8,128)(2,1)S(1)}, bf16[2,128,768]{2,1,0:T(8,128)(2,1)S(1)}, u32[]{:S(2)}, u32[]{:S(2)}) collective-permute-start(bf16[2,128,768]{2,1,0:T(8,128)(2,1)S(1)} %copy-done.8), channel_id=1, source_target_pairs={{0,8},{8,0},{1,9},{9,1},{2,10},{10,2},{3,11},{11,3},{4,12},{12,4},... | collective-permute-start | bytes 1179656 | tf_op jit(solution)/shard_map/ppermute | solution.py:290
  126.0 13.0 %all-to-all-done.3 = bf16[4,4,128,256]{3,2,1,0:T(8,128)(2,1)S(1)} async-done(((bf16[4,4,128,256]{3,2,1,0:T(8,128)(2,1)}), bf16[4,4,128,256]{3,2,1,0:T(8,128)(2,1)S(1)}, u32[]{:S(2)}, u32[]{:S(2)}) %all-to-all-start.3) | async-done | bytes 1048608 | tf_op jit(solution)/shard_map/all_to_all | solution.py:366
  138.9 0.9 reduce_sum.24
  139.8 3.4 %all-to-all-start.4 = ((bf16[4,128,256]{2,1,0:T(8,128)(2,1)}), bf16[4,128,256]{2,1,0:T(8,128)(2,1)S(1)}, u32[]{:S(2)}, u32[]{:S(2)}) async-start(bf16[4,128,256]{2,1,0:T(8,128)(2,1)} %reduce_sum.24), calls=%async_computation.4 | async-start | bytes 524288 | tf_op jit(solution)/shard_map/all_to_all | solution.py:368
  143.4 2.7 %collective-permute-start.10 = (bf16[128,768]{1,0:T(8,128)(2,1)S(1)}, bf16[128,768]{1,0:T(8,128)(2,1)S(1)}, u32[]{:S(2)}, u32[]{:S(2)}) collective-permute-start(bf16[128,768]{1,0:T(8,128)(2,1)S(1)} %fusion.1), channel_id=1, source_target_pairs={{0,64},{64,0},{1,65},{65,1},{2,66},{66,2},{3,67},{67,3},{4,68},{68... | collective-permute-start | bytes 589832 | tf_op jit(solution)/shard_map/ppermute | solution.py:290
  146.1 5.9 %collective-permute-done.10 = bf16[128,768]{1,0:T(8,128)(2,1)S(1)} collective-permute-done((bf16[128,768]{1,0:T(8,128)(2,1)S(1)}, bf16[128,768]{1,0:T(8,128)(2,1)S(1)}, u32[]{:S(2)}, u32[]{:S(2)}) %collective-permute-start.10) | collective-permute-done | bytes 196640 | tf_op jit(solution)/shard_map/ppermute | solution.py:290
  152.7 6.0 %all-to-all-done.4 = bf16[4,128,256]{2,1,0:T(8,128)(2,1)S(1)} async-done(((bf16[4,128,256]{2,1,0:T(8,128)(2,1)}), bf16[4,128,256]{2,1,0:T(8,128)(2,1)S(1)}, u32[]{:S(2)}, u32[]{:S(2)}) %all-to-all-start.4) | async-done | bytes 262176 | tf_op jit(solution)/shard_map/all_to_all | solution.py:368
  (40 shorter events, 6.0 us)
Async XLA Ops:
  0.6 39.5 %copy-start = (bf16[128,768]{1,0:T(8,128)(2,1)S(1)}, bf16[128,768]{1,0:T(8,128)(2,1)}, u32[]{:S(2)}) copy-start(bf16[128,768]{1,0:T(8,128)(2,1)} %q_ref.1) | copy-start | bytes 589828
  1.4 17.3 %collective-permute-start.3 = (f32[8,128]{1,0:T(8,128)S(1)}, f32[8,128]{1,0:T(8,128)S(1)}, u32[]{:S(2)}, u32[]{:S(2)}) collective-permute-start(f32[8,128]{1,0:T(8,128)S(1)} %broadcast_select_fusion), channel_id=1, source_target_pairs={{0,1},{1,0},{2,3},{3,2},{4,5},{5,4},{6,7},{7,6},{8,9},{9,8},{10,11... | collective-permute-start | bytes 12296 | tf_op jit(solution)/shard_map/ppermute | solution.py:290
  18.8 4.3 %collective-permute-start.4 = (f32[8,128]{1,0:T(8,128)S(1)}, f32[8,128]{1,0:T(8,128)S(1)}, u32[]{:S(2)}, u32[]{:S(2)}) collective-permute-start(f32[8,128]{1,0:T(8,128)S(1)} %fusion.5), channel_id=1, source_target_pairs={{0,2},{2,0},{4,6},{6,4},{1,3},{3,1},{5,7},{7,5},{8,10},{10,8},{12,... | collective-permute-start | bytes 12296 | tf_op jit(solution)/shard_map/ppermute | solution.py:314
  23.2 5.8 %collective-permute-start.5 = (f32[8,128]{1,0:T(8,128)S(1)}, f32[8,128]{1,0:T(8,128)S(1)}, u32[]{:S(2)}, u32[]{:S(2)}) collective-permute-start(f32[8,128]{1,0:T(8,128)S(1)} %fusion.8), channel_id=1, source_target_pairs={{0,4},{2,6},{4,0},{6,2},{1,5},{3,7},{5,1},{7,3},{8,12},{10,14},{12... | collective-permute-start | bytes 12296 | tf_op jit(solution)/shard_map/ppermute | solution.py:314
  29.7 10.4 %copy-start.2 = (bf16[128,128]{1,0:T(8,128)(2,1)S(1)}, bf16[128,128]{1,0:T(8,128)(2,1)}, u32[]{:S(2)}) copy-start(bf16[128,128]{1,0:T(8,128)(2,1)} %k_ref.1) | copy-start | bytes 98308
  29.7 10.4 %copy-start.3 = (bf16[128,128]{1,0:T(8,128)(2,1)S(1)}, bf16[128,128]{1,0:T(8,128)(2,1)}, u32[]{:S(2)}) copy-start(bf16[128,128]{1,0:T(8,128)(2,1)} %v_ref.1) | copy-start | bytes 98308
  29.7 21.5 %all-to-all-start.2 = ((f32[16,8,128]{2,1,0:T(8,128)}), f32[16,8,128]{2,1,0:T(8,128)S(1)}, u32[]{:S(2)}, u32[]{:S(2)}) async-start(f32[16,8,128]{2,1,0:T(8,128)} %broadcast_in_dim.30), calls=%async_computation.2 | async-start | bytes 131072 | tf_op jit(solution)/shard_map/all_to_all | solution.py:323
  40.1 0.7 copy-start.4
  40.7 0.9 copy-start.1
  51.2 12.6 %all-to-all-start = ((bf16[4,128,256]{2,1,0:T(8,128)(2,1)}), bf16[4,128,256]{2,1,0:T(8,128)(2,1)S(1)}, u32[]{:S(2)}, u32[]{:S(2)}) async-start(bf16[4,128,256]{2,1,0:T(8,128)(2,1)} %get-tuple-element.10), calls=%async_computation | async-start | bytes 524288 | tf_op jit(solution)/shard_map/all_to_all | solution.py:316
  54.6 22.4 %collective-permute-start.1 = (bf16[144,1536]{1,0:T(8,128)(2,1)S(1)}, bf16[144,1536]{1,0:T(8,128)(2,1)S(1)}, u32[]{:S(2)}, u32[]{:S(2)}) collective-permute-start(bf16[144,1536]{1,0:T(8,128)(2,1)S(1)} %get-tuple-element.9.qg0_ref), channel_id=1, source_target_pairs={{0,64},{64,0},{1,65},{65,1},{2,66},{66,2},{3,67},{67,3},{4,68},{68... | collective-permute-start | bytes 1327112 | tf_op jit(solution)/shard_map/ppermute | solution.py:290
  65.0 15.8 %all-to-all-start.1 = ((bf16[4,4,128,256]{3,2,1,0:T(8,128)(2,1)}), bf16[4,4,128,256]{3,2,1,0:T(8,128)(2,1)S(1)}, u32[]{:S(2)}, u32[]{:S(2)}) async-start(bf16[4,4,128,256]{3,2,1,0:T(8,128)(2,1)} %broadcast_in_dim.26), calls=%async_computation.1 | async-start | bytes 2097152 | tf_op jit(solution)/shard_map/all_to_all | solution.py:320
  68.5 10.6 %collective-permute-start = (bf16[144,1536]{1,0:T(8,128)(2,1)S(1)}, bf16[144,1536]{1,0:T(8,128)(2,1)S(1)}, u32[]{:S(2)}, u32[]{:S(2)}) collective-permute-start(bf16[144,1536]{1,0:T(8,128)(2,1)S(1)} %get-tuple-element.9.qg0_ref), channel_id=1, source_target_pairs={{0,8},{8,0},{1,9},{9,1},{2,10},{10,2},{3,11},{11,3},{4,12},{12,4},... | collective-permute-start | bytes 1327112 | tf_op jit(solution)/shard_map/ppermute | solution.py:290
  77.0 3.7 %collective-permute-start.2 = (bf16[144,1536]{1,0:T(8,128)(2,1)S(1)}, bf16[144,1536]{1,0:T(8,128)(2,1)S(1)}, u32[]{:S(2)}, u32[]{:S(2)}) collective-permute-start(bf16[144,1536]{1,0:T(8,128)(2,1)S(1)} %collective-permute-done.1.qg2_ref), channel_id=1, source_target_pairs={{0,8},{8,0},{1,9},{9,1},{2,10},{10,2},{3,11},{11,3},{4,12},{12,4},... | collective-permute-start | bytes 1327112 | tf_op jit(solution)/shard_map/ppermute | solution.py:290
  80.7 8.1 %copy-start.5 = (bf16[144,1536]{1,0:T(8,128)(2,1)}, bf16[144,1536]{1,0:T(8,128)(2,1)S(1)}, u32[]{:S(2)}) copy-start(bf16[144,1536]{1,0:T(8,128)(2,1)S(1)} %collective-permute-done.2.qg3_ref) | copy-start | bytes 1327108
  80.7 0.7 copy-start.9
  80.7 0.7 copy-start.10
  88.8 16.6 %collective-permute-start.8 = (f32[16,1536]{1,0:T(8,128)S(1)}, f32[16,1536]{1,0:T(8,128)S(1)}, u32[]{:S(2)}, u32[]{:S(2)}) collective-permute-start(f32[16,1536]{1,0:T(8,128)S(1)} %shard_map.104.stat0_ref), channel_id=1, source_target_pairs={{0,72},{8,64},{64,8},{72,0},{1,73},{9,65},{65,9},{73,1},{2,74},{10... | collective-permute-start | bytes 294920 | tf_op jit(solution)/shard_map/ppermute | solution.py:294
  101.2 5.4 %collective-permute-start.7 = (f32[16,1536]{1,0:T(8,128)S(1)}, f32[16,1536]{1,0:T(8,128)S(1)}, u32[]{:S(2)}, u32[]{:S(2)}) collective-permute-start(f32[16,1536]{1,0:T(8,128)S(1)} %shard_map.104.stat0_ref), channel_id=1, source_target_pairs={{0,64},{64,0},{1,65},{65,1},{2,66},{66,2},{3,67},{67,3},{4,68},{68... | collective-permute-start | bytes 294920 | tf_op jit(solution)/shard_map/ppermute | solution.py:290
  103.1 3.4 %collective-permute-start.6 = (f32[16,1536]{1,0:T(8,128)S(1)}, f32[16,1536]{1,0:T(8,128)S(1)}, u32[]{:S(2)}, u32[]{:S(2)}) collective-permute-start(f32[16,1536]{1,0:T(8,128)S(1)} %shard_map.104.stat0_ref), channel_id=1, source_target_pairs={{0,8},{8,0},{1,9},{9,1},{2,10},{10,2},{3,11},{11,3},{4,12},{12,4},... | collective-permute-start | bytes 294920 | tf_op jit(solution)/shard_map/ppermute | solution.py:290
  106.5 1.0 copy-start.6
  119.5 0.7 copy-start.7
  120.2 3.7 %copy-start.8 = (bf16[2,128,768]{2,1,0:T(8,128)(2,1)S(1)}, bf16[2,128,768]{2,1,0:T(8,128)(2,1)}, u32[]{:S(2)}) copy-start(bf16[2,128,768]{2,1,0:T(8,128)(2,1)} %copy-done.7) | copy-start | bytes 1179652
  120.2 18.7 %all-to-all-start.3 = ((bf16[4,4,128,256]{3,2,1,0:T(8,128)(2,1)}), bf16[4,4,128,256]{3,2,1,0:T(8,128)(2,1)S(1)}, u32[]{:S(2)}, u32[]{:S(2)}) async-start(bf16[4,4,128,256]{3,2,1,0:T(8,128)(2,1)} %get-tuple-element.14), calls=%async_computation.3 | async-start | bytes 2097152 | tf_op jit(solution)/shard_map/all_to_all | solution.py:366
  123.9 19.4 %collective-permute-start.9 = (bf16[2,128,768]{2,1,0:T(8,128)(2,1)S(1)}, bf16[2,128,768]{2,1,0:T(8,128)(2,1)S(1)}, u32[]{:S(2)}, u32[]{:S(2)}) collective-permute-start(bf16[2,128,768]{2,1,0:T(8,128)(2,1)S(1)} %copy-done.8), channel_id=1, source_target_pairs={{0,8},{8,0},{1,9},{9,1},{2,10},{10,2},{3,11},{11,3},{4,12},{12,4},... | collective-permute-start | bytes 1179656 | tf_op jit(solution)/shard_map/ppermute | solution.py:290
  139.8 18.8 %all-to-all-start.4 = ((bf16[4,128,256]{2,1,0:T(8,128)(2,1)}), bf16[4,128,256]{2,1,0:T(8,128)(2,1)S(1)}, u32[]{:S(2)}, u32[]{:S(2)}) async-start(bf16[4,128,256]{2,1,0:T(8,128)(2,1)} %reduce_sum.24), calls=%async_computation.4 | async-start | bytes 524288 | tf_op jit(solution)/shard_map/all_to_all | solution.py:368
  143.4 8.6 %collective-permute-start.10 = (bf16[128,768]{1,0:T(8,128)(2,1)S(1)}, bf16[128,768]{1,0:T(8,128)(2,1)S(1)}, u32[]{:S(2)}, u32[]{:S(2)}) collective-permute-start(bf16[128,768]{1,0:T(8,128)(2,1)S(1)} %fusion.1), channel_id=1, source_target_pairs={{0,64},{64,0},{1,65},{65,1},{2,66},{66,2},{3,67},{67,3},{4,68},{68... | collective-permute-start | bytes 589832 | tf_op jit(solution)/shard_map/ppermute | solution.py:290

commit v2 on v1

v2 whole, which is shorter than its diff:
```python
import functools
import math

import jax
import jax.numpy as jnp
from jax import lax
from jax.experimental import pallas as pl
from jax.experimental.pallas import tpu as pltpu
from jax.sharding import Mesh, PartitionSpec as P

E = 128
GROUP = 6
HALF = 64
ROWS = 2 * HALF
TEAM = 4
LINE = 8
PARTS = LINE // 2
TILE = 4 * HALF
HEAD_COLS = TEAM * HALF
COLS = GROUP * HEAD_COLS
LAST = 2 * (LINE * TEAM * 2) - 1
NEG = -1e30
SCALE = 1.0 / math.sqrt(E)
SCALE2 = SCALE * math.log2(math.e)
LOG2E = math.log2(math.e)
F32 = jnp.float32
BF16 = jnp.bfloat16
I32 = jnp.int32
VMEM = 24 * 1024 * 1024


def dot(left, right, left_dim, right_dim):
    return lax.dot_general(
        left, right, (((left_dim,), (right_dim,)), ((), ())), preferred_element_type=F32
    )


def iota(shape, dim):
    return lax.broadcasted_iota(I32, shape, dim)


def call(kernel, outs, scratch=(), scalars=0, inputs=0, cost=None):
    spec = pl.BlockSpec(memory_space=pltpu.VMEM)
    return pl.pallas_call(
        kernel,
        out_shape=outs,
        in_specs=[pl.BlockSpec(memory_space=pltpu.SMEM)] * scalars + [spec] * inputs,
        out_specs=jax.tree.map(lambda _: spec, outs),
        scratch_shapes=list(scratch),
        compiler_params=pltpu.CompilerParams(vmem_limit_bytes=VMEM),
        cost_estimate=cost,
    )


def pack_kernel(
    where_ref, q_ref, g_ref, slot_ref, length_ref, return_ref, qg_ref, seg_ref
):
    line_place, core = where_ref[0], where_ref[2]
    width = GROUP * E
    qg_ref[0, :ROWS, :] = q_ref[...]
    qg_ref[1, :ROWS, :] = g_ref[...]
    slot = slot_ref[...]
    row = iota((16, ROWS), 0)
    coded = jnp.where(row == 0, slot >> 7, jnp.where(row == 1, slot & 127, 0))
    qg_ref[:, ROWS:, :] = jnp.zeros((2, 16, width), BF16)
    qg_ref[0, ROWS:, :ROWS] = coded.astype(F32).astype(BF16)

    lengths_row = length_ref[...].astype(F32)
    before = iota((E, E), 1) <= iota((E, E), 0)
    own = iota((E, E), 1) == iota((E, E), 0)
    ends = jnp.sum(jnp.where(before, lengths_row, 0.0), axis=1, keepdims=True)
    lengths = jnp.sum(jnp.where(own, lengths_row, 0.0), axis=1, keepdims=True)
    returns = jnp.sum(jnp.where(own, return_ref[...], 0.0), axis=1, keepdims=True)
    starts = ends - lengths
    column = iota((1, ROWS), 1)
    line = iota((8, ROWS), 0)
    block = jnp.zeros((8, ROWS), F32)
    for slot in range(TEAM):
        owner = 2 * (line_place * TEAM + slot) + core
        place_of = jnp.where(column < HALF, owner, LAST - owner)
        pos = (place_of * HALF + (column & 63)).astype(F32)
        inside = (pos >= starts) & (pos < ends)
        part = jnp.sum(jnp.where(inside, returns, 0.0), axis=0, keepdims=True)
        block = jnp.where(line == TEAM + slot, part, block)
    seg_ref[...] = block


def arrange(slots, refs, out_ref):
    for group in range(2):
        for head in range(GROUP):
            for ref, slot in zip(refs, slots):
                start = pl.multiple_of(head * HEAD_COLS + slot * HALF, HALF)
                out_ref[group, pl.ds(start, HALF), :] = ref[
                    group * HALF : (group + 1) * HALF, head * E : (head + 1) * E
                ]


def place(where_ref):
    z, ring, core = (where_ref[i] for i in range(3))
    return z, ring, core, [(ring - step) & 3 for step in range(TEAM)]


def causal_mask(group, z, ring, core):
    key_row = iota((TILE, 1), 0)
    piece = key_row >> 6
    key_owner = 2 * (((z & 6) + (piece & 1)) * TEAM + ring) + (core ^ (piece >> 1))
    column = iota((1, HEAD_COLS), 1)
    query_owner = 2 * (z * TEAM + (column >> 6)) + core
    if group == 1:
        key_owner, query_owner = LAST - key_owner, LAST - query_owner
    key_pos = key_owner * HALF + (key_row & 63)
    query_pos = query_owner * HALF + (column & 63)
    return key_pos <= query_pos


def free_visit(index, edge):
    wide = index < PARTS
    rest = index - PARTS
    early = rest < edge
    group = jnp.where(wide, 1, jnp.where(early, 0, 1))
    half = jnp.where(wide, 0, jnp.where(early, 0, 1))
    part = jnp.where(wide, index, jnp.where(early, rest, rest + 1))
    return group, half, part


def key_value_tile(kv_refs, half, part):
    rows = pl.ds(pl.multiple_of(half * HALF, HALF), HALF)
    pieces = [ref[pl.ds(part * 2, 2), rows, :].reshape(2 * HALF, 2 * E) for ref in kv_refs]
    return jnp.concatenate(pieces, axis=0)


def forward_kernel(
    where_ref, qg0_ref, qg1_ref, q2_ref, g2_ref, qg3_ref, kv0_ref, kv1_ref,
    stat_ref, qs_ref, gs_ref, top_ref, sum_ref, term_ref,
):
    z, ring, core, slots = place(where_ref)
    arrange(slots, (qg0_ref.at[0], qg1_ref.at[0], q2_ref, qg3_ref.at[0]), qs_ref)
    arrange(slots, (qg0_ref.at[1], qg1_ref.at[1], g2_ref, qg3_ref.at[1]), gs_ref)
    kv_refs = (kv0_ref, kv1_ref)
    edge = z >> 1
    top_ref[...] = jnp.full(top_ref.shape, NEG, F32)
    sum_ref[...] = jnp.zeros(sum_ref.shape, F32)
    term_ref[...] = jnp.zeros(term_ref.shape, F32)

    def visit(group, half, part, mask):
        key_value = key_value_tile(kv_refs, half, part)
        key, value = key_value[:, :E], key_value[:, E:]
        for head in range(GROUP):
            cols = slice(head * HEAD_COLS, (head + 1) * HEAD_COLS)
            scores = dot(key, qs_ref[group, cols, :], 1, 1) * SCALE2
            dots = dot(value, gs_ref[group, cols, :], 1, 1)
            if mask is not None:
                scores = jnp.where(mask, scores, NEG)
            scores = scores.reshape(TILE // 8, 8, HEAD_COLS)
            dots = dots.reshape(TILE // 8, 8, HEAD_COLS)
            old = top_ref[group, :, cols]
            top = jnp.maximum(old, jnp.max(scores, axis=0))
            factor = jnp.exp2(old - top)
            prob = jnp.exp2(scores - top[None])
            top_ref[group, :, cols] = top
            sum_ref[group, :, cols] = factor * sum_ref[group, :, cols] + jnp.sum(prob, axis=0)
            term_ref[group, :, cols] = factor * term_ref[group, :, cols] + jnp.sum(
                prob * dots, axis=0
            )

    @pl.loop(0, 2 * PARTS - 1)
    def _(index):
        visit(*free_visit(index, edge), None)

    for group in range(2):
        visit(group, group, edge, causal_mask(group, z, ring, core))

    stat_ref[...] = jnp.zeros(stat_ref.shape, F32)
    for group in range(2):
        top = top_ref[group]
        best = jnp.max(top, axis=0, keepdims=True)
        factor = jnp.exp2(top - best)
        stat_ref[3 * group : 3 * group + 1, :] = best
        stat_ref[3 * group + 1 : 3 * group + 2, :] = jnp.sum(
            factor * sum_ref[group], axis=0, keepdims=True
        )
        stat_ref[3 * group + 2 : 3 * group + 3, :] = jnp.sum(
            factor * term_ref[group], axis=0, keepdims=True
        )


def lookup_kernel(
    where_ref, qg0_ref, qg1_ref, q2_ref, g2_ref, qg3_ref, stat_ref, table_ref, seg_ref, out_ref
):
    z, ring, core, slots = place(where_ref)
    refs = (qg0_ref.at[0], qg1_ref.at[0], q2_ref, qg3_ref.at[0])
    table = table_ref[:, 0, :]
    high = table.astype(BF16)
    rest = table - high.astype(F32)
    middle = rest.astype(BF16)
    low = (rest - middle.astype(F32)).astype(BF16)
    lane = iota((E, ROWS), 0)
    device = iota((2 * LINE, ROWS), 0)
    line = iota((8, ROWS), 0)
    block = seg_ref[...]
    for ref, slot in zip(refs, slots):
        code = ref[ROWS : ROWS + 16, :ROWS].astype(F32)
        owner = code[0:1].astype(I32)
        entry = code[1:2].astype(I32)
        pick = (lane == entry).astype(F32).astype(BF16)
        picked = dot(high, pick, 1, 0) + dot(middle, pick, 1, 0) + dot(low, pick, 1, 0)
        line_place = (owner >> 3) ^ jnp.where(((entry >> 4) & 1) == where_ref[3], 0, 4)
        row = jnp.where(((owner >> 1) & 3) == ring, line_place * 2 + (owner & 1), -1)
        part = jnp.sum(jnp.where(device == row, picked, 0.0), axis=0, keepdims=True)
        block = jnp.where(line == slot, part, block)
    for copy in range(TEAM):
        out_ref[copy] = stat_ref[...]
        for row in range(8):
            out_ref[copy, 6:7, row * ROWS : (row + 1) * ROWS] = block[row : row + 1]


def row_weights(stats):
    logw = [
        stats[0][6:7, (TEAM + s) * ROWS : (TEAM + s + 1) * ROWS]
        - sum(st[6:7, s * ROWS : (s + 1) * ROWS] for st in stats)
        for s in range(TEAM)
    ]
    low_lane = iota((1, ROWS), 1) < HALF
    groups = []
    for group in range(2):
        pieces = []
        for first in (0, 2):
            a, b = logw[first], logw[first + 1]
            if group == 0:
                b = pltpu.roll(jnp.broadcast_to(b, (8, ROWS)), HALF, 1)[0:1]
            else:
                a = pltpu.roll(jnp.broadcast_to(a, (8, ROWS)), HALF, 1)[0:1]
            pieces.append(jnp.where(low_lane, a, b))
        groups.append(jnp.concatenate(pieces, axis=1))
    return groups


def merge_stats(stat_ref, shift_ref, term_ref):
    stats = [stat_ref.at[s] for s in range(TEAM)]
    weights = row_weights(stats)
    for group in range(2):
        tops = [st[3 * group : 3 * group + 1, :] for st in stats]
        best = functools.reduce(jnp.maximum, tops)
        factors = [jnp.exp2(top - best) for top in tops]
        total = sum(f * st[3 * group + 1 : 3 * group + 2, :] for f, st in zip(factors, stats))
        term = sum(f * st[3 * group + 2 : 3 * group + 3, :] for f, st in zip(factors, stats))
        shift = best + jnp.log2(total)
        term_ref[group] = term / total
        for head in range(GROUP):
            cols = slice(head * HEAD_COLS, (head + 1) * HEAD_COLS)
            shift_ref[group, :, cols] = shift[:, cols] - weights[group] * LOG2E


def backward_kernel(
    where_ref, qg0_ref, qg1_ref, q2_ref, g2_ref, qg3_ref, kv0_ref, kv1_ref, stat_ref,
    dkv0_ref, dkv1_ref, dq0_ref, dq1_ref, dq2_ref, dq3_ref,
    qs_ref, gs_ref, dqt_ref, acc_ref, shift_ref, term_ref, prob_ref, slope_ref, turn_ref,
):
    z, ring, core, slots = place(where_ref)
    kv_refs = (kv0_ref, kv1_ref)
    arrange(slots, (qg0_ref.at[0], qg1_ref.at[0], q2_ref, qg3_ref.at[0]), qs_ref)
    arrange(slots, (qg0_ref.at[1], qg1_ref.at[1], g2_ref, qg3_ref.at[1]), gs_ref)
    merge_stats(stat_ref, shift_ref, term_ref)
    acc_ref[...] = jnp.zeros(acc_ref.shape, F32)
    dqt_ref[...] = jnp.zeros(dqt_ref.shape, F32)
    edge, pair = z >> 1, z & 1

    def visit(group, half, part, mask):
        key_value = key_value_tile(kv_refs, half, part)
        key, value = key_value[:, :E], key_value[:, E:]
        for head in range(GROUP):
            cols = slice(head * HEAD_COLS, (head + 1) * HEAD_COLS)
            scores = dot(key, qs_ref[group, cols, :], 1, 1) * SCALE2
            dots = dot(value, gs_ref[group, cols, :], 1, 1)
            if mask is not None:
                scores = jnp.where(mask, scores, NEG)
            prob = jnp.exp2(scores - shift_ref[group, :, cols])
            prob_ref[:, cols] = prob.astype(BF16)
            slope_ref[:, cols] = (prob * (dots - term_ref[group, :, cols])).astype(BF16)
        slope = slope_ref[...]
        acc_ref[half, part, :, :E] += dot(slope, qs_ref[group], 1, 0)
        acc_ref[half, part, :, E:] += dot(prob_ref[...], gs_ref[group], 1, 0)
        dqt_ref[group] += dot(key, slope, 0, 0)

    @pl.loop(0, 2 * PARTS - 1)
    def _(index):
        visit(*free_visit(index, edge), None)

    for group in range(2):
        visit(group, group, edge, causal_mask(group, z, ring, core))

    scales = jnp.where(iota((1, 2 * E), 1) < E, SCALE, 1.0)
    for half in range(2):
        for part in range(PARTS):
            tile = (acc_ref[half, part] * scales).reshape(2, 2, HALF, 2 * E)
            rows = slice(half * HALF, (half + 1) * HALF)
            for piece in range(2):
                dkv0_ref[piece ^ pair, part, rows, :] = tile[0, piece]
                dkv1_ref[piece ^ pair, part, rows, :] = tile[1, piece].astype(BF16)
    targets = (dq0_ref, dq1_ref, dq2_ref, dq3_ref)
    for group in range(2):
        for head in range(GROUP):
            cols = slice(head * HEAD_COLS, (head + 1) * HEAD_COLS)
            turn_ref[...] = dqt_ref[group, :, cols].T * SCALE
            for ref, slot in zip(targets, slots):
                start = pl.multiple_of(slot * HALF, HALF)
                ref[group * HALF : (group + 1) * HALF, head * E : (head + 1) * E] = turn_ref[
                    pl.ds(start, HALF), :
                ].astype(ref.dtype)


def shape(dims, dtype):
    return jax.ShapeDtypeStruct(dims, dtype)


def swapped(x, axis):
    return lax.ppermute(x, axis, [(0, 1), (1, 0)])


def far_swapped(x):
    pairs = [(i, i ^ 5) for i in range(LINE)]
    return lax.ppermute(x, ("quad", "far"), pairs)


def from_ring(x, step):
    return lax.ppermute(x, "ring", [(i, (i + step) % TEAM) for i in range(TEAM)])


def per_device(queries, keys, values, cotangent, seg_lengths, seg_return, owner_slot, ref_term):
    head = lax.axis_index(("far_col", "near_col", "far"))
    place_names = (("quad", "pair"), "ring", "core", "far")
    where = jnp.stack([lax.axis_index(name) for name in place_names]).astype(I32)
    width = GROUP * E

    kv_own = jnp.broadcast_to(
        jnp.concatenate([keys, values], axis=1)[None], (LINE, ROWS, 2 * E)
    )
    qg, seg = call(
        pack_kernel,
        (shape((2, ROWS + 16, width), BF16), shape((8, E), F32)),
        scalars=1,
        inputs=5,
    )(
        where, queries, cotangent, owner_slot.reshape(1, ROWS),
        seg_lengths.reshape(1, E), seg_return.reshape(1, E),
    )
    lane = iota((8, E), 1)
    terms = jnp.where((lane >> 4) == head, jnp.tile(ref_term, 8)[None], 0.0)
    terms = terms + far_swapped(terms)
    kv_own, terms, qg = lax.optimization_barrier((kv_own, terms, qg))
    kv0 = lax.all_to_all(kv_own, ("quad", "pair"), 0, 0, tiled=True)
    qg1, qg3 = from_ring(qg, 1), from_ring(qg, 3)
    terms = terms + swapped(terms, "near_col")
    qg1, qg3, terms = lax.optimization_barrier((qg1, qg3, terms))
    terms = terms + swapped(terms, "far_col")
    team = [qg, qg1, from_ring(qg1[0], 1), from_ring(qg3[1], 3), qg3]
    kv0, terms, *team = lax.optimization_barrier((kv0, terms, *team))
    kv1 = swapped(kv0, "core")
    table = lax.all_to_all(
        jnp.broadcast_to(terms[None], (2 * LINE, 8, E)), ("quad", "pair", "core"), 0, 0, tiled=True
    )
    pairs = 9 * TILE * COLS
    kv_scratch = [pltpu.VMEM((2, COLS, E), BF16), pltpu.VMEM((2, COLS, E), BF16)]
    stat = call(
        forward_kernel,
        shape((8, COLS), F32),
        kv_scratch + [pltpu.VMEM((2, 8, COLS), F32)] * 3,
        scalars=1,
        inputs=7,
        cost=pl.CostEstimate(flops=4 * E * pairs, bytes_accessed=4 << 20, transcendentals=pairs),
    )(where, *team, kv0, kv1)
    stat = call(lookup_kernel, shape((TEAM, 8, COLS), F32), scalars=1, inputs=8)(
        where, *team, stat, table, seg
    )
    stats = lax.all_to_all(stat, "ring", 0, 0, tiled=True)
    core_grad = (2, LINE // 2, ROWS, 2 * E)
    query_grad = shape((ROWS, width), BF16)
    grad0, grad1, dq0, *dqs = call(
        backward_kernel,
        (
            shape(core_grad, F32), shape(core_grad, BF16), shape((ROWS, width), F32),
            query_grad, query_grad, query_grad,
        ),
        kv_scratch
        + [
            pltpu.VMEM((2, E, COLS), F32),
            pltpu.VMEM((2, PARTS, TILE, 2 * E), F32),
            pltpu.VMEM((2, 1, COLS), F32),
            pltpu.VMEM((2, 1, COLS), F32),
            pltpu.VMEM((TILE, COLS), BF16),
            pltpu.VMEM((TILE, COLS), BF16),
            pltpu.VMEM((HEAD_COLS, E), F32),
        ],
        scalars=1,
        inputs=8,
        cost=pl.CostEstimate(flops=10 * E * pairs, bytes_accessed=5 << 20, transcendentals=pairs),
    )(where, *team, kv0, kv1, stats)

    own = grad0 + swapped(grad1, "core").astype(F32)
    parts = (own[0] + swapped(own[1].astype(BF16), "pair").astype(F32)).astype(BF16)
    parts = lax.all_to_all(parts, "quad", 0, 0, tiled=True)
    kv_grad = jnp.sum(parts.astype(F32), axis=0).astype(BF16)

    for step, part in enumerate(dqs, 1):
        dq0 = dq0 + from_ring(part, TEAM - step).astype(F32)
    return dq0.astype(BF16), kv_grad[:, :E], kv_grad[:, E:]


def solution(mesh):
    fine = Mesh(
        mesh.devices.reshape(LINE // 2, 2, TEAM, 2, 2, 2, 2),
        ("quad", "pair", "ring", "core", "far_col", "near_col", "far"),
    )
    ctx = ("quad", "pair", "ring", "core")
    head = ("far_col", "near_col", "far")
    return jax.shard_map(
        per_device,
        mesh=fine,
        in_specs=(
            P(ctx, head), P(ctx, head), P(ctx, head), P(ctx, head),
            P(), P(), P(ctx), P(ctx + head),
        ),
        out_specs=(P(ctx, head), P(ctx, head), P(ctx, head)),
        check_vma=False,
    )
```

time: 161 us -> 140 us (0.87)
  waiting for transfers between devices: 45.5 us -> 29.9 us
  starting transfers between devices: 83.7 us -> 73.4 us
  blocking collectives: 0 us -> 7.54 us
  local copies, waits for them, and re-layouts: 7.1 us -> 4.59 us
    all_to_all x4 -> x2, waiting for transfers between devices: 27.5 us -> 2.92 us  [the longest x1 2.92 us: per_device(): lax.all_to_all(jnp.broadcast_to(terms[None], (2 * LINE, 8, E)), ('quad',...]
    ppermute x8 -> x5, starting transfers between devices: 39.2 us -> 19.6 us  [swapped(): return lax.ppermute(x, axis, [(0, 1), (1, 0)])]
    ppermute x3 -> x8, starting transfers between devices: 20.1 us -> 32.9 us  [the longest x7 19.6 us: from_ring(): lax.ppermute(x, 'ring', [(i, (i + step) % TEAM) for i in range(TEAM)])]
    ppermute x3 -> x8, waiting for transfers between devices: 2.42 us -> 15.1 us  [the longest x7 15.1 us: from_ring(): lax.ppermute(x, 'ring', [(i, (i + step) % TEAM) for i in range(TEAM)])]
    all_to_all x0 -> x1, blocking collectives: none -> 7.54 us  [per_device(): stats = lax.all_to_all(stat, 'ring', 0, 0, tiled=True)]
    all_to_all x1, waiting for transfers between devices: 5.96 us -> 0.01 us  [per_device(): parts = lax.all_to_all(parts, 'quad', 0, 0, tiled=True)]
    all_to_all x4 -> x2, starting transfers between devices: 20.9 us -> 15.7 us  [the longest x1 9.75 us: per_device(): lax.all_to_all(jnp.broadcast_to(terms[None], (2 * LINE, 8, E)), ('quad',...]
    unnamed x22 -> x18, local copies, waits for them, and re-layouts: 4.03 us -> 1.63 us
  transfers between devices with their start and end apart: 16 -> 16, of which waited for: 10 -> 9; matrix products, arithmetic and copies ran while one was open for 2% -> 2% of each run, Pallas kernels for 0% -> 6%
where the time goes in v2:
time: 140 us; the launch traced here: 139 us
  starting transfers between devices  73.4 us (52%)
  waiting for transfers between devices  29.9 us (21%)
  Pallas kernels  20.1 us (14%)
  blocking collectives  7.54 us (5%)
  local copies, waits for them, and re-layouts  4.59 us (3%)
  other arithmetic  2.6 us (2%)
    ppermute x7, starting transfers between devices, from_ring(): lax.ppermute(x, 'ring', [(i, (i + step) % TEAM) for i in range(TEAM)])  19.6 us
    ppermute x5, starting transfers between devices, swapped(): return lax.ppermute(x, axis, [(0, 1), (1, 0)])  19.6 us
    ppermute x7, waiting for transfers between devices, from_ring(): lax.ppermute(x, 'ring', [(i, (i + step) % TEAM) for i in range(TEAM)])  15.1 us
    ppermute x1, starting transfers between devices, far_swapped(): return lax.ppermute(x, ('quad', 'far'), pairs)  13.3 us
    ppermute x5, waiting for transfers between devices, swapped(): return lax.ppermute(x, axis, [(0, 1), (1, 0)])  11.9 us
    pallas_call x1, Pallas kernels, per_device(): call(backward_kernel, (shape(core_grad, F32), shape(core_grad, BF16), sha...  11.5 us
    all_to_all x1, starting transfers between devices, per_device(): lax.all_to_all(jnp.broadcast_to(terms[None], (2 * LINE, 8, E)), ('quad',...  9.75 us
    all_to_all x1, blocking collectives, per_device(): stats = lax.all_to_all(stat, 'ring', 0, 0, tiled=True)  7.54 us
  transfers between devices with their start and end apart: 16, of which 9 were waited for; matrix products, arithmetic and copies ran while one was open for 2% of the time, Pallas kernels for 6%

profile of v2, /device:TPU:1, one launch (start us, length us, event | category | flops | bytes accessed | tf_op | source)
XLA Modules:
  0.0 139.1 jit_solution(6486903220566265851)
XLA Ops:
  1.5 13.3 %collective-permute-start = (f32[8,128]{1,0:T(8,128)S(1)}, f32[8,128]{1,0:T(8,128)S(1)}, u32[]{:S(2)}, u32[]{:S(2)}) collective-permute-start(f32[8,128]{1,0:T(8,128)S(1)} %broadcast_select_fusion), channel_id=1, source_target_pairs={{0,257},{1,256},{128,385},{129,384},{256,1},{257,0},{384,129},{385... | collective-permute-start | bytes 12296 | tf_op jit(solution)/shard_map/ppermute | solution.py:322
  14.8 0.8 pad_maximum_fusion
  16.3 0.9 copy-done.1
  17.9 0.8 broadcast_in_dim.26
  18.8 5.9 %all-to-all-start = ((bf16[8,128,256]{2,1,0:T(8,128)(2,1)}), bf16[8,128,256]{2,1,0:T(8,128)(2,1)S(1)}, u32[]{:S(2)}, u32[]{:S(2)}) async-start(bf16[8,128,256]{2,1,0:T(8,128)(2,1)} %broadcast_in_dim.26), calls=%async_computation | async-start | bytes 1048576 | tf_op jit(solution)/shard_map/all_to_all | solution.py:351
  24.7 4.6 %collective-permute-start.2 = (bf16[2,144,768]{2,1,0:T(8,128)(2,1)S(1)}, bf16[2,144,768]{2,1,0:T(8,128)(2,1)S(1)}, u32[]{:S(2)}, u32[]{:S(2)}) collective-permute-start(bf16[2,144,768]{2,1,0:T(8,128)(2,1)S(1)} %get-tuple-element.31.qg0_ref), channel_id=1, source_target_pairs={{0,48},{16,0},{32,16},{48,32},{1,49},{17,1},{33,17},{49,33},{2,50}... | collective-permute-start | bytes 1327112 | tf_op jit(solution)/shard_map/ppermute | solution.py:326
  29.3 1.9 %collective-permute-start.1 = (bf16[2,144,768]{2,1,0:T(8,128)(2,1)S(1)}, bf16[2,144,768]{2,1,0:T(8,128)(2,1)S(1)}, u32[]{:S(2)}, u32[]{:S(2)}) collective-permute-start(bf16[2,144,768]{2,1,0:T(8,128)(2,1)S(1)} %get-tuple-element.31.qg0_ref), channel_id=1, source_target_pairs={{0,16},{16,32},{32,48},{48,0},{1,17},{17,33},{33,49},{49,1},{2,18}... | collective-permute-start | bytes 1327112 | tf_op jit(solution)/shard_map/ppermute | solution.py:326
  31.3 3.1 %collective-permute-start.3 = (f32[8,128]{1,0:T(8,128)S(1)}, f32[8,128]{1,0:T(8,128)S(1)}, u32[]{:S(2)}, u32[]{:S(2)}) collective-permute-start(f32[8,128]{1,0:T(8,128)S(1)} %fusion.3), channel_id=1, source_target_pairs={{0,2},{2,0},{1,3},{3,1},{4,6},{6,4},{5,7},{7,5},{8,10},{10,8},{9,1... | collective-permute-start | bytes 12296 | tf_op jit(solution)/shard_map/ppermute | solution.py:317
  34.4 1.5 %collective-permute-done.3 = f32[8,128]{1,0:T(8,128)S(1)} collective-permute-done((f32[8,128]{1,0:T(8,128)S(1)}, f32[8,128]{1,0:T(8,128)S(1)}, u32[]{:S(2)}, u32[]{:S(2)}) %collective-permute-start.3) | collective-permute-done | bytes 4128 | tf_op jit(solution)/shard_map/ppermute | solution.py:317
  35.9 1.6 %collective-permute-done.2.qg3_ref = bf16[2,144,768]{2,1,0:T(8,128)(2,1)S(1)} collective-permute-done((bf16[2,144,768]{2,1,0:T(8,128)(2,1)S(1)}, bf16[2,144,768]{2,1,0:T(8,128)(2,1)S(1)}, u32[]{:S(2)}, u32[]{:S(2)}) %collective-permute-start.2) | collective-permute-done | bytes 442400 | tf_op jit(solution)/shard_map/ppermute | solution.py:326
  37.5 5.0 %collective-permute-done.1.qg1_ref = bf16[2,144,768]{2,1,0:T(8,128)(2,1)S(1)} collective-permute-done((bf16[2,144,768]{2,1,0:T(8,128)(2,1)S(1)}, bf16[2,144,768]{2,1,0:T(8,128)(2,1)S(1)}, u32[]{:S(2)}, u32[]{:S(2)}) %collective-permute-start.1) | collective-permute-done | bytes 442400 | tf_op jit(solution)/shard_map/ppermute | solution.py:326
  42.6 1.9 %collective-permute-start.6 = (bf16[144,768]{1,0:T(8,128)(2,1)S(1)}, bf16[144,768]{1,0:T(8,128)(2,1)S(1)}, u32[]{:S(2)}, u32[]{:S(2)}) collective-permute-start(bf16[144,768]{1,0:T(8,128)(2,1)S(1)} %slice_bitcast_fusion.1), channel_id=1, source_target_pairs={{0,48},{16,0},{32,16},{48,32},{1,49},{17,1},{33,17},{49,33},{2,50}... | collective-permute-start | bytes 663560 | tf_op jit(solution)/shard_map/ppermute | solution.py:326
  44.6 3.4 %collective-permute-start.5 = (bf16[144,768]{1,0:T(8,128)(2,1)S(1)}, bf16[144,768]{1,0:T(8,128)(2,1)S(1)}, u32[]{:S(2)}, u32[]{:S(2)}) collective-permute-start(bf16[144,768]{1,0:T(8,128)(2,1)S(1)} %slice_bitcast_fusion.2), channel_id=1, source_target_pairs={{0,16},{16,32},{32,48},{48,0},{1,17},{17,33},{33,49},{49,1},{2,18}... | collective-permute-start | bytes 663560 | tf_op jit(solution)/shard_map/ppermute | solution.py:326
  47.9 4.7 %collective-permute-start.4 = (f32[8,128]{1,0:T(8,128)S(1)}, f32[8,128]{1,0:T(8,128)S(1)}, u32[]{:S(2)}, u32[]{:S(2)}) collective-permute-start(f32[8,128]{1,0:T(8,128)S(1)} %add.37), channel_id=1, source_target_pairs={{0,4},{4,0},{1,5},{5,1},{2,6},{6,2},{3,7},{7,3},{8,12},{12,8},{9,1... | collective-permute-start | bytes 12296 | tf_op jit(solution)/shard_map/ppermute | solution.py:317
  52.6 1.4 %collective-permute-done.4 = f32[8,128]{1,0:T(8,128)S(1)} collective-permute-done((f32[8,128]{1,0:T(8,128)S(1)}, f32[8,128]{1,0:T(8,128)S(1)}, u32[]{:S(2)}, u32[]{:S(2)}) %collective-permute-start.4) | collective-permute-done | bytes 4128 | tf_op jit(solution)/shard_map/ppermute | solution.py:317
  54.0 5.9 %collective-permute-start.7 = (bf16[8,128,256]{2,1,0:T(8,128)(2,1)S(1)}, bf16[8,128,256]{2,1,0:T(8,128)(2,1)S(1)}, u32[]{:S(2)}, u32[]{:S(2)}) collective-permute-start(bf16[8,128,256]{2,1,0:T(8,128)(2,1)S(1)} %all-to-all-done.kv0_ref), channel_id=1, source_target_pairs={{0,8},{8,0},{1,9},{9,1},{2,10},{10,2},{3,11},{11,3},{4,12},{12,4},... | collective-permute-start | bytes 1572872 | tf_op jit(solution)/shard_map/ppermute | solution.py:317
  60.5 9.8 %all-to-all-start.1 = ((f32[16,8,128]{2,1,0:T(8,128)}), f32[16,8,128]{2,1,0:T(8,128)S(1)}, u32[]{:S(2)}, u32[]{:S(2)}) async-start(f32[16,8,128]{2,1,0:T(8,128)} %broadcast_in_dim.30), calls=%async_computation.1 | async-start | bytes 131072 | tf_op jit(solution)/shard_map/all_to_all | solution.py:359
  70.3 7.1 %shard_map.104.stat_ref = f32[8,1536]{1,0:T(8,128)S(1)} custom-call(s32[4]{0:T(128)S(1)} %pad_add_fusion.where_ref, bf16[2,144,768]{2,1,0:T(8,128)(2,1)S(1)} %get-tuple-element.31.qg0_ref, bf16[2,144,768]{2,1,0:T(8,128)(2,1)S(1)} %collective-permute-done.1.qg1_ref, bf16[144,768]{1,0:T(8,128)(2,1)S(1)} %collective-permute-done.5.q2_ref, ...), custom_call_target="tpu_custom_call" | custom-call | flops 1811939328 | bytes 4194304 | tf_op jit(solution)/shard_map/pallas_call | solution.py:364
  77.4 2.9 %all-to-all-done.1.table_ref = f32[16,8,128]{2,1,0:T(8,128)S(1)} async-done(((f32[16,8,128]{2,1,0:T(8,128)}), f32[16,8,128]{2,1,0:T(8,128)S(1)}, u32[]{:S(2)}, u32[]{:S(2)}) %all-to-all-start.1) | async-done | bytes 65568 | tf_op jit(solution)/shard_map/all_to_all | solution.py:359
  80.3 0.8 shard_map.105
  81.1 7.5 %all_to_all.20.stat_ref = f32[4,8,1536]{2,1,0:T(8,128)S(1)} all-to-all(f32[4,8,1536]{2,1,0:T(8,128)S(1)} %shard_map.105), channel_id=1, replica_groups=mesh['quad'=4,'pair'=2,'ring'=4,'core'=2,'far_col'=2,'near_col'=2,'far'=..., dimensions={0} | all-to-all | bytes 393216 | tf_op jit(solution)/shard_map/all_to_all | solution.py:375
  88.7 11.5 %shard_map.106 = (f32[2,4,128,256]{3,2,1,0:T(8,128)S(1)}, bf16[2,4,128,256]{3,2,1,0:T(8,128)(2,1)S(1)}, f32[128,768]{1,0:T(8,128)S(1)}, bf16[128,768]{1,0:T(8,12...) custom-call(s32[4]{0:T(128)S(1)} %pad_add_fusion.where_ref, ...), custom_call_target="tpu_custom_call" | custom-call | flops 4529848320 | bytes 5242880 | tf_op jit(solution)/shard_map/pallas_call | solution.py:378
  100.2 4.1 %collective-permute-start.11 = (bf16[2,4,128,256]{3,2,1,0:T(8,128)(2,1)S(1)}, bf16[2,4,128,256]{3,2,1,0:T(8,128)(2,1)S(1)}, u32[]{:S(2)}, u32[]{:S(2)}) collective-permute-start(bf16[2,4,128,256]{3,2,1,0:T(8,128)(2,1)S(1)} %get-tuple-element.44), channel_id=1, source_target_pairs={{0,8},{8,0},{1,9},{9,1},{2,10},{10,2},{3,11},{11,3},{4,12},{12,4},... | collective-permute-start | bytes 1572872 | tf_op jit(solution)/shard_map/ppermute | solution.py:317
  104.3 1.5 %collective-permute-done.11 = bf16[2,4,128,256]{3,2,1,0:T(8,128)(2,1)S(1)} collective-permute-done((bf16[2,4,128,256]{3,2,1,0:T(8,128)(2,1)S(1)}, bf16[2,4,128,256]{3,2,1,0:T(8,128)(2,1)S(1)}, u32[]{:S(2)}, u32[]{:S(2)}) %collective-permute-start.11) | collective-permute-done | bytes 524320 | tf_op jit(solution)/shard_map/ppermute | solution.py:317
  106.0 1.9 %collective-permute-start.12 = (bf16[4,128,256]{2,1,0:T(8,128)(2,1)S(1)}, bf16[4,128,256]{2,1,0:T(8,128)(2,1)S(1)}, u32[]{:S(2)}, u32[]{:S(2)}) collective-permute-start(bf16[4,128,256]{2,1,0:T(8,128)(2,1)S(1)} %fusion.2), channel_id=1, source_target_pairs={{0,64},{64,0},{1,65},{65,1},{2,66},{66,2},{3,67},{67,3},{4,68},{68... | collective-permute-start | bytes 786440 | tf_op jit(solution)/shard_map/ppermute | solution.py:317
  107.9 7.5 %collective-permute-done.12 = bf16[4,128,256]{2,1,0:T(8,128)(2,1)S(1)} collective-permute-done((bf16[4,128,256]{2,1,0:T(8,128)(2,1)S(1)}, bf16[4,128,256]{2,1,0:T(8,128)(2,1)S(1)}, u32[]{:S(2)}, u32[]{:S(2)}) %collective-permute-start.12) | collective-permute-done | bytes 262176 | tf_op jit(solution)/shard_map/ppermute | solution.py:317
  116.2 5.2 %all-to-all-start.3 = ((bf16[4,128,256]{2,1,0:T(8,128)(2,1)}), bf16[4,128,256]{2,1,0:T(8,128)(2,1)S(1)}, u32[]{:S(2)}, u32[]{:S(2)}) async-start(bf16[4,128,256]{2,1,0:T(8,128)(2,1)} %fusion.1), calls=%async_computation.3 | async-start | bytes 524288 | tf_op jit(solution)/shard_map/all_to_all | solution.py:401
  121.4 2.8 %collective-permute-start.8 = (bf16[128,768]{1,0:T(8,128)(2,1)S(1)}, bf16[128,768]{1,0:T(8,128)(2,1)S(1)}, u32[]{:S(2)}, u32[]{:S(2)}) collective-permute-start(bf16[128,768]{1,0:T(8,128)(2,1)S(1)} %copy-done.8), channel_id=1, source_target_pairs={{0,48},{16,0},{32,16},{48,32},{1,49},{17,1},{33,17},{49,33},{2,50}... | collective-permute-start | bytes 589832 | tf_op jit(solution)/shard_map/ppermute | solution.py:326
  124.2 3.1 %collective-permute-start.9 = (bf16[128,768]{1,0:T(8,128)(2,1)S(1)}, bf16[128,768]{1,0:T(8,128)(2,1)S(1)}, u32[]{:S(2)}, u32[]{:S(2)}) collective-permute-start(bf16[128,768]{1,0:T(8,128)(2,1)S(1)} %copy-done.6), channel_id=1, source_target_pairs={{0,32},{16,48},{32,0},{48,16},{1,33},{17,49},{33,1},{49,17},{2,34}... | collective-permute-start | bytes 589832 | tf_op jit(solution)/shard_map/ppermute | solution.py:326
  127.3 1.9 %collective-permute-start.10 = (bf16[128,768]{1,0:T(8,128)(2,1)S(1)}, bf16[128,768]{1,0:T(8,128)(2,1)S(1)}, u32[]{:S(2)}, u32[]{:S(2)}) collective-permute-start(bf16[128,768]{1,0:T(8,128)(2,1)S(1)} %get-tuple-element.42), channel_id=1, source_target_pairs={{0,16},{16,32},{32,48},{48,0},{1,17},{17,33},{33,49},{49,1},{2,18}... | collective-permute-start | bytes 589832 | tf_op jit(solution)/shard_map/ppermute | solution.py:326
  129.2 2.9 %collective-permute-done.9 = bf16[128,768]{1,0:T(8,128)(2,1)S(1)} collective-permute-done((bf16[128,768]{1,0:T(8,128)(2,1)S(1)}, bf16[128,768]{1,0:T(8,128)(2,1)S(1)}, u32[]{:S(2)}, u32[]{:S(2)}) %collective-permute-start.9) | collective-permute-done | bytes 196640 | tf_op jit(solution)/shard_map/ppermute | solution.py:326
  132.1 5.5 %collective-permute-done.10 = bf16[128,768]{1,0:T(8,128)(2,1)S(1)} collective-permute-done((bf16[128,768]{1,0:T(8,128)(2,1)S(1)}, bf16[128,768]{1,0:T(8,128)(2,1)S(1)}, u32[]{:S(2)}, u32[]{:S(2)}) %collective-permute-start.10) | collective-permute-done | bytes 196640 | tf_op jit(solution)/shard_map/ppermute | solution.py:326
  (42 shorter events, 5.3 us)
Async XLA Ops:
  0.6 15.0 %copy-start = (bf16[128,768]{1,0:T(8,128)(2,1)S(1)}, bf16[128,768]{1,0:T(8,128)(2,1)}, u32[]{:S(2)}) copy-start(bf16[128,768]{1,0:T(8,128)(2,1)} %q_ref.1) | copy-start | bytes 589828
  1.5 16.5 %collective-permute-start = (f32[8,128]{1,0:T(8,128)S(1)}, f32[8,128]{1,0:T(8,128)S(1)}, u32[]{:S(2)}, u32[]{:S(2)}) collective-permute-start(f32[8,128]{1,0:T(8,128)S(1)} %broadcast_select_fusion), channel_id=1, source_target_pairs={{0,257},{1,256},{128,385},{129,384},{256,1},{257,0},{384,129},{385... | collective-permute-start | bytes 12296 | tf_op jit(solution)/shard_map/ppermute | solution.py:322
  15.6 0.7 copy-start.2
  15.6 0.7 copy-start.3
  15.6 0.7 copy-start.4
  16.3 0.9 copy-start.1
  18.8 35.2 %all-to-all-start = ((bf16[8,128,256]{2,1,0:T(8,128)(2,1)}), bf16[8,128,256]{2,1,0:T(8,128)(2,1)S(1)}, u32[]{:S(2)}, u32[]{:S(2)}) async-start(bf16[8,128,256]{2,1,0:T(8,128)(2,1)} %broadcast_in_dim.26), calls=%async_computation | async-start | bytes 1048576 | tf_op jit(solution)/shard_map/all_to_all | solution.py:351
  24.7 12.8 %collective-permute-start.2 = (bf16[2,144,768]{2,1,0:T(8,128)(2,1)S(1)}, bf16[2,144,768]{2,1,0:T(8,128)(2,1)S(1)}, u32[]{:S(2)}, u32[]{:S(2)}) collective-permute-start(bf16[2,144,768]{2,1,0:T(8,128)(2,1)S(1)} %get-tuple-element.31.qg0_ref), channel_id=1, source_target_pairs={{0,48},{16,0},{32,16},{48,32},{1,49},{17,1},{33,17},{49,33},{2,50}... | collective-permute-start | bytes 1327112 | tf_op jit(solution)/shard_map/ppermute | solution.py:326
  29.3 13.2 %collective-permute-start.1 = (bf16[2,144,768]{2,1,0:T(8,128)(2,1)S(1)}, bf16[2,144,768]{2,1,0:T(8,128)(2,1)S(1)}, u32[]{:S(2)}, u32[]{:S(2)}) collective-permute-start(bf16[2,144,768]{2,1,0:T(8,128)(2,1)S(1)} %get-tuple-element.31.qg0_ref), channel_id=1, source_target_pairs={{0,16},{16,32},{32,48},{48,0},{1,17},{17,33},{33,49},{49,1},{2,18}... | collective-permute-start | bytes 1327112 | tf_op jit(solution)/shard_map/ppermute | solution.py:326
  31.3 4.6 %collective-permute-start.3 = (f32[8,128]{1,0:T(8,128)S(1)}, f32[8,128]{1,0:T(8,128)S(1)}, u32[]{:S(2)}, u32[]{:S(2)}) collective-permute-start(f32[8,128]{1,0:T(8,128)S(1)} %fusion.3), channel_id=1, source_target_pairs={{0,2},{2,0},{1,3},{3,1},{4,6},{6,4},{5,7},{7,5},{8,10},{10,8},{9,1... | collective-permute-start | bytes 12296 | tf_op jit(solution)/shard_map/ppermute | solution.py:317
  42.6 11.4 %collective-permute-start.6 = (bf16[144,768]{1,0:T(8,128)(2,1)S(1)}, bf16[144,768]{1,0:T(8,128)(2,1)S(1)}, u32[]{:S(2)}, u32[]{:S(2)}) collective-permute-start(bf16[144,768]{1,0:T(8,128)(2,1)S(1)} %slice_bitcast_fusion.1), channel_id=1, source_target_pairs={{0,48},{16,0},{32,16},{48,32},{1,49},{17,1},{33,17},{49,33},{2,50}... | collective-permute-start | bytes 663560 | tf_op jit(solution)/shard_map/ppermute | solution.py:326
  44.6 9.4 %collective-permute-start.5 = (bf16[144,768]{1,0:T(8,128)(2,1)S(1)}, bf16[144,768]{1,0:T(8,128)(2,1)S(1)}, u32[]{:S(2)}, u32[]{:S(2)}) collective-permute-start(bf16[144,768]{1,0:T(8,128)(2,1)S(1)} %slice_bitcast_fusion.2), channel_id=1, source_target_pairs={{0,16},{16,32},{32,48},{48,0},{1,17},{17,33},{33,49},{49,1},{2,18}... | collective-permute-start | bytes 663560 | tf_op jit(solution)/shard_map/ppermute | solution.py:326
  47.9 6.1 %collective-permute-start.4 = (f32[8,128]{1,0:T(8,128)S(1)}, f32[8,128]{1,0:T(8,128)S(1)}, u32[]{:S(2)}, u32[]{:S(2)}) collective-permute-start(f32[8,128]{1,0:T(8,128)S(1)} %add.37), channel_id=1, source_target_pairs={{0,4},{4,0},{1,5},{5,1},{2,6},{6,2},{3,7},{7,3},{8,12},{12,8},{9,1... | collective-permute-start | bytes 12296 | tf_op jit(solution)/shard_map/ppermute | solution.py:317
  54.0 16.2 %collective-permute-start.7 = (bf16[8,128,256]{2,1,0:T(8,128)(2,1)S(1)}, bf16[8,128,256]{2,1,0:T(8,128)(2,1)S(1)}, u32[]{:S(2)}, u32[]{:S(2)}) collective-permute-start(bf16[8,128,256]{2,1,0:T(8,128)(2,1)S(1)} %all-to-all-done.kv0_ref), channel_id=1, source_target_pairs={{0,8},{8,0},{1,9},{9,1},{2,10},{10,2},{3,11},{11,3},{4,12},{12,4},... | collective-permute-start | bytes 1572872 | tf_op jit(solution)/shard_map/ppermute | solution.py:317
  60.5 19.8 %all-to-all-start.1 = ((f32[16,8,128]{2,1,0:T(8,128)}), f32[16,8,128]{2,1,0:T(8,128)S(1)}, u32[]{:S(2)}, u32[]{:S(2)}) async-start(f32[16,8,128]{2,1,0:T(8,128)} %broadcast_in_dim.30), calls=%async_computation.1 | async-start | bytes 131072 | tf_op jit(solution)/shard_map/all_to_all | solution.py:359
  100.2 5.7 %copy-start.5 = (bf16[128,768]{1,0:T(8,128)(2,1)}, bf16[128,768]{1,0:T(8,128)(2,1)S(1)}, u32[]{:S(2)}) copy-start(bf16[128,768]{1,0:T(8,128)(2,1)S(1)} %get-tuple-element.41) | copy-start | bytes 589828
  100.2 5.7 %copy-start.7 = (bf16[128,768]{1,0:T(8,128)(2,1)}, bf16[128,768]{1,0:T(8,128)(2,1)S(1)}, u32[]{:S(2)}) copy-start(bf16[128,768]{1,0:T(8,128)(2,1)S(1)} %get-tuple-element.40) | copy-start | bytes 589828
  100.2 5.6 %collective-permute-start.11 = (bf16[2,4,128,256]{3,2,1,0:T(8,128)(2,1)S(1)}, bf16[2,4,128,256]{3,2,1,0:T(8,128)(2,1)S(1)}, u32[]{:S(2)}, u32[]{:S(2)}) collective-permute-start(bf16[2,4,128,256]{3,2,1,0:T(8,128)(2,1)S(1)} %get-tuple-element.44), channel_id=1, source_target_pairs={{0,8},{8,0},{1,9},{9,1},{2,10},{10,2},{3,11},{11,3},{4,12},{12,4},... | collective-permute-start | bytes 1572872 | tf_op jit(solution)/shard_map/ppermute | solution.py:317
  106.0 9.4 %collective-permute-start.12 = (bf16[4,128,256]{2,1,0:T(8,128)(2,1)S(1)}, bf16[4,128,256]{2,1,0:T(8,128)(2,1)S(1)}, u32[]{:S(2)}, u32[]{:S(2)}) collective-permute-start(bf16[4,128,256]{2,1,0:T(8,128)(2,1)S(1)} %fusion.2), channel_id=1, source_target_pairs={{0,64},{64,0},{1,65},{65,1},{2,66},{66,2},{3,67},{67,3},{4,68},{68... | collective-permute-start | bytes 786440 | tf_op jit(solution)/shard_map/ppermute | solution.py:317
  116.2 5.2 %copy-start.8 = (bf16[128,768]{1,0:T(8,128)(2,1)S(1)}, bf16[128,768]{1,0:T(8,128)(2,1)}, u32[]{:S(2)}) copy-start(bf16[128,768]{1,0:T(8,128)(2,1)} %copy-done.7) | copy-start | bytes 589828
  116.2 8.0 %copy-start.6 = (bf16[128,768]{1,0:T(8,128)(2,1)S(1)}, bf16[128,768]{1,0:T(8,128)(2,1)}, u32[]{:S(2)}) copy-start(bf16[128,768]{1,0:T(8,128)(2,1)} %copy-done.5) | copy-start | bytes 589828
  116.2 22.2 %all-to-all-start.3 = ((bf16[4,128,256]{2,1,0:T(8,128)(2,1)}), bf16[4,128,256]{2,1,0:T(8,128)(2,1)S(1)}, u32[]{:S(2)}, u32[]{:S(2)}) async-start(bf16[4,128,256]{2,1,0:T(8,128)(2,1)} %fusion.1), calls=%async_computation.3 | async-start | bytes 524288 | tf_op jit(solution)/shard_map/all_to_all | solution.py:401
  121.4 7.8 %collective-permute-start.8 = (bf16[128,768]{1,0:T(8,128)(2,1)S(1)}, bf16[128,768]{1,0:T(8,128)(2,1)S(1)}, u32[]{:S(2)}, u32[]{:S(2)}) collective-permute-start(bf16[128,768]{1,0:T(8,128)(2,1)S(1)} %copy-done.8), channel_id=1, source_target_pairs={{0,48},{16,0},{32,16},{48,32},{1,49},{17,1},{33,17},{49,33},{2,50}... | collective-permute-start | bytes 589832 | tf_op jit(solution)/shard_map/ppermute | solution.py:326
  124.2 7.9 %collective-permute-start.9 = (bf16[128,768]{1,0:T(8,128)(2,1)S(1)}, bf16[128,768]{1,0:T(8,128)(2,1)S(1)}, u32[]{:S(2)}, u32[]{:S(2)}) collective-permute-start(bf16[128,768]{1,0:T(8,128)(2,1)S(1)} %copy-done.6), channel_id=1, source_target_pairs={{0,32},{16,48},{32,0},{48,16},{1,33},{17,49},{33,1},{49,17},{2,34}... | collective-permute-start | bytes 589832 | tf_op jit(solution)/shard_map/ppermute | solution.py:326
  127.3 10.4 %collective-permute-start.10 = (bf16[128,768]{1,0:T(8,128)(2,1)S(1)}, bf16[128,768]{1,0:T(8,128)(2,1)S(1)}, u32[]{:S(2)}, u32[]{:S(2)}) collective-permute-start(bf16[128,768]{1,0:T(8,128)(2,1)S(1)} %get-tuple-element.42), channel_id=1, source_target_pairs={{0,16},{16,32},{32,48},{48,0},{1,17},{17,33},{33,49},{49,1},{2,18}... | collective-permute-start | bytes 589832 | tf_op jit(solution)/shard_map/ppermute | solution.py:326

commit v3 on v2

--- a/solution.py
+++ b/solution.py
@@ -53,17 +53,16 @@
 
 
 def pack_kernel(
-    where_ref, q_ref, g_ref, slot_ref, length_ref, return_ref, qg_ref, seg_ref
+    where_ref, q_ref, slot_ref, length_ref, return_ref, out_ref, seg_ref
 ):
     line_place, core = where_ref[0], where_ref[2]
     width = GROUP * E
-    qg_ref[0, :ROWS, :] = q_ref[...]
-    qg_ref[1, :ROWS, :] = g_ref[...]
+    out_ref[:ROWS, :] = q_ref[...]
     slot = slot_ref[...]
     row = iota((16, ROWS), 0)
     coded = jnp.where(row == 0, slot >> 7, jnp.where(row == 1, slot & 127, 0))
-    qg_ref[:, ROWS:, :] = jnp.zeros((2, 16, width), BF16)
-    qg_ref[0, ROWS:, :ROWS] = coded.astype(F32).astype(BF16)
+    out_ref[ROWS:, :] = jnp.zeros((16, width), BF16)
+    out_ref[ROWS:, :ROWS] = coded.astype(F32).astype(BF16)
 
     lengths_row = length_ref[...].astype(F32)
     before = iota((E, E), 1) <= iota((E, E), 0)
@@ -130,12 +129,12 @@
 
 
 def forward_kernel(
-    where_ref, qg0_ref, qg1_ref, q2_ref, g2_ref, qg3_ref, kv0_ref, kv1_ref,
+    where_ref, q0_ref, q1_ref, q2_ref, q3_ref, g0_ref, g1_ref, g2_ref, g3_ref, kv0_ref, kv1_ref,
     stat_ref, qs_ref, gs_ref, top_ref, sum_ref, term_ref,
 ):
     z, ring, core, slots = place(where_ref)
-    arrange(slots, (qg0_ref.at[0], qg1_ref.at[0], q2_ref, qg3_ref.at[0]), qs_ref)
-    arrange(slots, (qg0_ref.at[1], qg1_ref.at[1], g2_ref, qg3_ref.at[1]), gs_ref)
+    arrange(slots, (q0_ref, q1_ref, q2_ref, q3_ref), qs_ref)
+    arrange(slots, (g0_ref, g1_ref, g2_ref, g3_ref), gs_ref)
     kv_refs = (kv0_ref, kv1_ref)
     edge = z >> 1
     top_ref[...] = jnp.full(top_ref.shape, NEG, F32)
@@ -163,7 +162,7 @@
                 prob * dots, axis=0
             )
 
-    @pl.loop(0, 2 * PARTS - 1)
+    @pl.loop(0, 2 * PARTS - 1, unroll=True)
     def _(index):
         visit(*free_visit(index, edge), None)
 
@@ -185,10 +184,10 @@
 
 
 def lookup_kernel(
-    where_ref, qg0_ref, qg1_ref, q2_ref, g2_ref, qg3_ref, stat_ref, table_ref, seg_ref, out_ref
+    where_ref, q0_ref, q1_ref, q2_ref, q3_ref, stat_ref, table_ref, seg_ref, out_ref
 ):
     z, ring, core, slots = place(where_ref)
-    refs = (qg0_ref.at[0], qg1_ref.at[0], q2_ref, qg3_ref.at[0])
+    refs = (q0_ref, q1_ref, q2_ref, q3_ref)
     table = table_ref[:, 0, :]
     high = table.astype(BF16)
     rest = table - high.astype(F32)
@@ -252,14 +251,14 @@
 
 
 def backward_kernel(
-    where_ref, qg0_ref, qg1_ref, q2_ref, g2_ref, qg3_ref, kv0_ref, kv1_ref, stat_ref,
+    where_ref, q0_ref, q1_ref, q2_ref, q3_ref, g0_ref, g1_ref, g2_ref, g3_ref, kv0_ref, kv1_ref, stat_ref,
     dkv0_ref, dkv1_ref, dq0_ref, dq1_ref, dq2_ref, dq3_ref,
     qs_ref, gs_ref, dqt_ref, acc_ref, shift_ref, term_ref, prob_ref, slope_ref, turn_ref,
 ):
     z, ring, core, slots = place(where_ref)
     kv_refs = (kv0_ref, kv1_ref)
-    arrange(slots, (qg0_ref.at[0], qg1_ref.at[0], q2_ref, qg3_ref.at[0]), qs_ref)
-    arrange(slots, (qg0_ref.at[1], qg1_ref.at[1], g2_ref, qg3_ref.at[1]), gs_ref)
+    arrange(slots, (q0_ref, q1_ref, q2_ref, q3_ref), qs_ref)
+    arrange(slots, (g0_ref, g1_ref, g2_ref, g3_ref), gs_ref)
     merge_stats(stat_ref, shift_ref, term_ref)
     acc_ref[...] = jnp.zeros(acc_ref.shape, F32)
     dqt_ref[...] = jnp.zeros(dqt_ref.shape, F32)
@@ -282,7 +281,7 @@
         acc_ref[half, part, :, E:] += dot(prob_ref[...], gs_ref[group], 1, 0)
         dqt_ref[group] += dot(key, slope, 0, 0)
 
-    @pl.loop(0, 2 * PARTS - 1)
+    @pl.loop(0, 2 * PARTS - 1, unroll=True)
     def _(index):
         visit(*free_visit(index, edge), None)
 
@@ -335,27 +334,33 @@
     kv_own = jnp.broadcast_to(
         jnp.concatenate([keys, values], axis=1)[None], (LINE, ROWS, 2 * E)
     )
-    qg, seg = call(
+    q0, seg = call(
         pack_kernel,
-        (shape((2, ROWS + 16, width), BF16), shape((8, E), F32)),
+        (shape((ROWS + 16, width), BF16), shape((8, E), F32)),
         scalars=1,
-        inputs=5,
+        inputs=4,
     )(
-        where, queries, cotangent, owner_slot.reshape(1, ROWS),
+        where, queries, owner_slot.reshape(1, ROWS),
         seg_lengths.reshape(1, E), seg_return.reshape(1, E),
     )
-    lane = iota((8, E), 1)
-    terms = jnp.where((lane >> 4) == head, jnp.tile(ref_term, 8)[None], 0.0)
-    terms = terms + far_swapped(terms)
-    kv_own, terms, qg = lax.optimization_barrier((kv_own, terms, qg))
+    from_far = far_swapped(ref_term)
+    lane = iota((8, E), 1) >> 4
+    terms = jnp.where(lane == head, jnp.tile(ref_term, 8)[None], 0.0)
+    terms = jnp.where(lane == (head ^ 1), jnp.tile(from_far, 8)[None], terms)
+    kv_own, terms, q0 = lax.optimization_barrier((kv_own, terms, q0))
     kv0 = lax.all_to_all(kv_own, ("quad", "pair"), 0, 0, tiled=True)
-    qg1, qg3 = from_ring(qg, 1), from_ring(qg, 3)
+    g0 = cotangent
+    g3, q1 = from_ring(g0, 3), from_ring(q0, 1)
+    q3, g1 = from_ring(q0, 3), from_ring(g0, 1)
     terms = terms + swapped(terms, "near_col")
-    qg1, qg3, terms = lax.optimization_barrier((qg1, qg3, terms))
+    q1, g3, terms = lax.optimization_barrier((q1, g3, terms))
+    q2, g2 = from_ring(q1, 1), from_ring(g3, 3)
     terms = terms + swapped(terms, "far_col")
-    team = [qg, qg1, from_ring(qg1[0], 1), from_ring(qg3[1], 3), qg3]
-    kv0, terms, *team = lax.optimization_barrier((kv0, terms, *team))
+    kv0, terms, q1, q2, q3, g1, g2, g3 = lax.optimization_barrier(
+        (kv0, terms, q1, q2, q3, g1, g2, g3)
+    )
     kv1 = swapped(kv0, "core")
+    qs, gs = (q0, q1, q2, q3), (g0, g1, g2, g3)
     table = lax.all_to_all(
         jnp.broadcast_to(terms[None], (2 * LINE, 8, E)), ("quad", "pair", "core"), 0, 0, tiled=True
     )
@@ -366,11 +371,11 @@
         shape((8, COLS), F32),
         kv_scratch + [pltpu.VMEM((2, 8, COLS), F32)] * 3,
         scalars=1,
-        inputs=7,
+        inputs=10,
         cost=pl.CostEstimate(flops=4 * E * pairs, bytes_accessed=4 << 20, transcendentals=pairs),
-    )(where, *team, kv0, kv1)
-    stat = call(lookup_kernel, shape((TEAM, 8, COLS), F32), scalars=1, inputs=8)(
-        where, *team, stat, table, seg
+    )(where, *qs, *gs, kv0, kv1)
+    stat = call(lookup_kernel, shape((TEAM, 8, COLS), F32), scalars=1, inputs=7)(
+        where, *qs, stat, table, seg
     )
     stats = lax.all_to_all(stat, "ring", 0, 0, tiled=True)
     core_grad = (2, LINE // 2, ROWS, 2 * E)
@@ -392,9 +397,9 @@
             pltpu.VMEM((HEAD_COLS, E), F32),
         ],
         scalars=1,
-        inputs=8,
+        inputs=11,
         cost=pl.CostEstimate(flops=10 * E * pairs, bytes_accessed=5 << 20, transcendentals=pairs),
-    )(where, *team, kv0, kv1, stats)
+    )(where, *qs, *gs, kv0, kv1, stats)
 
     own = grad0 + swapped(grad1, "core").astype(F32)
     parts = (own[0] + swapped(own[1].astype(BF16), "pair").astype(F32)).astype(BF16)

time: 140 us -> 136 us (0.971)
  waiting for transfers between devices: 29.9 us -> 23.5 us
  starting transfers between devices: 73.4 us -> 78.9 us
  Pallas kernels: 20.1 us -> 17.3 us
    ppermute x7 -> x9, waiting for transfers between devices: 15.1 us -> 8.45 us  [from_ring(): lax.ppermute(x, 'ring', [(i, (i + step) % TEAM) for i in range(TEAM)])]
    ppermute x7 -> x9, starting transfers between devices: 19.6 us -> 26.1 us  [from_ring(): lax.ppermute(x, 'ring', [(i, (i + step) % TEAM) for i in range(TEAM)])]
    all_to_all x1, starting transfers between devices: 5.2 us -> 3.63 us  [per_device(): parts = lax.all_to_all(parts, 'quad', 0, 0, tiled=True)]
    pallas_call x1, Pallas kernels: 11.5 us -> 10 us  [per_device(): call(backward_kernel, (shape(core_grad, F32), shape(core_grad, BF16), sha...]
  transfers between devices with their start and end apart: 16 -> 18, of which waited for: 9 -> 6; matrix products, arithmetic and copies ran while one was open for 2% -> 2% of each run, Pallas kernels for 6% -> 5%
where the time goes in v3:
time: 136 us; the launch traced here: 135 us
  starting transfers between devices  78.9 us (58%)
  waiting for transfers between devices  23.5 us (17%)
  Pallas kernels  17.3 us (13%)
  blocking collectives  7.77 us (6%)
  local copies, waits for them, and re-layouts  3.68 us (3%)
  other arithmetic  2.57 us (2%)
    ppermute x9, starting transfers between devices, from_ring(): lax.ppermute(x, 'ring', [(i, (i + step) % TEAM) for i in range(TEAM)])  26.1 us
    ppermute x5, starting transfers between devices, swapped(): return lax.ppermute(x, axis, [(0, 1), (1, 0)])  19.6 us
    ppermute x1, starting transfers between devices, far_swapped(): return lax.ppermute(x, ('quad', 'far'), pairs)  13.4 us
    ppermute x5, waiting for transfers between devices, swapped(): return lax.ppermute(x, axis, [(0, 1), (1, 0)])  10.8 us
    all_to_all x1, starting transfers between devices, per_device(): lax.all_to_all(jnp.broadcast_to(terms[None], (2 * LINE, 8, E)), ('quad',...  10 us
    pallas_call x1, Pallas kernels, per_device(): call(backward_kernel, (shape(core_grad, F32), shape(core_grad, BF16), sha...  10 us
    ppermute x9, waiting for transfers between devices, from_ring(): lax.ppermute(x, 'ring', [(i, (i + step) % TEAM) for i in range(TEAM)])  8.45 us
    all_to_all x1, blocking collectives, per_device(): stats = lax.all_to_all(stat, 'ring', 0, 0, tiled=True)  7.77 us
  transfers between devices with their start and end apart: 18, of which 6 were waited for; matrix products, arithmetic and copies ran while one was open for 2% of the time, Pallas kernels for 5%

profile of v3, /device:TPU:1, one launch (start us, length us, event | category | flops | bytes accessed | tf_op | source)
XLA Modules:
  0.0 134.6 jit_solution(10452801743419694736)
XLA Ops:
  0.6 13.4 %collective-permute-start = (f32[16]{0:T(128)}, f32[16]{0:T(128)S(1)}, u32[]{:S(2)}, u32[]{:S(2)}) collective-permute-start(f32[16]{0:T(128)} %param.15), channel_id=1, source_target_pairs={{0,257},{1,256},{128,385},{129,384},{256,1},{257,0},{384,129},{385... | collective-permute-start | bytes 200 | tf_op jit(solution)/shard_map/ppermute | solution.py:321
  14.9 0.8 pad_maximum_fusion
  17.2 0.8 broadcast_in_dim.36
  18.0 6.0 %all-to-all-start = ((bf16[8,128,256]{2,1,0:T(8,128)(2,1)}), bf16[8,128,256]{2,1,0:T(8,128)(2,1)S(1)}, u32[]{:S(2)}, u32[]{:S(2)}) async-start(bf16[8,128,256]{2,1,0:T(8,128)(2,1)} %broadcast_in_dim.36), calls=%async_computation | async-start | bytes 1048576 | tf_op jit(solution)/shard_map/all_to_all | solution.py:351
  24.1 3.2 %collective-permute-start.1 = (bf16[144,768]{1,0:T(8,128)(2,1)S(1)}, bf16[144,768]{1,0:T(8,128)(2,1)S(1)}, u32[]{:S(2)}, u32[]{:S(2)}) collective-permute-start(bf16[144,768]{1,0:T(8,128)(2,1)S(1)} %get-tuple-element.26.q0_ref), channel_id=1, source_target_pairs={{0,16},{16,32},{32,48},{48,0},{1,17},{17,33},{33,49},{49,1},{2,18}... | collective-permute-start | bytes 663560 | tf_op jit(solution)/shard_map/ppermute | solution.py:325
  27.3 3.4 %collective-permute-start.2 = (bf16[128,768]{1,0:T(8,128)(2,1)S(1)}, bf16[128,768]{1,0:T(8,128)(2,1)S(1)}, u32[]{:S(2)}, u32[]{:S(2)}) collective-permute-start(bf16[128,768]{1,0:T(8,128)(2,1)S(1)} %copy-done.4), channel_id=1, source_target_pairs={{0,48},{16,0},{32,16},{48,32},{1,49},{17,1},{33,17},{49,33},{2,50}... | collective-permute-start | bytes 589832 | tf_op jit(solution)/shard_map/ppermute | solution.py:325
  30.7 3.1 %collective-permute-start.3 = (f32[8,128]{1,0:T(8,128)S(1)}, f32[8,128]{1,0:T(8,128)S(1)}, u32[]{:S(2)}, u32[]{:S(2)}) collective-permute-start(f32[8,128]{1,0:T(8,128)S(1)} %select_select_fusion), channel_id=1, source_target_pairs={{0,2},{2,0},{1,3},{3,1},{4,6},{6,4},{5,7},{7,5},{8,10},{10,8},{9,1... | collective-permute-start | bytes 12296 | tf_op jit(solution)/shard_map/ppermute | solution.py:316
  33.8 3.4 %collective-permute-start.6 = (bf16[144,768]{1,0:T(8,128)(2,1)S(1)}, bf16[144,768]{1,0:T(8,128)(2,1)S(1)}, u32[]{:S(2)}, u32[]{:S(2)}) collective-permute-start(bf16[144,768]{1,0:T(8,128)(2,1)S(1)} %get-tuple-element.26.q0_ref), channel_id=1, source_target_pairs={{0,48},{16,0},{32,16},{48,32},{1,49},{17,1},{33,17},{49,33},{2,50}... | collective-permute-start | bytes 663560 | tf_op jit(solution)/shard_map/ppermute | solution.py:325
  37.2 1.9 %collective-permute-start.5 = (bf16[144,768]{1,0:T(8,128)(2,1)S(1)}, bf16[144,768]{1,0:T(8,128)(2,1)S(1)}, u32[]{:S(2)}, u32[]{:S(2)}) collective-permute-start(bf16[144,768]{1,0:T(8,128)(2,1)S(1)} %collective-permute-done.1.q1_ref), channel_id=1, source_target_pairs={{0,16},{16,32},{32,48},{48,0},{1,17},{17,33},{33,49},{49,1},{2,18}... | collective-permute-start | bytes 663560 | tf_op jit(solution)/shard_map/ppermute | solution.py:325
  39.1 1.9 %collective-permute-start.7 = (bf16[128,768]{1,0:T(8,128)(2,1)S(1)}, bf16[128,768]{1,0:T(8,128)(2,1)S(1)}, u32[]{:S(2)}, u32[]{:S(2)}) collective-permute-start(bf16[128,768]{1,0:T(8,128)(2,1)S(1)} %copy-done.4), channel_id=1, source_target_pairs={{0,16},{16,32},{32,48},{48,0},{1,17},{17,33},{33,49},{49,1},{2,18}... | collective-permute-start | bytes 589832 | tf_op jit(solution)/shard_map/ppermute | solution.py:325
  41.1 4.6 %collective-permute-start.8 = (bf16[128,768]{1,0:T(8,128)(2,1)S(1)}, bf16[128,768]{1,0:T(8,128)(2,1)S(1)}, u32[]{:S(2)}, u32[]{:S(2)}) collective-permute-start(bf16[128,768]{1,0:T(8,128)(2,1)S(1)} %collective-permute-done.2.g3_ref), channel_id=1, source_target_pairs={{0,48},{16,0},{32,16},{48,32},{1,49},{17,1},{33,17},{49,33},{2,50}... | collective-permute-start | bytes 589832 | tf_op jit(solution)/shard_map/ppermute | solution.py:325
  45.6 4.4 %collective-permute-start.4 = (f32[8,128]{1,0:T(8,128)S(1)}, f32[8,128]{1,0:T(8,128)S(1)}, u32[]{:S(2)}, u32[]{:S(2)}) collective-permute-start(f32[8,128]{1,0:T(8,128)S(1)} %add.33), channel_id=1, source_target_pairs={{0,4},{4,0},{1,5},{5,1},{2,6},{6,2},{3,7},{7,3},{8,12},{12,8},{9,1... | collective-permute-start | bytes 12296 | tf_op jit(solution)/shard_map/ppermute | solution.py:316
  50.0 1.8 %collective-permute-done.4 = f32[8,128]{1,0:T(8,128)S(1)} collective-permute-done((f32[8,128]{1,0:T(8,128)S(1)}, f32[8,128]{1,0:T(8,128)S(1)}, u32[]{:S(2)}, u32[]{:S(2)}) %collective-permute-start.4) | collective-permute-done | bytes 4128 | tf_op jit(solution)/shard_map/ppermute | solution.py:316
  51.8 5.9 %collective-permute-start.9 = (bf16[8,128,256]{2,1,0:T(8,128)(2,1)S(1)}, bf16[8,128,256]{2,1,0:T(8,128)(2,1)S(1)}, u32[]{:S(2)}, u32[]{:S(2)}) collective-permute-start(bf16[8,128,256]{2,1,0:T(8,128)(2,1)S(1)} %all-to-all-done.kv0_ref), channel_id=1, source_target_pairs={{0,8},{8,0},{1,9},{9,1},{2,10},{10,2},{3,11},{11,3},{4,12},{12,4},... | collective-permute-start | bytes 1572872 | tf_op jit(solution)/shard_map/ppermute | solution.py:316
  58.4 10.0 %all-to-all-start.1 = ((f32[16,8,128]{2,1,0:T(8,128)}), f32[16,8,128]{2,1,0:T(8,128)S(1)}, u32[]{:S(2)}, u32[]{:S(2)}) async-start(f32[16,8,128]{2,1,0:T(8,128)} %broadcast_in_dim.42), calls=%async_computation.1 | async-start | bytes 131072 | tf_op jit(solution)/shard_map/all_to_all | solution.py:364
  68.4 5.8 %shard_map.104.stat_ref = f32[8,1536]{1,0:T(8,128)S(1)} custom-call(s32[4]{0:T(128)S(1)} %pad_add_fusion.where_ref, bf16[144,768]{1,0:T(8,128)(2,1)S(1)} %get-tuple-element.26.q0_ref, bf16[144,768]{1,0:T(8,128)(2,1)S(1)} %collective-permute-done.1.q1_ref, bf16[144,768]{1,0:T(8,128)(2,1)S(1)} %collective-permute-done.5.q2_ref, ...), custom_call_target="tpu_custom_call" | custom-call | flops 1811939328 | bytes 4194304 | tf_op jit(solution)/shard_map/pallas_call | solution.py:369
  74.3 4.2 %all-to-all-done.1.table_ref = f32[16,8,128]{2,1,0:T(8,128)S(1)} async-done(((f32[16,8,128]{2,1,0:T(8,128)}), f32[16,8,128]{2,1,0:T(8,128)S(1)}, u32[]{:S(2)}, u32[]{:S(2)}) %all-to-all-start.1) | async-done | bytes 65568 | tf_op jit(solution)/shard_map/all_to_all | solution.py:364
  78.5 0.8 shard_map.105
  79.3 7.8 %all_to_all.20.stat_ref = f32[4,8,1536]{2,1,0:T(8,128)S(1)} all-to-all(f32[4,8,1536]{2,1,0:T(8,128)S(1)} %shard_map.105), channel_id=1, replica_groups=mesh['quad'=4,'pair'=2,'ring'=4,'core'=2,'far_col'=2,'near_col'=2,'far'=..., dimensions={0} | all-to-all | bytes 393216 | tf_op jit(solution)/shard_map/all_to_all | solution.py:380
  87.1 10.0 %shard_map.106 = (f32[2,4,128,256]{3,2,1,0:T(8,128)S(1)}, bf16[2,4,128,256]{3,2,1,0:T(8,128)(2,1)S(1)}, f32[128,768]{1,0:T(8,128)S(1)}, bf16[128,768]{1,0:T(8,12...) custom-call(s32[4]{0:T(128)S(1)} %pad_add_fusion.where_ref, ...), custom_call_target="tpu_custom_call" | custom-call | flops 4529848320 | bytes 5242880 | tf_op jit(solution)/shard_map/pallas_call | solution.py:383
  97.1 4.3 %collective-permute-start.13 = (bf16[2,4,128,256]{3,2,1,0:T(8,128)(2,1)S(1)}, bf16[2,4,128,256]{3,2,1,0:T(8,128)(2,1)S(1)}, u32[]{:S(2)}, u32[]{:S(2)}) collective-permute-start(bf16[2,4,128,256]{3,2,1,0:T(8,128)(2,1)S(1)} %get-tuple-element.46), channel_id=1, source_target_pairs={{0,8},{8,0},{1,9},{9,1},{2,10},{10,2},{3,11},{11,3},{4,12},{12,4},... | collective-permute-start | bytes 1572872 | tf_op jit(solution)/shard_map/ppermute | solution.py:316
  101.4 1.5 %collective-permute-done.13 = bf16[2,4,128,256]{3,2,1,0:T(8,128)(2,1)S(1)} collective-permute-done((bf16[2,4,128,256]{3,2,1,0:T(8,128)(2,1)S(1)}, bf16[2,4,128,256]{3,2,1,0:T(8,128)(2,1)S(1)}, u32[]{:S(2)}, u32[]{:S(2)}) %collective-permute-start.13) | collective-permute-done | bytes 524320 | tf_op jit(solution)/shard_map/ppermute | solution.py:316
  103.1 1.9 %collective-permute-start.14 = (bf16[4,128,256]{2,1,0:T(8,128)(2,1)S(1)}, bf16[4,128,256]{2,1,0:T(8,128)(2,1)S(1)}, u32[]{:S(2)}, u32[]{:S(2)}) collective-permute-start(bf16[4,128,256]{2,1,0:T(8,128)(2,1)S(1)} %fusion.2), channel_id=1, source_target_pairs={{0,64},{64,0},{1,65},{65,1},{2,66},{66,2},{3,67},{67,3},{4,68},{68... | collective-permute-start | bytes 786440 | tf_op jit(solution)/shard_map/ppermute | solution.py:316
  105.0 7.5 %collective-permute-done.14 = bf16[4,128,256]{2,1,0:T(8,128)(2,1)S(1)} collective-permute-done((bf16[4,128,256]{2,1,0:T(8,128)(2,1)S(1)}, bf16[4,128,256]{2,1,0:T(8,128)(2,1)S(1)}, u32[]{:S(2)}, u32[]{:S(2)}) %collective-permute-start.14) | collective-permute-done | bytes 262176 | tf_op jit(solution)/shard_map/ppermute | solution.py:316
  112.5 0.8 fusion.1
  113.3 3.6 %all-to-all-start.3 = ((bf16[4,128,256]{2,1,0:T(8,128)(2,1)}), bf16[4,128,256]{2,1,0:T(8,128)(2,1)S(1)}, u32[]{:S(2)}, u32[]{:S(2)}) async-start(bf16[4,128,256]{2,1,0:T(8,128)(2,1)} %fusion.1), calls=%async_computation.3 | async-start | bytes 524288 | tf_op jit(solution)/shard_map/all_to_all | solution.py:406
  116.9 2.8 %collective-permute-start.10 = (bf16[128,768]{1,0:T(8,128)(2,1)S(1)}, bf16[128,768]{1,0:T(8,128)(2,1)S(1)}, u32[]{:S(2)}, u32[]{:S(2)}) collective-permute-start(bf16[128,768]{1,0:T(8,128)(2,1)S(1)} %copy-done.6), channel_id=1, source_target_pairs={{0,48},{16,0},{32,16},{48,32},{1,49},{17,1},{33,17},{49,33},{2,50}... | collective-permute-start | bytes 589832 | tf_op jit(solution)/shard_map/ppermute | solution.py:325
  119.7 3.1 %collective-permute-start.11 = (bf16[128,768]{1,0:T(8,128)(2,1)S(1)}, bf16[128,768]{1,0:T(8,128)(2,1)S(1)}, u32[]{:S(2)}, u32[]{:S(2)}) collective-permute-start(bf16[128,768]{1,0:T(8,128)(2,1)S(1)} %get-tuple-element.43), channel_id=1, source_target_pairs={{0,32},{16,48},{32,0},{48,16},{1,33},{17,49},{33,1},{49,17},{2,34}... | collective-permute-start | bytes 589832 | tf_op jit(solution)/shard_map/ppermute | solution.py:325
  122.8 1.9 %collective-permute-start.12 = (bf16[128,768]{1,0:T(8,128)(2,1)S(1)}, bf16[128,768]{1,0:T(8,128)(2,1)S(1)}, u32[]{:S(2)}, u32[]{:S(2)}) collective-permute-start(bf16[128,768]{1,0:T(8,128)(2,1)S(1)} %get-tuple-element.44), channel_id=1, source_target_pairs={{0,16},{16,32},{32,48},{48,0},{1,17},{17,33},{33,49},{49,1},{2,18}... | collective-permute-start | bytes 589832 | tf_op jit(solution)/shard_map/ppermute | solution.py:325
  124.8 2.9 %collective-permute-done.11 = bf16[128,768]{1,0:T(8,128)(2,1)S(1)} collective-permute-done((bf16[128,768]{1,0:T(8,128)(2,1)S(1)}, bf16[128,768]{1,0:T(8,128)(2,1)S(1)}, u32[]{:S(2)}, u32[]{:S(2)}) %collective-permute-start.11) | collective-permute-done | bytes 196640 | tf_op jit(solution)/shard_map/ppermute | solution.py:325
  127.6 5.5 %collective-permute-done.12 = bf16[128,768]{1,0:T(8,128)(2,1)S(1)} collective-permute-done((bf16[128,768]{1,0:T(8,128)(2,1)S(1)}, bf16[128,768]{1,0:T(8,128)(2,1)S(1)}, u32[]{:S(2)}, u32[]{:S(2)}) %collective-permute-start.12) | collective-permute-done | bytes 196640 | tf_op jit(solution)/shard_map/ppermute | solution.py:325
  133.2 0.8 add_convert_fusion
  (41 shorter events, 3.8 us)
Async XLA Ops:
  0.6 15.1 %copy-start = (bf16[128,768]{1,0:T(8,128)(2,1)S(1)}, bf16[128,768]{1,0:T(8,128)(2,1)}, u32[]{:S(2)}) copy-start(bf16[128,768]{1,0:T(8,128)(2,1)} %q_ref.1) | copy-start | bytes 589828
  0.6 16.4 %collective-permute-start = (f32[16]{0:T(128)}, f32[16]{0:T(128)S(1)}, u32[]{:S(2)}, u32[]{:S(2)}) collective-permute-start(f32[16]{0:T(128)} %param.15), channel_id=1, source_target_pairs={{0,257},{1,256},{128,385},{129,384},{256,1},{257,0},{384,129},{385... | collective-permute-start | bytes 200 | tf_op jit(solution)/shard_map/ppermute | solution.py:321
  15.7 0.7 copy-start.1
  15.7 0.7 copy-start.2
  15.7 0.7 copy-start.3
  18.0 9.2 %copy-start.4 = (bf16[128,768]{1,0:T(8,128)(2,1)S(1)}, bf16[128,768]{1,0:T(8,128)(2,1)}, u32[]{:S(2)}) copy-start(bf16[128,768]{1,0:T(8,128)(2,1)} %g0_ref.3) | copy-start | bytes 589828
  18.0 33.8 %all-to-all-start = ((bf16[8,128,256]{2,1,0:T(8,128)(2,1)}), bf16[8,128,256]{2,1,0:T(8,128)(2,1)S(1)}, u32[]{:S(2)}, u32[]{:S(2)}) async-start(bf16[8,128,256]{2,1,0:T(8,128)(2,1)} %broadcast_in_dim.36), calls=%async_computation | async-start | bytes 1048576 | tf_op jit(solution)/shard_map/all_to_all | solution.py:351
  24.1 13.1 %collective-permute-start.1 = (bf16[144,768]{1,0:T(8,128)(2,1)S(1)}, bf16[144,768]{1,0:T(8,128)(2,1)S(1)}, u32[]{:S(2)}, u32[]{:S(2)}) collective-permute-start(bf16[144,768]{1,0:T(8,128)(2,1)S(1)} %get-tuple-element.26.q0_ref), channel_id=1, source_target_pairs={{0,16},{16,32},{32,48},{48,0},{1,17},{17,33},{33,49},{49,1},{2,18}... | collective-permute-start | bytes 663560 | tf_op jit(solution)/shard_map/ppermute | solution.py:325
  27.3 9.9 %collective-permute-start.2 = (bf16[128,768]{1,0:T(8,128)(2,1)S(1)}, bf16[128,768]{1,0:T(8,128)(2,1)S(1)}, u32[]{:S(2)}, u32[]{:S(2)}) collective-permute-start(bf16[128,768]{1,0:T(8,128)(2,1)S(1)} %copy-done.4), channel_id=1, source_target_pairs={{0,48},{16,0},{32,16},{48,32},{1,49},{17,1},{33,17},{49,33},{2,50}... | collective-permute-start | bytes 589832 | tf_op jit(solution)/shard_map/ppermute | solution.py:325
  30.7 6.5 %collective-permute-start.3 = (f32[8,128]{1,0:T(8,128)S(1)}, f32[8,128]{1,0:T(8,128)S(1)}, u32[]{:S(2)}, u32[]{:S(2)}) collective-permute-start(f32[8,128]{1,0:T(8,128)S(1)} %select_select_fusion), channel_id=1, source_target_pairs={{0,2},{2,0},{1,3},{3,1},{4,6},{6,4},{5,7},{7,5},{8,10},{10,8},{9,1... | collective-permute-start | bytes 12296 | tf_op jit(solution)/shard_map/ppermute | solution.py:316
  33.8 18.0 %collective-permute-start.6 = (bf16[144,768]{1,0:T(8,128)(2,1)S(1)}, bf16[144,768]{1,0:T(8,128)(2,1)S(1)}, u32[]{:S(2)}, u32[]{:S(2)}) collective-permute-start(bf16[144,768]{1,0:T(8,128)(2,1)S(1)} %get-tuple-element.26.q0_ref), channel_id=1, source_target_pairs={{0,48},{16,0},{32,16},{48,32},{1,49},{17,1},{33,17},{49,33},{2,50}... | collective-permute-start | bytes 663560 | tf_op jit(solution)/shard_map/ppermute | solution.py:325
  37.2 14.6 %collective-permute-start.5 = (bf16[144,768]{1,0:T(8,128)(2,1)S(1)}, bf16[144,768]{1,0:T(8,128)(2,1)S(1)}, u32[]{:S(2)}, u32[]{:S(2)}) collective-permute-start(bf16[144,768]{1,0:T(8,128)(2,1)S(1)} %collective-permute-done.1.q1_ref), channel_id=1, source_target_pairs={{0,16},{16,32},{32,48},{48,0},{1,17},{17,33},{33,49},{49,1},{2,18}... | collective-permute-start | bytes 663560 | tf_op jit(solution)/shard_map/ppermute | solution.py:325
  39.1 12.7 %collective-permute-start.7 = (bf16[128,768]{1,0:T(8,128)(2,1)S(1)}, bf16[128,768]{1,0:T(8,128)(2,1)S(1)}, u32[]{:S(2)}, u32[]{:S(2)}) collective-permute-start(bf16[128,768]{1,0:T(8,128)(2,1)S(1)} %copy-done.4), channel_id=1, source_target_pairs={{0,16},{16,32},{32,48},{48,0},{1,17},{17,33},{33,49},{49,1},{2,18}... | collective-permute-start | bytes 589832 | tf_op jit(solution)/shard_map/ppermute | solution.py:325
  41.1 10.7 %collective-permute-start.8 = (bf16[128,768]{1,0:T(8,128)(2,1)S(1)}, bf16[128,768]{1,0:T(8,128)(2,1)S(1)}, u32[]{:S(2)}, u32[]{:S(2)}) collective-permute-start(bf16[128,768]{1,0:T(8,128)(2,1)S(1)} %collective-permute-done.2.g3_ref), channel_id=1, source_target_pairs={{0,48},{16,0},{32,16},{48,32},{1,49},{17,1},{33,17},{49,33},{2,50}... | collective-permute-start | bytes 589832 | tf_op jit(solution)/shard_map/ppermute | solution.py:325
  45.6 6.2 %collective-permute-start.4 = (f32[8,128]{1,0:T(8,128)S(1)}, f32[8,128]{1,0:T(8,128)S(1)}, u32[]{:S(2)}, u32[]{:S(2)}) collective-permute-start(f32[8,128]{1,0:T(8,128)S(1)} %add.33), channel_id=1, source_target_pairs={{0,4},{4,0},{1,5},{5,1},{2,6},{6,2},{3,7},{7,3},{8,12},{12,8},{9,1... | collective-permute-start | bytes 12296 | tf_op jit(solution)/shard_map/ppermute | solution.py:316
  51.8 16.6 %collective-permute-start.9 = (bf16[8,128,256]{2,1,0:T(8,128)(2,1)S(1)}, bf16[8,128,256]{2,1,0:T(8,128)(2,1)S(1)}, u32[]{:S(2)}, u32[]{:S(2)}) collective-permute-start(bf16[8,128,256]{2,1,0:T(8,128)(2,1)S(1)} %all-to-all-done.kv0_ref), channel_id=1, source_target_pairs={{0,8},{8,0},{1,9},{9,1},{2,10},{10,2},{3,11},{11,3},{4,12},{12,4},... | collective-permute-start | bytes 1572872 | tf_op jit(solution)/shard_map/ppermute | solution.py:316
  58.4 20.1 %all-to-all-start.1 = ((f32[16,8,128]{2,1,0:T(8,128)}), f32[16,8,128]{2,1,0:T(8,128)S(1)}, u32[]{:S(2)}, u32[]{:S(2)}) async-start(f32[16,8,128]{2,1,0:T(8,128)} %broadcast_in_dim.42), calls=%async_computation.1 | async-start | bytes 131072 | tf_op jit(solution)/shard_map/all_to_all | solution.py:364
  97.1 6.0 %copy-start.5 = (bf16[128,768]{1,0:T(8,128)(2,1)}, bf16[128,768]{1,0:T(8,128)(2,1)S(1)}, u32[]{:S(2)}) copy-start(bf16[128,768]{1,0:T(8,128)(2,1)S(1)} %get-tuple-element.42) | copy-start | bytes 589828
  97.1 5.9 %collective-permute-start.13 = (bf16[2,4,128,256]{3,2,1,0:T(8,128)(2,1)S(1)}, bf16[2,4,128,256]{3,2,1,0:T(8,128)(2,1)S(1)}, u32[]{:S(2)}, u32[]{:S(2)}) collective-permute-start(bf16[2,4,128,256]{3,2,1,0:T(8,128)(2,1)S(1)} %get-tuple-element.46), channel_id=1, source_target_pairs={{0,8},{8,0},{1,9},{9,1},{2,10},{10,2},{3,11},{11,3},{4,12},{12,4},... | collective-permute-start | bytes 1572872 | tf_op jit(solution)/shard_map/ppermute | solution.py:316
  103.1 9.4 %collective-permute-start.14 = (bf16[4,128,256]{2,1,0:T(8,128)(2,1)S(1)}, bf16[4,128,256]{2,1,0:T(8,128)(2,1)S(1)}, u32[]{:S(2)}, u32[]{:S(2)}) collective-permute-start(bf16[4,128,256]{2,1,0:T(8,128)(2,1)S(1)} %fusion.2), channel_id=1, source_target_pairs={{0,64},{64,0},{1,65},{65,1},{2,66},{66,2},{3,67},{67,3},{4,68},{68... | collective-permute-start | bytes 786440 | tf_op jit(solution)/shard_map/ppermute | solution.py:316
  113.3 3.6 %copy-start.6 = (bf16[128,768]{1,0:T(8,128)(2,1)S(1)}, bf16[128,768]{1,0:T(8,128)(2,1)}, u32[]{:S(2)}) copy-start(bf16[128,768]{1,0:T(8,128)(2,1)} %copy-done.5) | copy-start | bytes 589828
  113.3 20.7 %all-to-all-start.3 = ((bf16[4,128,256]{2,1,0:T(8,128)(2,1)}), bf16[4,128,256]{2,1,0:T(8,128)(2,1)S(1)}, u32[]{:S(2)}, u32[]{:S(2)}) async-start(bf16[4,128,256]{2,1,0:T(8,128)(2,1)} %fusion.1), calls=%async_computation.3 | async-start | bytes 524288 | tf_op jit(solution)/shard_map/all_to_all | solution.py:406
  116.9 7.8 %collective-permute-start.10 = (bf16[128,768]{1,0:T(8,128)(2,1)S(1)}, bf16[128,768]{1,0:T(8,128)(2,1)S(1)}, u32[]{:S(2)}, u32[]{:S(2)}) collective-permute-start(bf16[128,768]{1,0:T(8,128)(2,1)S(1)} %copy-done.6), channel_id=1, source_target_pairs={{0,48},{16,0},{32,16},{48,32},{1,49},{17,1},{33,17},{49,33},{2,50}... | collective-permute-start | bytes 589832 | tf_op jit(solution)/shard_map/ppermute | solution.py:325
  119.7 7.9 %collective-permute-start.11 = (bf16[128,768]{1,0:T(8,128)(2,1)S(1)}, bf16[128,768]{1,0:T(8,128)(2,1)S(1)}, u32[]{:S(2)}, u32[]{:S(2)}) collective-permute-start(bf16[128,768]{1,0:T(8,128)(2,1)S(1)} %get-tuple-element.43), channel_id=1, source_target_pairs={{0,32},{16,48},{32,0},{48,16},{1,33},{17,49},{33,1},{49,17},{2,34}... | collective-permute-start | bytes 589832 | tf_op jit(solution)/shard_map/ppermute | solution.py:325
  122.8 10.4 %collective-permute-start.12 = (bf16[128,768]{1,0:T(8,128)(2,1)S(1)}, bf16[128,768]{1,0:T(8,128)(2,1)S(1)}, u32[]{:S(2)}, u32[]{:S(2)}) collective-permute-start(bf16[128,768]{1,0:T(8,128)(2,1)S(1)} %get-tuple-element.44), channel_id=1, source_target_pairs={{0,16},{16,32},{32,48},{48,0},{1,17},{17,33},{33,49},{49,1},{2,18}... | collective-permute-start | bytes 589832 | tf_op jit(solution)/shard_map/ppermute | solution.py:325

commit v4 on v2

--- a/solution.py
+++ b/solution.py
@@ -53,17 +53,17 @@
 
 
 def pack_kernel(
-    where_ref, q_ref, g_ref, slot_ref, length_ref, return_ref, qg_ref, seg_ref
+    where_ref, q_ref, g_ref, slot_ref, length_ref, return_ref, out_ref, seg_ref
 ):
     line_place, core = where_ref[0], where_ref[2]
     width = GROUP * E
-    qg_ref[0, :ROWS, :] = q_ref[...]
-    qg_ref[1, :ROWS, :] = g_ref[...]
+    out_ref[0, :ROWS, :] = q_ref[...]
+    out_ref[1, :ROWS, :] = g_ref[...]
     slot = slot_ref[...]
     row = iota((16, ROWS), 0)
     coded = jnp.where(row == 0, slot >> 7, jnp.where(row == 1, slot & 127, 0))
-    qg_ref[:, ROWS:, :] = jnp.zeros((2, 16, width), BF16)
-    qg_ref[0, ROWS:, :ROWS] = coded.astype(F32).astype(BF16)
+    out_ref[:, ROWS:, :] = jnp.zeros((2, 16, width), BF16)
+    out_ref[0, ROWS:, :ROWS] = coded.astype(F32).astype(BF16)
 
     lengths_row = length_ref[...].astype(F32)
     before = iota((E, E), 1) <= iota((E, E), 0)
@@ -130,12 +130,13 @@
 
 
 def forward_kernel(
-    where_ref, qg0_ref, qg1_ref, q2_ref, g2_ref, qg3_ref, kv0_ref, kv1_ref,
+    where_ref, qg0_ref, qg1_ref, qg2_ref, qg3_ref, kv0_ref, kv1_ref,
     stat_ref, qs_ref, gs_ref, top_ref, sum_ref, term_ref,
 ):
     z, ring, core, slots = place(where_ref)
-    arrange(slots, (qg0_ref.at[0], qg1_ref.at[0], q2_ref, qg3_ref.at[0]), qs_ref)
-    arrange(slots, (qg0_ref.at[1], qg1_ref.at[1], g2_ref, qg3_ref.at[1]), gs_ref)
+    refs = (qg0_ref, qg1_ref, qg2_ref, qg3_ref)
+    arrange(slots, [ref.at[0] for ref in refs], qs_ref)
+    arrange(slots, [ref.at[1] for ref in refs], gs_ref)
     kv_refs = (kv0_ref, kv1_ref)
     edge = z >> 1
     top_ref[...] = jnp.full(top_ref.shape, NEG, F32)
@@ -163,7 +164,7 @@
                 prob * dots, axis=0
             )
 
-    @pl.loop(0, 2 * PARTS - 1)
+    @pl.loop(0, 2 * PARTS - 1, unroll=True)
     def _(index):
         visit(*free_visit(index, edge), None)
 
@@ -185,10 +186,10 @@
 
 
 def lookup_kernel(
-    where_ref, qg0_ref, qg1_ref, q2_ref, g2_ref, qg3_ref, stat_ref, table_ref, seg_ref, out_ref
+    where_ref, qg0_ref, qg1_ref, qg2_ref, qg3_ref, stat_ref, table_ref, seg_ref, out_ref
 ):
     z, ring, core, slots = place(where_ref)
-    refs = (qg0_ref.at[0], qg1_ref.at[0], q2_ref, qg3_ref.at[0])
+    refs = [ref.at[0] for ref in (qg0_ref, qg1_ref, qg2_ref, qg3_ref)]
     table = table_ref[:, 0, :]
     high = table.astype(BF16)
     rest = table - high.astype(F32)
@@ -252,14 +253,15 @@
 
 
 def backward_kernel(
-    where_ref, qg0_ref, qg1_ref, q2_ref, g2_ref, qg3_ref, kv0_ref, kv1_ref, stat_ref,
+    where_ref, qg0_ref, qg1_ref, qg2_ref, qg3_ref, kv0_ref, kv1_ref, stat_ref,
     dkv0_ref, dkv1_ref, dq0_ref, dq1_ref, dq2_ref, dq3_ref,
     qs_ref, gs_ref, dqt_ref, acc_ref, shift_ref, term_ref, prob_ref, slope_ref, turn_ref,
 ):
     z, ring, core, slots = place(where_ref)
     kv_refs = (kv0_ref, kv1_ref)
-    arrange(slots, (qg0_ref.at[0], qg1_ref.at[0], q2_ref, qg3_ref.at[0]), qs_ref)
-    arrange(slots, (qg0_ref.at[1], qg1_ref.at[1], g2_ref, qg3_ref.at[1]), gs_ref)
+    refs = (qg0_ref, qg1_ref, qg2_ref, qg3_ref)
+    arrange(slots, [ref.at[0] for ref in refs], qs_ref)
+    arrange(slots, [ref.at[1] for ref in refs], gs_ref)
     merge_stats(stat_ref, shift_ref, term_ref)
     acc_ref[...] = jnp.zeros(acc_ref.shape, F32)
     dqt_ref[...] = jnp.zeros(dqt_ref.shape, F32)
@@ -282,7 +284,7 @@
         acc_ref[half, part, :, E:] += dot(prob_ref[...], gs_ref[group], 1, 0)
         dqt_ref[group] += dot(key, slope, 0, 0)
 
-    @pl.loop(0, 2 * PARTS - 1)
+    @pl.loop(0, 2 * PARTS - 1, unroll=True)
     def _(index):
         visit(*free_visit(index, edge), None)
 
@@ -332,10 +334,10 @@
     where = jnp.stack([lax.axis_index(name) for name in place_names]).astype(I32)
     width = GROUP * E
 
-    kv_own = jnp.broadcast_to(
-        jnp.concatenate([keys, values], axis=1)[None], (LINE, ROWS, 2 * E)
-    )
-    qg, seg = call(
+    kv_own = jnp.concatenate(
+        [jnp.broadcast_to(x[None], (LINE, ROWS, E)) for x in (keys, values)], axis=2
+    )
+    qg0, seg = call(
         pack_kernel,
         (shape((2, ROWS + 16, width), BF16), shape((8, E), F32)),
         scalars=1,
@@ -344,17 +346,19 @@
         where, queries, cotangent, owner_slot.reshape(1, ROWS),
         seg_lengths.reshape(1, E), seg_return.reshape(1, E),
     )
-    lane = iota((8, E), 1)
-    terms = jnp.where((lane >> 4) == head, jnp.tile(ref_term, 8)[None], 0.0)
-    terms = terms + far_swapped(terms)
-    kv_own, terms, qg = lax.optimization_barrier((kv_own, terms, qg))
+    from_far = far_swapped(ref_term)
+    lane = iota((8, E), 1) >> 4
+    terms = jnp.where(lane == head, jnp.tile(ref_term, 8)[None], 0.0)
+    terms = jnp.where(lane == (head ^ 1), jnp.tile(from_far, 8)[None], terms)
+    kv_own, terms, qg0 = lax.optimization_barrier((kv_own, terms, qg0))
     kv0 = lax.all_to_all(kv_own, ("quad", "pair"), 0, 0, tiled=True)
-    qg1, qg3 = from_ring(qg, 1), from_ring(qg, 3)
+    qg1, qg3 = from_ring(qg0, 1), from_ring(qg0, 3)
     terms = terms + swapped(terms, "near_col")
-    qg1, qg3, terms = lax.optimization_barrier((qg1, qg3, terms))
+    qg1, terms = lax.optimization_barrier((qg1, terms))
+    qg2 = from_ring(qg1, 1)
     terms = terms + swapped(terms, "far_col")
-    team = [qg, qg1, from_ring(qg1[0], 1), from_ring(qg3[1], 3), qg3]
-    kv0, terms, *team = lax.optimization_barrier((kv0, terms, *team))
+    kv0, terms, qg1, qg2, qg3 = lax.optimization_barrier((kv0, terms, qg1, qg2, qg3))
+    team = (qg0, qg1, qg2, qg3)
     kv1 = swapped(kv0, "core")
     table = lax.all_to_all(
         jnp.broadcast_to(terms[None], (2 * LINE, 8, E)), ("quad", "pair", "core"), 0, 0, tiled=True
@@ -366,10 +370,10 @@
         shape((8, COLS), F32),
         kv_scratch + [pltpu.VMEM((2, 8, COLS), F32)] * 3,
         scalars=1,
-        inputs=7,
+        inputs=6,
         cost=pl.CostEstimate(flops=4 * E * pairs, bytes_accessed=4 << 20, transcendentals=pairs),
     )(where, *team, kv0, kv1)
-    stat = call(lookup_kernel, shape((TEAM, 8, COLS), F32), scalars=1, inputs=8)(
+    stat = call(lookup_kernel, shape((TEAM, 8, COLS), F32), scalars=1, inputs=7)(
         where, *team, stat, table, seg
     )
     stats = lax.all_to_all(stat, "ring", 0, 0, tiled=True)
@@ -392,7 +396,7 @@
             pltpu.VMEM((HEAD_COLS, E), F32),
         ],
         scalars=1,
-        inputs=8,
+        inputs=7,
         cost=pl.CostEstimate(flops=10 * E * pairs, bytes_accessed=5 << 20, transcendentals=pairs),
     )(where, *team, kv0, kv1, stats)
 

time: 140 us -> 132 us (0.943)
  starting transfers between devices: 73.4 us -> 67.4 us
  Pallas kernels: 20.1 us -> 17.2 us
  waiting for transfers between devices: 29.9 us -> 31.8 us
    ppermute x7 -> x6, starting transfers between devices: 19.6 us -> 16.2 us  [from_ring(): lax.ppermute(x, 'ring', [(i, (i + step) % TEAM) for i in range(TEAM)])]
    ppermute x7 -> x6, waiting for transfers between devices: 15.1 us -> 17 us  [from_ring(): lax.ppermute(x, 'ring', [(i, (i + step) % TEAM) for i in range(TEAM)])]
    pallas_call x1, Pallas kernels: 11.5 us -> 9.99 us  [per_device(): call(backward_kernel, (shape(core_grad, F32), shape(core_grad, BF16), sha...]
    ppermute x5, waiting for transfers between devices: 11.9 us -> 10.5 us  [swapped(): return lax.ppermute(x, axis, [(0, 1), (1, 0)])]
  transfers between devices with their start and end apart: 16 -> 15, of which waited for: 9 -> 8; matrix products, arithmetic and copies ran while one was open for 2% -> 2% of each run, Pallas kernels for 6% -> 5%
where the time goes in v4:
time: 132 us; the launch traced here: 131 us
  starting transfers between devices  67.4 us (51%)
  waiting for transfers between devices  31.8 us (24%)
  Pallas kernels  17.2 us (13%)
  blocking collectives  7.54 us (6%)
  local copies, waits for them, and re-layouts  3.65 us (3%)
  other arithmetic  2.66 us (2%)
    ppermute x5, starting transfers between devices, swapped(): return lax.ppermute(x, axis, [(0, 1), (1, 0)])  19 us
    ppermute x6, waiting for transfers between devices, from_ring(): lax.ppermute(x, 'ring', [(i, (i + step) % TEAM) for i in range(TEAM)])  17 us
    ppermute x6, starting transfers between devices, from_ring(): lax.ppermute(x, 'ring', [(i, (i + step) % TEAM) for i in range(TEAM)])  16.2 us
    ppermute x1, starting transfers between devices, far_swapped(): return lax.ppermute(x, ('quad', 'far'), pairs)  13.3 us
    ppermute x5, waiting for transfers between devices, swapped(): return lax.ppermute(x, axis, [(0, 1), (1, 0)])  10.5 us
    pallas_call x1, Pallas kernels, per_device(): call(backward_kernel, (shape(core_grad, F32), shape(core_grad, BF16), sha...  9.99 us
    all_to_all x1, starting transfers between devices, per_device(): lax.all_to_all(jnp.broadcast_to(terms[None], (2 * LINE, 8, E)), ('quad',...  9.12 us
    all_to_all x1, blocking collectives, per_device(): stats = lax.all_to_all(stat, 'ring', 0, 0, tiled=True)  7.54 us
  transfers between devices with their start and end apart: 15, of which 8 were waited for; matrix products, arithmetic and copies ran while one was open for 2% of the time, Pallas kernels for 5%

profile of v4, /device:TPU:1, one launch (start us, length us, event | category | flops | bytes accessed | tf_op | source)
XLA Modules:
  0.0 131.2 jit_solution(5679900803653901891)
XLA Ops:
  0.6 13.3 %collective-permute-start = (f32[16]{0:T(128)}, f32[16]{0:T(128)S(1)}, u32[]{:S(2)}, u32[]{:S(2)}) collective-permute-start(f32[16]{0:T(128)} %param.15), channel_id=1, source_target_pairs={{0,257},{1,256},{128,385},{129,384},{256,1},{257,0},{384,129},{385... | collective-permute-start | bytes 200 | tf_op jit(solution)/shard_map/ppermute | solution.py:324
  14.8 0.7 copy-done.10
  15.5 0.9 pad_maximum_fusion
  17.2 0.7 shard_map.103
  18.0 5.9 %all-to-all-start = ((bf16[8,128,256]{2,1,0:T(8,128)(2,1)}), bf16[8,128,256]{2,1,0:T(8,128)(2,1)S(1)}, u32[]{:S(2)}, u32[]{:S(2)}) async-start(bf16[8,128,256]{2,1,0:T(8,128)(2,1)} %pad_maximum_fusion), calls=%async_computation | async-start | bytes 1048576 | tf_op jit(solution)/shard_map/all_to_all | solution.py:354
  23.9 3.2 %collective-permute-start.1 = (bf16[2,144,768]{2,1,0:T(8,128)(2,1)S(1)}, bf16[2,144,768]{2,1,0:T(8,128)(2,1)S(1)}, u32[]{:S(2)}, u32[]{:S(2)}) collective-permute-start(bf16[2,144,768]{2,1,0:T(8,128)(2,1)S(1)} %get-tuple-element.22.qg0_ref), channel_id=1, source_target_pairs={{0,16},{16,32},{32,48},{48,0},{1,17},{17,33},{33,49},{49,1},{2,18}... | collective-permute-start | bytes 1327112 | tf_op jit(solution)/shard_map/ppermute | solution.py:328
  27.1 3.1 %collective-permute-start.2 = (f32[8,128]{1,0:T(8,128)S(1)}, f32[8,128]{1,0:T(8,128)S(1)}, u32[]{:S(2)}, u32[]{:S(2)}) collective-permute-start(f32[8,128]{1,0:T(8,128)S(1)} %select_select_fusion), channel_id=1, source_target_pairs={{0,2},{2,0},{1,3},{3,1},{4,6},{6,4},{5,7},{7,5},{8,10},{10,8},{9,1... | collective-permute-start | bytes 12296 | tf_op jit(solution)/shard_map/ppermute | solution.py:319
  30.3 3.4 %collective-permute-start.5 = (bf16[2,144,768]{2,1,0:T(8,128)(2,1)S(1)}, bf16[2,144,768]{2,1,0:T(8,128)(2,1)S(1)}, u32[]{:S(2)}, u32[]{:S(2)}) collective-permute-start(bf16[2,144,768]{2,1,0:T(8,128)(2,1)S(1)} %get-tuple-element.22.qg0_ref), channel_id=1, source_target_pairs={{0,48},{16,0},{32,16},{48,32},{1,49},{17,1},{33,17},{49,33},{2,50}... | collective-permute-start | bytes 1327112 | tf_op jit(solution)/shard_map/ppermute | solution.py:328
  33.6 3.9 %collective-permute-done.1.qg1_ref = bf16[2,144,768]{2,1,0:T(8,128)(2,1)S(1)} collective-permute-done((bf16[2,144,768]{2,1,0:T(8,128)(2,1)S(1)}, bf16[2,144,768]{2,1,0:T(8,128)(2,1)S(1)}, u32[]{:S(2)}, u32[]{:S(2)}) %collective-permute-start.1) | collective-permute-done | bytes 442400 | tf_op jit(solution)/shard_map/ppermute | solution.py:328
  37.6 1.9 %collective-permute-start.4 = (bf16[2,144,768]{2,1,0:T(8,128)(2,1)S(1)}, bf16[2,144,768]{2,1,0:T(8,128)(2,1)S(1)}, u32[]{:S(2)}, u32[]{:S(2)}) collective-permute-start(bf16[2,144,768]{2,1,0:T(8,128)(2,1)S(1)} %collective-permute-done.1.qg1_ref), channel_id=1, source_target_pairs={{0,16},{16,32},{32,48},{48,0},{1,17},{17,33},{33,49},{49,1},{2,18}... | collective-permute-start | bytes 1327112 | tf_op jit(solution)/shard_map/ppermute | solution.py:328
  39.5 4.7 %collective-permute-start.3 = (f32[8,128]{1,0:T(8,128)S(1)}, f32[8,128]{1,0:T(8,128)S(1)}, u32[]{:S(2)}, u32[]{:S(2)}) collective-permute-start(f32[8,128]{1,0:T(8,128)S(1)} %add.33), channel_id=1, source_target_pairs={{0,4},{4,0},{1,5},{5,1},{2,6},{6,2},{3,7},{7,3},{8,12},{12,8},{9,1... | collective-permute-start | bytes 12296 | tf_op jit(solution)/shard_map/ppermute | solution.py:319
  44.2 1.5 %collective-permute-done.3 = f32[8,128]{1,0:T(8,128)S(1)} collective-permute-done((f32[8,128]{1,0:T(8,128)S(1)}, f32[8,128]{1,0:T(8,128)S(1)}, u32[]{:S(2)}, u32[]{:S(2)}) %collective-permute-start.3) | collective-permute-done | bytes 4128 | tf_op jit(solution)/shard_map/ppermute | solution.py:319
  45.7 4.6 %collective-permute-done.4.qg2_ref = bf16[2,144,768]{2,1,0:T(8,128)(2,1)S(1)} collective-permute-done((bf16[2,144,768]{2,1,0:T(8,128)(2,1)S(1)}, bf16[2,144,768]{2,1,0:T(8,128)(2,1)S(1)}, u32[]{:S(2)}, u32[]{:S(2)}) %collective-permute-start.4) | collective-permute-done | bytes 442400 | tf_op jit(solution)/shard_map/ppermute | solution.py:328
  50.2 5.3 %collective-permute-start.6 = (bf16[8,128,256]{2,1,0:T(8,128)(2,1)S(1)}, bf16[8,128,256]{2,1,0:T(8,128)(2,1)S(1)}, u32[]{:S(2)}, u32[]{:S(2)}) collective-permute-start(bf16[8,128,256]{2,1,0:T(8,128)(2,1)S(1)} %all-to-all-done.kv0_ref), channel_id=1, source_target_pairs={{0,8},{8,0},{1,9},{9,1},{2,10},{10,2},{3,11},{11,3},{4,12},{12,4},... | collective-permute-start | bytes 1572872 | tf_op jit(solution)/shard_map/ppermute | solution.py:319
  56.1 9.1 %all-to-all-start.1 = ((f32[16,8,128]{2,1,0:T(8,128)}), f32[16,8,128]{2,1,0:T(8,128)S(1)}, u32[]{:S(2)}, u32[]{:S(2)}) async-start(f32[16,8,128]{2,1,0:T(8,128)} %broadcast_in_dim.49), calls=%async_computation.1 | async-start | bytes 131072 | tf_op jit(solution)/shard_map/all_to_all | solution.py:363
  65.3 5.8 %shard_map.104.stat_ref = f32[8,1536]{1,0:T(8,128)S(1)} custom-call(s32[4]{0:T(128)S(1)} %pad_add_fusion.where_ref, bf16[2,144,768]{2,1,0:T(8,128)(2,1)S(1)} %get-tuple-element.22.qg0_ref, bf16[2,144,768]{2,1,0:T(8,128)(2,1)S(1)} %collective-permute-done.1.qg1_ref, bf16[2,144,768]{2,1,0:T(8,128)(2,1)S(1)} %collective-permute-done.4.qg2_ref, ...), custom_call_target="tpu_custom_call" | custom-call | flops 1811939328 | bytes 4194304 | tf_op jit(solution)/shard_map/pallas_call | solution.py:368
  71.1 4.3 %all-to-all-done.1.table_ref = f32[16,8,128]{2,1,0:T(8,128)S(1)} async-done(((f32[16,8,128]{2,1,0:T(8,128)}), f32[16,8,128]{2,1,0:T(8,128)S(1)}, u32[]{:S(2)}, u32[]{:S(2)}) %all-to-all-start.1) | async-done | bytes 65568 | tf_op jit(solution)/shard_map/all_to_all | solution.py:363
  75.3 0.8 shard_map.105
  76.1 7.5 %all_to_all.20.stat_ref = f32[4,8,1536]{2,1,0:T(8,128)S(1)} all-to-all(f32[4,8,1536]{2,1,0:T(8,128)S(1)} %shard_map.105), channel_id=1, replica_groups=mesh['quad'=4,'pair'=2,'ring'=4,'core'=2,'far_col'=2,'near_col'=2,'far'=..., dimensions={0} | all-to-all | bytes 393216 | tf_op jit(solution)/shard_map/all_to_all | solution.py:379
  83.7 10.0 %shard_map.106 = (f32[2,4,128,256]{3,2,1,0:T(8,128)S(1)}, bf16[2,4,128,256]{3,2,1,0:T(8,128)(2,1)S(1)}, f32[128,768]{1,0:T(8,128)S(1)}, bf16[128,768]{1,0:T(8,12...) custom-call(s32[4]{0:T(128)S(1)} %pad_add_fusion.where_ref, ...), custom_call_target="tpu_custom_call" | custom-call | flops 4529848320 | bytes 5242880 | tf_op jit(solution)/shard_map/pallas_call | solution.py:382
  93.7 4.1 %collective-permute-start.10 = (bf16[2,4,128,256]{3,2,1,0:T(8,128)(2,1)S(1)}, bf16[2,4,128,256]{3,2,1,0:T(8,128)(2,1)S(1)}, u32[]{:S(2)}, u32[]{:S(2)}) collective-permute-start(bf16[2,4,128,256]{3,2,1,0:T(8,128)(2,1)S(1)} %get-tuple-element.38), channel_id=1, source_target_pairs={{0,8},{8,0},{1,9},{9,1},{2,10},{10,2},{3,11},{11,3},{4,12},{12,4},... | collective-permute-start | bytes 1572872 | tf_op jit(solution)/shard_map/ppermute | solution.py:319
  97.8 1.5 %collective-permute-done.10 = bf16[2,4,128,256]{3,2,1,0:T(8,128)(2,1)S(1)} collective-permute-done((bf16[2,4,128,256]{3,2,1,0:T(8,128)(2,1)S(1)}, bf16[2,4,128,256]{3,2,1,0:T(8,128)(2,1)S(1)}, u32[]{:S(2)}, u32[]{:S(2)}) %collective-permute-start.10) | collective-permute-done | bytes 524320 | tf_op jit(solution)/shard_map/ppermute | solution.py:319
  99.5 1.9 %collective-permute-start.11 = (bf16[4,128,256]{2,1,0:T(8,128)(2,1)S(1)}, bf16[4,128,256]{2,1,0:T(8,128)(2,1)S(1)}, u32[]{:S(2)}, u32[]{:S(2)}) collective-permute-start(bf16[4,128,256]{2,1,0:T(8,128)(2,1)S(1)} %fusion.2), channel_id=1, source_target_pairs={{0,64},{64,0},{1,65},{65,1},{2,66},{66,2},{3,67},{67,3},{4,68},{68... | collective-permute-start | bytes 786440 | tf_op jit(solution)/shard_map/ppermute | solution.py:319
  101.4 7.5 %collective-permute-done.11 = bf16[4,128,256]{2,1,0:T(8,128)(2,1)S(1)} collective-permute-done((bf16[4,128,256]{2,1,0:T(8,128)(2,1)S(1)}, bf16[4,128,256]{2,1,0:T(8,128)(2,1)S(1)}, u32[]{:S(2)}, u32[]{:S(2)}) %collective-permute-start.11) | collective-permute-done | bytes 262176 | tf_op jit(solution)/shard_map/ppermute | solution.py:319
  108.9 0.8 fusion.1
  109.6 3.8 %all-to-all-start.3 = ((bf16[4,128,256]{2,1,0:T(8,128)(2,1)}), bf16[4,128,256]{2,1,0:T(8,128)(2,1)S(1)}, u32[]{:S(2)}, u32[]{:S(2)}) async-start(bf16[4,128,256]{2,1,0:T(8,128)(2,1)} %fusion.1), calls=%async_computation.3 | async-start | bytes 524288 | tf_op jit(solution)/shard_map/all_to_all | solution.py:405
  113.5 2.8 %collective-permute-start.7 = (bf16[128,768]{1,0:T(8,128)(2,1)S(1)}, bf16[128,768]{1,0:T(8,128)(2,1)S(1)}, u32[]{:S(2)}, u32[]{:S(2)}) collective-permute-start(bf16[128,768]{1,0:T(8,128)(2,1)S(1)} %copy-done.8), channel_id=1, source_target_pairs={{0,48},{16,0},{32,16},{48,32},{1,49},{17,1},{33,17},{49,33},{2,50}... | collective-permute-start | bytes 589832 | tf_op jit(solution)/shard_map/ppermute | solution.py:328
  116.3 3.1 %collective-permute-start.8 = (bf16[128,768]{1,0:T(8,128)(2,1)S(1)}, bf16[128,768]{1,0:T(8,128)(2,1)S(1)}, u32[]{:S(2)}, u32[]{:S(2)}) collective-permute-start(bf16[128,768]{1,0:T(8,128)(2,1)S(1)} %copy-done.6), channel_id=1, source_target_pairs={{0,32},{16,48},{32,0},{48,16},{1,33},{17,49},{33,1},{49,17},{2,34}... | collective-permute-start | bytes 589832 | tf_op jit(solution)/shard_map/ppermute | solution.py:328
  119.4 1.9 %collective-permute-start.9 = (bf16[128,768]{1,0:T(8,128)(2,1)S(1)}, bf16[128,768]{1,0:T(8,128)(2,1)S(1)}, u32[]{:S(2)}, u32[]{:S(2)}) collective-permute-start(bf16[128,768]{1,0:T(8,128)(2,1)S(1)} %get-tuple-element.36), channel_id=1, source_target_pairs={{0,16},{16,32},{32,48},{48,0},{1,17},{17,33},{33,49},{49,1},{2,18}... | collective-permute-start | bytes 589832 | tf_op jit(solution)/shard_map/ppermute | solution.py:328
  121.3 2.9 %collective-permute-done.8 = bf16[128,768]{1,0:T(8,128)(2,1)S(1)} collective-permute-done((bf16[128,768]{1,0:T(8,128)(2,1)S(1)}, bf16[128,768]{1,0:T(8,128)(2,1)S(1)}, u32[]{:S(2)}, u32[]{:S(2)}) %collective-permute-start.8) | collective-permute-done | bytes 196640 | tf_op jit(solution)/shard_map/ppermute | solution.py:328
  124.2 5.6 %collective-permute-done.9 = bf16[128,768]{1,0:T(8,128)(2,1)S(1)} collective-permute-done((bf16[128,768]{1,0:T(8,128)(2,1)S(1)}, bf16[128,768]{1,0:T(8,128)(2,1)S(1)}, u32[]{:S(2)}, u32[]{:S(2)}) %collective-permute-start.9) | collective-permute-done | bytes 196640 | tf_op jit(solution)/shard_map/ppermute | solution.py:328
  129.7 0.8 add_convert_fusion
  (46 shorter events, 3.2 us)
Async XLA Ops:
  0.6 14.1 %copy-start.9 = (bf16[128,128]{1,0:T(8,128)(2,1)S(1)}, bf16[128,128]{1,0:T(8,128)(2,1)}, u32[]{:S(2)}) copy-start(bf16[128,128]{1,0:T(8,128)(2,1)} %param.9) | copy-start | bytes 98308
  0.6 17.3 %collective-permute-start = (f32[16]{0:T(128)}, f32[16]{0:T(128)S(1)}, u32[]{:S(2)}, u32[]{:S(2)}) collective-permute-start(f32[16]{0:T(128)} %param.15), channel_id=1, source_target_pairs={{0,257},{1,256},{128,385},{129,384},{256,1},{257,0},{384,129},{385... | collective-permute-start | bytes 200 | tf_op jit(solution)/shard_map/ppermute | solution.py:324
  13.9 0.7 copy-start.11
  14.7 0.8 copy-start.10
  15.5 1.0 copy-start
  15.5 1.2 copy-start.1
  16.5 0.7 copy-start.2
  16.5 0.7 copy-start.3
  16.5 0.7 copy-start.4
  18.0 32.2 %all-to-all-start = ((bf16[8,128,256]{2,1,0:T(8,128)(2,1)}), bf16[8,128,256]{2,1,0:T(8,128)(2,1)S(1)}, u32[]{:S(2)}, u32[]{:S(2)}) async-start(bf16[8,128,256]{2,1,0:T(8,128)(2,1)} %pad_maximum_fusion), calls=%async_computation | async-start | bytes 1048576 | tf_op jit(solution)/shard_map/all_to_all | solution.py:354
  23.9 13.7 %collective-permute-start.1 = (bf16[2,144,768]{2,1,0:T(8,128)(2,1)S(1)}, bf16[2,144,768]{2,1,0:T(8,128)(2,1)S(1)}, u32[]{:S(2)}, u32[]{:S(2)}) collective-permute-start(bf16[2,144,768]{2,1,0:T(8,128)(2,1)S(1)} %get-tuple-element.22.qg0_ref), channel_id=1, source_target_pairs={{0,16},{16,32},{32,48},{48,0},{1,17},{17,33},{33,49},{49,1},{2,18}... | collective-permute-start | bytes 1327112 | tf_op jit(solution)/shard_map/ppermute | solution.py:328
  27.1 6.5 %collective-permute-start.2 = (f32[8,128]{1,0:T(8,128)S(1)}, f32[8,128]{1,0:T(8,128)S(1)}, u32[]{:S(2)}, u32[]{:S(2)}) collective-permute-start(f32[8,128]{1,0:T(8,128)S(1)} %select_select_fusion), channel_id=1, source_target_pairs={{0,2},{2,0},{1,3},{3,1},{4,6},{6,4},{5,7},{7,5},{8,10},{10,8},{9,1... | collective-permute-start | bytes 12296 | tf_op jit(solution)/shard_map/ppermute | solution.py:319
  30.3 15.4 %collective-permute-start.5 = (bf16[2,144,768]{2,1,0:T(8,128)(2,1)S(1)}, bf16[2,144,768]{2,1,0:T(8,128)(2,1)S(1)}, u32[]{:S(2)}, u32[]{:S(2)}) collective-permute-start(bf16[2,144,768]{2,1,0:T(8,128)(2,1)S(1)} %get-tuple-element.22.qg0_ref), channel_id=1, source_target_pairs={{0,48},{16,0},{32,16},{48,32},{1,49},{17,1},{33,17},{49,33},{2,50}... | collective-permute-start | bytes 1327112 | tf_op jit(solution)/shard_map/ppermute | solution.py:328
  37.6 12.7 %collective-permute-start.4 = (bf16[2,144,768]{2,1,0:T(8,128)(2,1)S(1)}, bf16[2,144,768]{2,1,0:T(8,128)(2,1)S(1)}, u32[]{:S(2)}, u32[]{:S(2)}) collective-permute-start(bf16[2,144,768]{2,1,0:T(8,128)(2,1)S(1)} %collective-permute-done.1.qg1_ref), channel_id=1, source_target_pairs={{0,16},{16,32},{32,48},{48,0},{1,17},{17,33},{33,49},{49,1},{2,18}... | collective-permute-start | bytes 1327112 | tf_op jit(solution)/shard_map/ppermute | solution.py:328
  39.5 6.2 %collective-permute-start.3 = (f32[8,128]{1,0:T(8,128)S(1)}, f32[8,128]{1,0:T(8,128)S(1)}, u32[]{:S(2)}, u32[]{:S(2)}) collective-permute-start(f32[8,128]{1,0:T(8,128)S(1)} %add.33), channel_id=1, source_target_pairs={{0,4},{4,0},{1,5},{5,1},{2,6},{6,2},{3,7},{7,3},{8,12},{12,8},{9,1... | collective-permute-start | bytes 12296 | tf_op jit(solution)/shard_map/ppermute | solution.py:319
  50.2 15.0 %collective-permute-start.6 = (bf16[8,128,256]{2,1,0:T(8,128)(2,1)S(1)}, bf16[8,128,256]{2,1,0:T(8,128)(2,1)S(1)}, u32[]{:S(2)}, u32[]{:S(2)}) collective-permute-start(bf16[8,128,256]{2,1,0:T(8,128)(2,1)S(1)} %all-to-all-done.kv0_ref), channel_id=1, source_target_pairs={{0,8},{8,0},{1,9},{9,1},{2,10},{10,2},{3,11},{11,3},{4,12},{12,4},... | collective-permute-start | bytes 1572872 | tf_op jit(solution)/shard_map/ppermute | solution.py:319
  56.1 19.2 %all-to-all-start.1 = ((f32[16,8,128]{2,1,0:T(8,128)}), f32[16,8,128]{2,1,0:T(8,128)S(1)}, u32[]{:S(2)}, u32[]{:S(2)}) async-start(f32[16,8,128]{2,1,0:T(8,128)} %broadcast_in_dim.49), calls=%async_computation.1 | async-start | bytes 131072 | tf_op jit(solution)/shard_map/all_to_all | solution.py:363
  93.7 5.7 %copy-start.5 = (bf16[128,768]{1,0:T(8,128)(2,1)}, bf16[128,768]{1,0:T(8,128)(2,1)S(1)}, u32[]{:S(2)}) copy-start(bf16[128,768]{1,0:T(8,128)(2,1)S(1)} %get-tuple-element.35) | copy-start | bytes 589828
  93.7 5.7 %copy-start.7 = (bf16[128,768]{1,0:T(8,128)(2,1)}, bf16[128,768]{1,0:T(8,128)(2,1)S(1)}, u32[]{:S(2)}) copy-start(bf16[128,768]{1,0:T(8,128)(2,1)S(1)} %get-tuple-element.34) | copy-start | bytes 589828
  93.7 5.6 %collective-permute-start.10 = (bf16[2,4,128,256]{3,2,1,0:T(8,128)(2,1)S(1)}, bf16[2,4,128,256]{3,2,1,0:T(8,128)(2,1)S(1)}, u32[]{:S(2)}, u32[]{:S(2)}) collective-permute-start(bf16[2,4,128,256]{3,2,1,0:T(8,128)(2,1)S(1)} %get-tuple-element.38), channel_id=1, source_target_pairs={{0,8},{8,0},{1,9},{9,1},{2,10},{10,2},{3,11},{11,3},{4,12},{12,4},... | collective-permute-start | bytes 1572872 | tf_op jit(solution)/shard_map/ppermute | solution.py:319
  99.5 9.4 %collective-permute-start.11 = (bf16[4,128,256]{2,1,0:T(8,128)(2,1)S(1)}, bf16[4,128,256]{2,1,0:T(8,128)(2,1)S(1)}, u32[]{:S(2)}, u32[]{:S(2)}) collective-permute-start(bf16[4,128,256]{2,1,0:T(8,128)(2,1)S(1)} %fusion.2), channel_id=1, source_target_pairs={{0,64},{64,0},{1,65},{65,1},{2,66},{66,2},{3,67},{67,3},{4,68},{68... | collective-permute-start | bytes 786440 | tf_op jit(solution)/shard_map/ppermute | solution.py:319
  109.6 3.8 %copy-start.8 = (bf16[128,768]{1,0:T(8,128)(2,1)S(1)}, bf16[128,768]{1,0:T(8,128)(2,1)}, u32[]{:S(2)}) copy-start(bf16[128,768]{1,0:T(8,128)(2,1)} %copy-done.7) | copy-start | bytes 589828
  109.6 6.6 %copy-start.6 = (bf16[128,768]{1,0:T(8,128)(2,1)S(1)}, bf16[128,768]{1,0:T(8,128)(2,1)}, u32[]{:S(2)}) copy-start(bf16[128,768]{1,0:T(8,128)(2,1)} %copy-done.5) | copy-start | bytes 589828
  109.6 20.9 %all-to-all-start.3 = ((bf16[4,128,256]{2,1,0:T(8,128)(2,1)}), bf16[4,128,256]{2,1,0:T(8,128)(2,1)S(1)}, u32[]{:S(2)}, u32[]{:S(2)}) async-start(bf16[4,128,256]{2,1,0:T(8,128)(2,1)} %fusion.1), calls=%async_computation.3 | async-start | bytes 524288 | tf_op jit(solution)/shard_map/all_to_all | solution.py:405
  113.5 7.8 %collective-permute-start.7 = (bf16[128,768]{1,0:T(8,128)(2,1)S(1)}, bf16[128,768]{1,0:T(8,128)(2,1)S(1)}, u32[]{:S(2)}, u32[]{:S(2)}) collective-permute-start(bf16[128,768]{1,0:T(8,128)(2,1)S(1)} %copy-done.8), channel_id=1, source_target_pairs={{0,48},{16,0},{32,16},{48,32},{1,49},{17,1},{33,17},{49,33},{2,50}... | collective-permute-start | bytes 589832 | tf_op jit(solution)/shard_map/ppermute | solution.py:328
  116.3 7.9 %collective-permute-start.8 = (bf16[128,768]{1,0:T(8,128)(2,1)S(1)}, bf16[128,768]{1,0:T(8,128)(2,1)S(1)}, u32[]{:S(2)}, u32[]{:S(2)}) collective-permute-start(bf16[128,768]{1,0:T(8,128)(2,1)S(1)} %copy-done.6), channel_id=1, source_target_pairs={{0,32},{16,48},{32,0},{48,16},{1,33},{17,49},{33,1},{49,17},{2,34}... | collective-permute-start | bytes 589832 | tf_op jit(solution)/shard_map/ppermute | solution.py:328
  119.4 10.4 %collective-permute-start.9 = (bf16[128,768]{1,0:T(8,128)(2,1)S(1)}, bf16[128,768]{1,0:T(8,128)(2,1)S(1)}, u32[]{:S(2)}, u32[]{:S(2)}) collective-permute-start(bf16[128,768]{1,0:T(8,128)(2,1)S(1)} %get-tuple-element.36), channel_id=1, source_target_pairs={{0,16},{16,32},{32,48},{48,0},{1,17},{17,33},{33,49},{49,1},{2,18}... | collective-permute-start | bytes 589832 | tf_op jit(solution)/shard_map/ppermute | solution.py:328

commit v5 on v4

--- a/solution.py
+++ b/solution.py
@@ -347,10 +347,10 @@
         seg_lengths.reshape(1, E), seg_return.reshape(1, E),
     )
     from_far = far_swapped(ref_term)
+    kv_own, from_far = lax.optimization_barrier((kv_own, from_far))
     lane = iota((8, E), 1) >> 4
     terms = jnp.where(lane == head, jnp.tile(ref_term, 8)[None], 0.0)
     terms = jnp.where(lane == (head ^ 1), jnp.tile(from_far, 8)[None], terms)
-    kv_own, terms, qg0 = lax.optimization_barrier((kv_own, terms, qg0))
     kv0 = lax.all_to_all(kv_own, ("quad", "pair"), 0, 0, tiled=True)
     qg1, qg3 = from_ring(qg0, 1), from_ring(qg0, 3)
     terms = terms + swapped(terms, "near_col")

time: 132 us -> 131 us (level)
  waiting for transfers between devices: 31.8 us -> 29.2 us
    ppermute x6, waiting for transfers between devices: 17 us -> 14.4 us  [from_ring(): lax.ppermute(x, 'ring', [(i, (i + step) % TEAM) for i in range(TEAM)])]
  transfers between devices with their start and end apart: 15 -> 15, of which waited for: 8 -> 8; matrix products, arithmetic and copies ran while one was open for 2% -> 3% of each run, Pallas kernels for 5% -> 5%
where the time goes in v5:
time: 131 us; the launch traced here: 130 us
  starting transfers between devices  68.7 us (52%)
  waiting for transfers between devices  29.2 us (22%)
  Pallas kernels  17.2 us (13%)
  blocking collectives  7.54 us (6%)
  local copies, waits for them, and re-layouts  3.63 us (3%)
  other arithmetic  2.68 us (2%)
    ppermute x5, starting transfers between devices, swapped(): return lax.ppermute(x, axis, [(0, 1), (1, 0)])  19.5 us
    ppermute x6, starting transfers between devices, from_ring(): lax.ppermute(x, 'ring', [(i, (i + step) % TEAM) for i in range(TEAM)])  16.3 us
    ppermute x6, waiting for transfers between devices, from_ring(): lax.ppermute(x, 'ring', [(i, (i + step) % TEAM) for i in range(TEAM)])  14.4 us
    ppermute x1, starting transfers between devices, far_swapped(): return lax.ppermute(x, ('quad', 'far'), pairs)  13.3 us
    ppermute x5, waiting for transfers between devices, swapped(): return lax.ppermute(x, axis, [(0, 1), (1, 0)])  10.5 us
    pallas_call x1, Pallas kernels, per_device(): call(backward_kernel, (shape(core_grad, F32), shape(core_grad, BF16), sha...  10 us
    all_to_all x1, starting transfers between devices, per_device(): lax.all_to_all(jnp.broadcast_to(terms[None], (2 * LINE, 8, E)), ('quad',...  9.47 us
    all_to_all x1, blocking collectives, per_device(): stats = lax.all_to_all(stat, 'ring', 0, 0, tiled=True)  7.54 us
  transfers between devices with their start and end apart: 15, of which 8 were waited for; matrix products, arithmetic and copies ran while one was open for 3% of the time, Pallas kernels for 5%

profile of v5, /device:TPU:1, one launch (start us, length us, event | category | flops | bytes accessed | tf_op | source)
XLA Modules:
  0.0 129.9 jit_solution(14111501708823705531)
XLA Ops:
  0.6 13.3 %collective-permute-start = (f32[16]{0:T(128)}, f32[16]{0:T(128)S(1)}, u32[]{:S(2)}, u32[]{:S(2)}) collective-permute-start(f32[16]{0:T(128)} %param.15), channel_id=1, source_target_pairs={{0,257},{1,256},{128,385},{129,384},{256,1},{257,0},{384,129},{385... | collective-permute-start | bytes 200 | tf_op jit(solution)/shard_map/ppermute | solution.py:324
  13.9 0.8 broadcast_in_dim.42
  14.8 0.9 pad_maximum_fusion
  15.7 6.4 %all-to-all-start = ((bf16[8,128,256]{2,1,0:T(8,128)(2,1)}), bf16[8,128,256]{2,1,0:T(8,128)(2,1)S(1)}, u32[]{:S(2)}, u32[]{:S(2)}) async-start(bf16[8,128,256]{2,1,0:T(8,128)(2,1)} %pad_maximum_fusion), calls=%async_computation | async-start | bytes 1048576 | tf_op jit(solution)/shard_map/all_to_all | solution.py:354
  22.8 0.7 shard_map.103
  23.5 3.2 %collective-permute-start.1 = (bf16[2,144,768]{2,1,0:T(8,128)(2,1)S(1)}, bf16[2,144,768]{2,1,0:T(8,128)(2,1)S(1)}, u32[]{:S(2)}, u32[]{:S(2)}) collective-permute-start(bf16[2,144,768]{2,1,0:T(8,128)(2,1)S(1)} %get-tuple-element.20.qg0_ref), channel_id=1, source_target_pairs={{0,16},{16,32},{32,48},{48,0},{1,17},{17,33},{33,49},{49,1},{2,18}... | collective-permute-start | bytes 1327112 | tf_op jit(solution)/shard_map/ppermute | solution.py:328
  27.6 3.1 %collective-permute-start.2 = (f32[8,128]{1,0:T(8,128)S(1)}, f32[8,128]{1,0:T(8,128)S(1)}, u32[]{:S(2)}, u32[]{:S(2)}) collective-permute-start(f32[8,128]{1,0:T(8,128)S(1)} %select_select_fusion), channel_id=1, source_target_pairs={{0,2},{2,0},{1,3},{3,1},{4,6},{6,4},{5,7},{7,5},{8,10},{10,8},{9,1... | collective-permute-start | bytes 12296 | tf_op jit(solution)/shard_map/ppermute | solution.py:319
  30.7 3.4 %collective-permute-start.5 = (bf16[2,144,768]{2,1,0:T(8,128)(2,1)S(1)}, bf16[2,144,768]{2,1,0:T(8,128)(2,1)S(1)}, u32[]{:S(2)}, u32[]{:S(2)}) collective-permute-start(bf16[2,144,768]{2,1,0:T(8,128)(2,1)S(1)} %get-tuple-element.20.qg0_ref), channel_id=1, source_target_pairs={{0,48},{16,0},{32,16},{48,32},{1,49},{17,1},{33,17},{49,33},{2,50}... | collective-permute-start | bytes 1327112 | tf_op jit(solution)/shard_map/ppermute | solution.py:328
  34.1 2.2 %collective-permute-done.1.qg1_ref = bf16[2,144,768]{2,1,0:T(8,128)(2,1)S(1)} collective-permute-done((bf16[2,144,768]{2,1,0:T(8,128)(2,1)S(1)}, bf16[2,144,768]{2,1,0:T(8,128)(2,1)S(1)}, u32[]{:S(2)}, u32[]{:S(2)}) %collective-permute-start.1) | collective-permute-done | bytes 442400 | tf_op jit(solution)/shard_map/ppermute | solution.py:328
  36.3 1.9 %collective-permute-start.4 = (bf16[2,144,768]{2,1,0:T(8,128)(2,1)S(1)}, bf16[2,144,768]{2,1,0:T(8,128)(2,1)S(1)}, u32[]{:S(2)}, u32[]{:S(2)}) collective-permute-start(bf16[2,144,768]{2,1,0:T(8,128)(2,1)S(1)} %collective-permute-done.1.qg1_ref), channel_id=1, source_target_pairs={{0,16},{16,32},{32,48},{48,0},{1,17},{17,33},{33,49},{49,1},{2,18}... | collective-permute-start | bytes 1327112 | tf_op jit(solution)/shard_map/ppermute | solution.py:328
  38.2 4.7 %collective-permute-start.3 = (f32[8,128]{1,0:T(8,128)S(1)}, f32[8,128]{1,0:T(8,128)S(1)}, u32[]{:S(2)}, u32[]{:S(2)}) collective-permute-start(f32[8,128]{1,0:T(8,128)S(1)} %fusion.5), channel_id=1, source_target_pairs={{0,4},{4,0},{1,5},{5,1},{2,6},{6,2},{3,7},{7,3},{8,12},{12,8},{9,1... | collective-permute-start | bytes 12296 | tf_op jit(solution)/shard_map/ppermute | solution.py:319
  42.9 1.5 %collective-permute-done.3 = f32[8,128]{1,0:T(8,128)S(1)} collective-permute-done((f32[8,128]{1,0:T(8,128)S(1)}, f32[8,128]{1,0:T(8,128)S(1)}, u32[]{:S(2)}, u32[]{:S(2)}) %collective-permute-start.3) | collective-permute-done | bytes 4128 | tf_op jit(solution)/shard_map/ppermute | solution.py:319
  44.4 3.7 %collective-permute-done.4.qg2_ref = bf16[2,144,768]{2,1,0:T(8,128)(2,1)S(1)} collective-permute-done((bf16[2,144,768]{2,1,0:T(8,128)(2,1)S(1)}, bf16[2,144,768]{2,1,0:T(8,128)(2,1)S(1)}, u32[]{:S(2)}, u32[]{:S(2)}) %collective-permute-start.4) | collective-permute-done | bytes 442400 | tf_op jit(solution)/shard_map/ppermute | solution.py:328
  48.1 5.8 %collective-permute-start.6 = (bf16[8,128,256]{2,1,0:T(8,128)(2,1)S(1)}, bf16[8,128,256]{2,1,0:T(8,128)(2,1)S(1)}, u32[]{:S(2)}, u32[]{:S(2)}) collective-permute-start(bf16[8,128,256]{2,1,0:T(8,128)(2,1)S(1)} %all-to-all-done.kv0_ref), channel_id=1, source_target_pairs={{0,8},{8,0},{1,9},{9,1},{2,10},{10,2},{3,11},{11,3},{4,12},{12,4},... | collective-permute-start | bytes 1572872 | tf_op jit(solution)/shard_map/ppermute | solution.py:319
  54.5 9.5 %all-to-all-start.1 = ((f32[16,8,128]{2,1,0:T(8,128)}), f32[16,8,128]{2,1,0:T(8,128)S(1)}, u32[]{:S(2)}, u32[]{:S(2)}) async-start(f32[16,8,128]{2,1,0:T(8,128)} %broadcast_in_dim.49), calls=%async_computation.1 | async-start | bytes 131072 | tf_op jit(solution)/shard_map/all_to_all | solution.py:363
  64.0 5.8 %shard_map.104.stat_ref = f32[8,1536]{1,0:T(8,128)S(1)} custom-call(s32[4]{0:T(128)S(1)} %pad_add_fusion.where_ref, bf16[2,144,768]{2,1,0:T(8,128)(2,1)S(1)} %get-tuple-element.20.qg0_ref, bf16[2,144,768]{2,1,0:T(8,128)(2,1)S(1)} %collective-permute-done.1.qg1_ref, bf16[2,144,768]{2,1,0:T(8,128)(2,1)S(1)} %collective-permute-done.4.qg2_ref, ...), custom_call_target="tpu_custom_call" | custom-call | flops 1811939328 | bytes 4194304 | tf_op jit(solution)/shard_map/pallas_call | solution.py:368
  69.8 4.3 %all-to-all-done.1.table_ref = f32[16,8,128]{2,1,0:T(8,128)S(1)} async-done(((f32[16,8,128]{2,1,0:T(8,128)}), f32[16,8,128]{2,1,0:T(8,128)S(1)}, u32[]{:S(2)}, u32[]{:S(2)}) %all-to-all-start.1) | async-done | bytes 65568 | tf_op jit(solution)/shard_map/all_to_all | solution.py:363
  74.1 0.8 shard_map.105
  74.8 7.5 %all_to_all.20.stat_ref = f32[4,8,1536]{2,1,0:T(8,128)S(1)} all-to-all(f32[4,8,1536]{2,1,0:T(8,128)S(1)} %shard_map.105), channel_id=1, replica_groups=mesh['quad'=4,'pair'=2,'ring'=4,'core'=2,'far_col'=2,'near_col'=2,'far'=..., dimensions={0} | all-to-all | bytes 393216 | tf_op jit(solution)/shard_map/all_to_all | solution.py:379
  82.4 10.0 %shard_map.106 = (f32[2,4,128,256]{3,2,1,0:T(8,128)S(1)}, bf16[2,4,128,256]{3,2,1,0:T(8,128)(2,1)S(1)}, f32[128,768]{1,0:T(8,128)S(1)}, bf16[128,768]{1,0:T(8,12...) custom-call(s32[4]{0:T(128)S(1)} %pad_add_fusion.where_ref, ...), custom_call_target="tpu_custom_call" | custom-call | flops 4529848320 | bytes 5242880 | tf_op jit(solution)/shard_map/pallas_call | solution.py:382
  92.4 4.0 %collective-permute-start.10 = (bf16[2,4,128,256]{3,2,1,0:T(8,128)(2,1)S(1)}, bf16[2,4,128,256]{3,2,1,0:T(8,128)(2,1)S(1)}, u32[]{:S(2)}, u32[]{:S(2)}) collective-permute-start(bf16[2,4,128,256]{3,2,1,0:T(8,128)(2,1)S(1)} %get-tuple-element.36), channel_id=1, source_target_pairs={{0,8},{8,0},{1,9},{9,1},{2,10},{10,2},{3,11},{11,3},{4,12},{12,4},... | collective-permute-start | bytes 1572872 | tf_op jit(solution)/shard_map/ppermute | solution.py:319
  96.5 1.5 %collective-permute-done.10 = bf16[2,4,128,256]{3,2,1,0:T(8,128)(2,1)S(1)} collective-permute-done((bf16[2,4,128,256]{3,2,1,0:T(8,128)(2,1)S(1)}, bf16[2,4,128,256]{3,2,1,0:T(8,128)(2,1)S(1)}, u32[]{:S(2)}, u32[]{:S(2)}) %collective-permute-start.10) | collective-permute-done | bytes 524320 | tf_op jit(solution)/shard_map/ppermute | solution.py:319
  98.2 1.9 %collective-permute-start.11 = (bf16[4,128,256]{2,1,0:T(8,128)(2,1)S(1)}, bf16[4,128,256]{2,1,0:T(8,128)(2,1)S(1)}, u32[]{:S(2)}, u32[]{:S(2)}) collective-permute-start(bf16[4,128,256]{2,1,0:T(8,128)(2,1)S(1)} %fusion.2), channel_id=1, source_target_pairs={{0,64},{64,0},{1,65},{65,1},{2,66},{66,2},{3,67},{67,3},{4,68},{68... | collective-permute-start | bytes 786440 | tf_op jit(solution)/shard_map/ppermute | solution.py:319
  100.1 7.5 %collective-permute-done.11 = bf16[4,128,256]{2,1,0:T(8,128)(2,1)S(1)} collective-permute-done((bf16[4,128,256]{2,1,0:T(8,128)(2,1)S(1)}, bf16[4,128,256]{2,1,0:T(8,128)(2,1)S(1)}, u32[]{:S(2)}, u32[]{:S(2)}) %collective-permute-start.11) | collective-permute-done | bytes 262176 | tf_op jit(solution)/shard_map/ppermute | solution.py:319
  107.6 0.8 fusion.1
  108.4 3.8 %all-to-all-start.3 = ((bf16[4,128,256]{2,1,0:T(8,128)(2,1)}), bf16[4,128,256]{2,1,0:T(8,128)(2,1)S(1)}, u32[]{:S(2)}, u32[]{:S(2)}) async-start(bf16[4,128,256]{2,1,0:T(8,128)(2,1)} %fusion.1), calls=%async_computation.3 | async-start | bytes 524288 | tf_op jit(solution)/shard_map/all_to_all | solution.py:405
  112.2 2.8 %collective-permute-start.7 = (bf16[128,768]{1,0:T(8,128)(2,1)S(1)}, bf16[128,768]{1,0:T(8,128)(2,1)S(1)}, u32[]{:S(2)}, u32[]{:S(2)}) collective-permute-start(bf16[128,768]{1,0:T(8,128)(2,1)S(1)} %copy-done.8), channel_id=1, source_target_pairs={{0,48},{16,0},{32,16},{48,32},{1,49},{17,1},{33,17},{49,33},{2,50}... | collective-permute-start | bytes 589832 | tf_op jit(solution)/shard_map/ppermute | solution.py:328
  115.0 3.1 %collective-permute-start.8 = (bf16[128,768]{1,0:T(8,128)(2,1)S(1)}, bf16[128,768]{1,0:T(8,128)(2,1)S(1)}, u32[]{:S(2)}, u32[]{:S(2)}) collective-permute-start(bf16[128,768]{1,0:T(8,128)(2,1)S(1)} %copy-done.6), channel_id=1, source_target_pairs={{0,32},{16,48},{32,0},{48,16},{1,33},{17,49},{33,1},{49,17},{2,34}... | collective-permute-start | bytes 589832 | tf_op jit(solution)/shard_map/ppermute | solution.py:328
  118.1 1.9 %collective-permute-start.9 = (bf16[128,768]{1,0:T(8,128)(2,1)S(1)}, bf16[128,768]{1,0:T(8,128)(2,1)S(1)}, u32[]{:S(2)}, u32[]{:S(2)}) collective-permute-start(bf16[128,768]{1,0:T(8,128)(2,1)S(1)} %get-tuple-element.34), channel_id=1, source_target_pairs={{0,16},{16,32},{32,48},{48,0},{1,17},{17,33},{33,49},{49,1},{2,18}... | collective-permute-start | bytes 589832 | tf_op jit(solution)/shard_map/ppermute | solution.py:328
  120.0 2.9 %collective-permute-done.8 = bf16[128,768]{1,0:T(8,128)(2,1)S(1)} collective-permute-done((bf16[128,768]{1,0:T(8,128)(2,1)S(1)}, bf16[128,768]{1,0:T(8,128)(2,1)S(1)}, u32[]{:S(2)}, u32[]{:S(2)}) %collective-permute-start.8) | collective-permute-done | bytes 196640 | tf_op jit(solution)/shard_map/ppermute | solution.py:328
  122.9 5.6 %collective-permute-done.9 = bf16[128,768]{1,0:T(8,128)(2,1)S(1)} collective-permute-done((bf16[128,768]{1,0:T(8,128)(2,1)S(1)}, bf16[128,768]{1,0:T(8,128)(2,1)S(1)}, u32[]{:S(2)}, u32[]{:S(2)}) %collective-permute-start.9) | collective-permute-done | bytes 196640 | tf_op jit(solution)/shard_map/ppermute | solution.py:328
  128.5 0.8 add_convert_fusion
  (44 shorter events, 3.1 us)
Async XLA Ops:
  0.6 14.1 %copy-start.9 = (bf16[128,128]{1,0:T(8,128)(2,1)S(1)}, bf16[128,128]{1,0:T(8,128)(2,1)}, u32[]{:S(2)}) copy-start(bf16[128,128]{1,0:T(8,128)(2,1)} %param.10) | copy-start | bytes 98308
  0.6 15.0 %collective-permute-start = (f32[16]{0:T(128)}, f32[16]{0:T(128)S(1)}, u32[]{:S(2)}, u32[]{:S(2)}) collective-permute-start(f32[16]{0:T(128)} %param.15), channel_id=1, source_target_pairs={{0,257},{1,256},{128,385},{129,384},{256,1},{257,0},{384,129},{385... | collective-permute-start | bytes 200 | tf_op jit(solution)/shard_map/ppermute | solution.py:324
  15.7 6.5 %copy-start = (bf16[128,768]{1,0:T(8,128)(2,1)S(1)}, bf16[128,768]{1,0:T(8,128)(2,1)}, u32[]{:S(2)}) copy-start(bf16[128,768]{1,0:T(8,128)(2,1)} %q_ref.1) | copy-start | bytes 589828
  15.7 6.5 %copy-start.1 = (bf16[128,768]{1,0:T(8,128)(2,1)S(1)}, bf16[128,768]{1,0:T(8,128)(2,1)}, u32[]{:S(2)}) copy-start(bf16[128,768]{1,0:T(8,128)(2,1)} %g_ref.1) | copy-start | bytes 589828
  15.7 32.4 %all-to-all-start = ((bf16[8,128,256]{2,1,0:T(8,128)(2,1)}), bf16[8,128,256]{2,1,0:T(8,128)(2,1)S(1)}, u32[]{:S(2)}, u32[]{:S(2)}) async-start(bf16[8,128,256]{2,1,0:T(8,128)(2,1)} %pad_maximum_fusion), calls=%async_computation | async-start | bytes 1048576 | tf_op jit(solution)/shard_map/all_to_all | solution.py:354
  22.1 0.7 copy-start.2
  22.1 0.7 copy-start.3
  22.1 0.7 copy-start.4
  23.5 12.8 %collective-permute-start.1 = (bf16[2,144,768]{2,1,0:T(8,128)(2,1)S(1)}, bf16[2,144,768]{2,1,0:T(8,128)(2,1)S(1)}, u32[]{:S(2)}, u32[]{:S(2)}) collective-permute-start(bf16[2,144,768]{2,1,0:T(8,128)(2,1)S(1)} %get-tuple-element.20.qg0_ref), channel_id=1, source_target_pairs={{0,16},{16,32},{32,48},{48,0},{1,17},{17,33},{33,49},{49,1},{2,18}... | collective-permute-start | bytes 1327112 | tf_op jit(solution)/shard_map/ppermute | solution.py:328
  26.7 0.7 copy-start.10
  27.6 6.5 %collective-permute-start.2 = (f32[8,128]{1,0:T(8,128)S(1)}, f32[8,128]{1,0:T(8,128)S(1)}, u32[]{:S(2)}, u32[]{:S(2)}) collective-permute-start(f32[8,128]{1,0:T(8,128)S(1)} %select_select_fusion), channel_id=1, source_target_pairs={{0,2},{2,0},{1,3},{3,1},{4,6},{6,4},{5,7},{7,5},{8,10},{10,8},{9,1... | collective-permute-start | bytes 12296 | tf_op jit(solution)/shard_map/ppermute | solution.py:319
  30.7 13.7 %collective-permute-start.5 = (bf16[2,144,768]{2,1,0:T(8,128)(2,1)S(1)}, bf16[2,144,768]{2,1,0:T(8,128)(2,1)S(1)}, u32[]{:S(2)}, u32[]{:S(2)}) collective-permute-start(bf16[2,144,768]{2,1,0:T(8,128)(2,1)S(1)} %get-tuple-element.20.qg0_ref), channel_id=1, source_target_pairs={{0,48},{16,0},{32,16},{48,32},{1,49},{17,1},{33,17},{49,33},{2,50}... | collective-permute-start | bytes 1327112 | tf_op jit(solution)/shard_map/ppermute | solution.py:328
  36.3 11.8 %collective-permute-start.4 = (bf16[2,144,768]{2,1,0:T(8,128)(2,1)S(1)}, bf16[2,144,768]{2,1,0:T(8,128)(2,1)S(1)}, u32[]{:S(2)}, u32[]{:S(2)}) collective-permute-start(bf16[2,144,768]{2,1,0:T(8,128)(2,1)S(1)} %collective-permute-done.1.qg1_ref), channel_id=1, source_target_pairs={{0,16},{16,32},{32,48},{48,0},{1,17},{17,33},{33,49},{49,1},{2,18}... | collective-permute-start | bytes 1327112 | tf_op jit(solution)/shard_map/ppermute | solution.py:328
  38.2 6.2 %collective-permute-start.3 = (f32[8,128]{1,0:T(8,128)S(1)}, f32[8,128]{1,0:T(8,128)S(1)}, u32[]{:S(2)}, u32[]{:S(2)}) collective-permute-start(f32[8,128]{1,0:T(8,128)S(1)} %fusion.5), channel_id=1, source_target_pairs={{0,4},{4,0},{1,5},{5,1},{2,6},{6,2},{3,7},{7,3},{8,12},{12,8},{9,1... | collective-permute-start | bytes 12296 | tf_op jit(solution)/shard_map/ppermute | solution.py:319
  48.1 15.9 %collective-permute-start.6 = (bf16[8,128,256]{2,1,0:T(8,128)(2,1)S(1)}, bf16[8,128,256]{2,1,0:T(8,128)(2,1)S(1)}, u32[]{:S(2)}, u32[]{:S(2)}) collective-permute-start(bf16[8,128,256]{2,1,0:T(8,128)(2,1)S(1)} %all-to-all-done.kv0_ref), channel_id=1, source_target_pairs={{0,8},{8,0},{1,9},{9,1},{2,10},{10,2},{3,11},{11,3},{4,12},{12,4},... | collective-permute-start | bytes 1572872 | tf_op jit(solution)/shard_map/ppermute | solution.py:319
  54.5 19.5 %all-to-all-start.1 = ((f32[16,8,128]{2,1,0:T(8,128)}), f32[16,8,128]{2,1,0:T(8,128)S(1)}, u32[]{:S(2)}, u32[]{:S(2)}) async-start(f32[16,8,128]{2,1,0:T(8,128)} %broadcast_in_dim.49), calls=%async_computation.1 | async-start | bytes 131072 | tf_op jit(solution)/shard_map/all_to_all | solution.py:363
  92.4 5.7 %copy-start.5 = (bf16[128,768]{1,0:T(8,128)(2,1)}, bf16[128,768]{1,0:T(8,128)(2,1)S(1)}, u32[]{:S(2)}) copy-start(bf16[128,768]{1,0:T(8,128)(2,1)S(1)} %get-tuple-element.33) | copy-start | bytes 589828
  92.4 5.7 %copy-start.7 = (bf16[128,768]{1,0:T(8,128)(2,1)}, bf16[128,768]{1,0:T(8,128)(2,1)S(1)}, u32[]{:S(2)}) copy-start(bf16[128,768]{1,0:T(8,128)(2,1)S(1)} %get-tuple-element.32) | copy-start | bytes 589828
  92.4 5.6 %collective-permute-start.10 = (bf16[2,4,128,256]{3,2,1,0:T(8,128)(2,1)S(1)}, bf16[2,4,128,256]{3,2,1,0:T(8,128)(2,1)S(1)}, u32[]{:S(2)}, u32[]{:S(2)}) collective-permute-start(bf16[2,4,128,256]{3,2,1,0:T(8,128)(2,1)S(1)} %get-tuple-element.36), channel_id=1, source_target_pairs={{0,8},{8,0},{1,9},{9,1},{2,10},{10,2},{3,11},{11,3},{4,12},{12,4},... | collective-permute-start | bytes 1572872 | tf_op jit(solution)/shard_map/ppermute | solution.py:319
  98.2 9.4 %collective-permute-start.11 = (bf16[4,128,256]{2,1,0:T(8,128)(2,1)S(1)}, bf16[4,128,256]{2,1,0:T(8,128)(2,1)S(1)}, u32[]{:S(2)}, u32[]{:S(2)}) collective-permute-start(bf16[4,128,256]{2,1,0:T(8,128)(2,1)S(1)} %fusion.2), channel_id=1, source_target_pairs={{0,64},{64,0},{1,65},{65,1},{2,66},{66,2},{3,67},{67,3},{4,68},{68... | collective-permute-start | bytes 786440 | tf_op jit(solution)/shard_map/ppermute | solution.py:319
  108.4 3.8 %copy-start.8 = (bf16[128,768]{1,0:T(8,128)(2,1)S(1)}, bf16[128,768]{1,0:T(8,128)(2,1)}, u32[]{:S(2)}) copy-start(bf16[128,768]{1,0:T(8,128)(2,1)} %copy-done.7) | copy-start | bytes 589828
  108.4 6.6 %copy-start.6 = (bf16[128,768]{1,0:T(8,128)(2,1)S(1)}, bf16[128,768]{1,0:T(8,128)(2,1)}, u32[]{:S(2)}) copy-start(bf16[128,768]{1,0:T(8,128)(2,1)} %copy-done.5) | copy-start | bytes 589828
  108.4 20.9 %all-to-all-start.3 = ((bf16[4,128,256]{2,1,0:T(8,128)(2,1)}), bf16[4,128,256]{2,1,0:T(8,128)(2,1)S(1)}, u32[]{:S(2)}, u32[]{:S(2)}) async-start(bf16[4,128,256]{2,1,0:T(8,128)(2,1)} %fusion.1), calls=%async_computation.3 | async-start | bytes 524288 | tf_op jit(solution)/shard_map/all_to_all | solution.py:405
  112.2 7.8 %collective-permute-start.7 = (bf16[128,768]{1,0:T(8,128)(2,1)S(1)}, bf16[128,768]{1,0:T(8,128)(2,1)S(1)}, u32[]{:S(2)}, u32[]{:S(2)}) collective-permute-start(bf16[128,768]{1,0:T(8,128)(2,1)S(1)} %copy-done.8), channel_id=1, source_target_pairs={{0,48},{16,0},{32,16},{48,32},{1,49},{17,1},{33,17},{49,33},{2,50}... | collective-permute-start | bytes 589832 | tf_op jit(solution)/shard_map/ppermute | solution.py:328
  115.0 7.9 %collective-permute-start.8 = (bf16[128,768]{1,0:T(8,128)(2,1)S(1)}, bf16[128,768]{1,0:T(8,128)(2,1)S(1)}, u32[]{:S(2)}, u32[]{:S(2)}) collective-permute-start(bf16[128,768]{1,0:T(8,128)(2,1)S(1)} %copy-done.6), channel_id=1, source_target_pairs={{0,32},{16,48},{32,0},{48,16},{1,33},{17,49},{33,1},{49,17},{2,34}... | collective-permute-start | bytes 589832 | tf_op jit(solution)/shard_map/ppermute | solution.py:328
  118.1 10.4 %collective-permute-start.9 = (bf16[128,768]{1,0:T(8,128)(2,1)S(1)}, bf16[128,768]{1,0:T(8,128)(2,1)S(1)}, u32[]{:S(2)}, u32[]{:S(2)}) collective-permute-start(bf16[128,768]{1,0:T(8,128)(2,1)S(1)} %get-tuple-element.34), channel_id=1, source_target_pairs={{0,16},{16,32},{32,48},{48,0},{1,17},{17,33},{33,49},{49,1},{2,18}... | collective-permute-start | bytes 589832 | tf_op jit(solution)/shard_map/ppermute | solution.py:328
